TPU v7x, 32 devices: a whole 2x2x4 slice. The times are simulated.
32 devices in a mesh: groups: 2 (over y), blk: 4 (over z), basis: 2 (over x), col: 2 (over core).
Axes of the slice: x: 2, y: 2, z: 4, core: 2. Of those that a mesh axis runs over, the one named last changes fastest.
Arguments:
- right_panel: float32 [256, 256, 64], P(('groups', 'blk'), None, 'col'), parts along dimension 0, may hold values from -6 to 6
- near_field_blocks: bfloat16 [1024, 256, 256], P(('groups', 'blk'), 'basis'), parts along dimension 0, may hold values from -0.1875 to 0.1875
- near_list: int32 [1024, 2], P(('groups', 'blk')), parts along dimension 0, may hold values from 0 to 127, as said below
- cluster_basis: bfloat16 [256, 256, 64], P(('groups', 'blk'), 'basis'), parts along dimension 0, may hold values from -0.375 to 0.375
- coupling: bfloat16 [1024, 64, 64], P(('groups', 'blk')), parts along dimension 0, may hold values from -0.375 to 0.375
- far_list: int32 [1024, 2], P(('groups', 'blk')), parts along dimension 0, may hold values from 0 to 127, as said below
Outputs:
- krylov_one: float32 [256, 256, 64], P(('groups', 'blk'), 'basis', 'col'), parts along dimension 0
- krylov_two: float32 [256, 256, 64], P(('groups', 'blk'), 'basis', 'col'), parts along dimension 0
There are 2 independent parts, one for each index of `groups`. A program takes and returns all parts, laid end to end along the dimension named above; each array names one. Nothing has to cross between parts.
Inputs may be any that keep to these rules, and one draw needn't show every extreme that they name: `near_list`: entry t names a row cluster held by blk index b = t // 128, that is within [b * 32, (b + 1) * 32), and a column cluster held by index b - 1, b or b + 1 of blk taken around the loop of all blk indices (4 here); every index has entries of all three kinds. Clusters may repeat. `far_list`: entry p names a row cluster held by blk index p // 128 and any column cluster. Pairs may repeat.
All inputs are finite; a program needn't handle non-finite values.
Results may differ from a plain program's by a relative error of at most 0.0053.
Values may be sent and summed in bfloat16 or wider, within the bound.
No kernel may reach another device: no remote copies, remote signals or barrier semaphores. Data moves between devices by JAX's collectives and lax.ppermute only.
A program may use at most 64 MiB of HBM per device.

v0:
```python
import jax
import jax.numpy as jnp
from jax import lax
from jax.sharding import PartitionSpec as P


def from_behind(array, axis, by):
    size = lax.axis_size(axis)
    return lax.ppermute(array, axis, [(i, (i + by) % size) for i in range(size)])


def on_device(right_panel, near_field_blocks, near_list, cluster_basis, coupling, far_list):
    highest_precision = lax.Precision.HIGHEST
    clusters = right_panel.shape[0]
    slab_rows = cluster_basis.shape[1]
    cycle_place = lax.axis_index("blk")
    cycle_size = lax.axis_size("blk")
    basis_owner = lax.axis_index("basis")
    cluster_ids = jnp.arange(clusters, dtype=jnp.int32)
    near_rows = near_list[:, 0] - cycle_place * clusters
    near_cols = near_list[:, 1]
    row_lookup_table = (near_rows[None, :] == cluster_ids[:, None]).astype(jnp.float32)
    far_table = ((far_list[:, 0] - cycle_place * clusters)[None, :] == cluster_ids[:, None]).astype(
        jnp.float32
    )
    slot_index = (
        near_cols // clusters - cycle_place + 1 + cycle_size
    ) % cycle_size * clusters + near_cols % clusters

    def apply_operator(panel_low):
        own_rows = lax.dynamic_slice_in_dim(panel_low, basis_owner * slab_rows, slab_rows, 1)
        partial_sum = jnp.einsum(
            "nrk,nrc->nkc", cluster_basis, own_rows, preferred_element_type=jnp.float32
        )
        projected = lax.psum(partial_sum, "basis").astype(jnp.bfloat16)
        projections_all = lax.all_gather(projected, "blk", axis=0, tiled=True)
        far_terms = jnp.einsum(
            "pkr,prc->pkc",
            coupling,
            projections_all[far_list[:, 1]],
            preferred_element_type=jnp.float32,
        )
        far_sum = jnp.einsum("np,pkc->nkc", far_table, far_terms, precision=highest_precision)
        far_low = far_sum.astype(jnp.bfloat16)
        pieces = []
        for offset in (1, -1):
            pieces.append(from_behind(panel_low, "blk", offset))
        window = jnp.concatenate([pieces[0], panel_low, pieces[1]], 0)
        source_vector = window[slot_index]
        near_field_products = jnp.einsum(
            "fpz,fzg->fpg", near_field_blocks, source_vector, preferred_element_type=jnp.float32
        )
        near_field_total = jnp.einsum(
            "id,dpb->ipb", row_lookup_table, near_field_products, precision=highest_precision
        )
        far_part = jnp.einsum(
            "nrk,nkc->nrc", cluster_basis, far_low, preferred_element_type=jnp.float32
        )
        return far_part + near_field_total

    krylov_one = apply_operator(right_panel.astype(jnp.bfloat16))
    second_low = lax.all_gather(krylov_one.astype(jnp.bfloat16), "basis", axis=1, tiled=True)
    krylov_two = apply_operator(second_low)
    return (krylov_one, krylov_two)


def solution(mesh):
    placed = (
        P(("groups", "blk"), None, "col"),
        P(("groups", "blk"), "basis", None),
        P(("groups", "blk"), None),
        P(("groups", "blk"), "basis", None),
        P(("groups", "blk"), None, None),
        P(("groups", "blk"), None),
    )
    return jax.shard_map(
        on_device,
        mesh=mesh,
        in_specs=placed,
        out_specs=(P(("groups", "blk"), "basis", "col"), P(("groups", "blk"), "basis", "col")),
        check_vma=False,
    )
```

profile of v0, /device:TPU:0, one launch (start us, length us, event | category | flops | bytes accessed | tf_op | source)
XLA Modules:
  0.0 146.5 jit_solution(4731631576522560520)
XLA Ops:
  0.6 0.0 copy-start
  0.6 1.4 convert_element_type.20
  2.0 5.1 %collective-permute-start.1 = (bf16[32,256,32]{1,2,0:T(8,128)(2,1)S(1)}, bf16[32,256,32]{1,2,0:T(8,128)(2,1)}, u32[]{:S(2)}, u32[]{:S(2)}) collective-permute-start(bf16[32,256,32]{1,2,0:T(8,128)(2,1)S(1)} %convert_element_type.20), channel_id=1, source_target_pairs={{0,12},{4,0},{8,4},{12,8},{1,13},{5,1},{9,5},{13,9},{2,14},{6,2},{... | collective-permute-start | bytes 1572872 | tf_op jit(solution)/shard_map/ppermute | solution.py:9
  7.1 0.8 subtract_bitcast_fusion
  7.9 0.8 subtract_bitcast_fusion.1
  8.7 0.4 convolution_bitcast_fusion.5
  9.1 16.6 %all-reduce.2 = bf16[32,64,32]{1,2,0:T(8,128)(2,1)S(1)} all-reduce(f32[32,64,32]{1,2,0:T(8,128)S(1)} %convolution_bitcast_fusion.5), channel_id=1, replica_groups=mesh['groups'=2,'blk'=4,'basis'=2,'col'=2] {'basis'}, use_global_device_ids=true, to_apply=%region_0.1 | all-reduce | flops 65536 | bytes 393216 | tf_op jit(solution)/shard_map/psum | solution.py:35
  25.7 22.8 %all_gather.9 = bf16[128,64,32]{1,2,0:T(8,128)(2,1)} all-gather(bf16[32,64,32]{1,2,0:T(8,128)(2,1)S(1)} %all-reduce.2), channel_id=1, replica_groups=mesh['groups'=2,'blk'=4,'basis'=2,'col'=2] {'blk'}, dimensions={0}, use_global_device_ids=true | all-gather | bytes 655360 | tf_op jit(solution)/shard_map/all_gather | solution.py:36
  48.5 4.7 %copy.12 = bf16[128,64,64]{1,2,0:T(8,128)(2,1)S(1)} copy(bf16[128,64,64]{0,2,1:T(8,128)(2,1)} %param.10) | data formatting | bytes 2097152 | tf_op args[4]
  53.2 3.7 %gather_fusion = bf16[128,64,32]{1,2,0:T(8,128)(2,1)} fusion(bf16[128,64,32]{1,2,0:T(8,128)(2,1)} %all_gather.9, s32[1024]{0:T(1024)S(1)} %pad_clamp_fusion.1), kind=kCustom, calls=%fused_computation | custom fusion | bytes 1049088 | tf_op jit(solution)/shard_map/gather | solution.py:40
  56.9 1.9 %convolution_bitcast_fusion.1 = f32[128,64,32]{1,2,0:T(8,128)S(1)} fusion(bf16[128,64,32]{1,2,0:T(8,128)(2,1)} %gather_fusion, bf16[128,64,64]{1,2,0:T(8,128)(2,1)S(1)} %copy.12), kind=kOutput, calls=%fused_computation.15 | convolution fusion | flops 33554432 | bytes 2621440 | tf_op jit(solution)/shard_map/pkr,prc->pkc/dot_general | solution.py:37
  58.8 2.0 %fusion.8 = bf16[32,64,32]{1,0,2:T(8,128)(2,1)S(1)} fusion(f32[128,64,32]{1,2,0:T(8,128)S(1)} %convolution_bitcast_fusion.1, s32[128]{0:T(128)S(1)} %get-tuple-element.2), kind=kOutput, calls=%fused_computation.12 | convolution fusion | flops 100667392 | bytes 1180160 | tf_op jit(solution)/shard_map/np,pkc->nkc/dot_general | solution.py:43
  60.8 0.0 collective-permute-done
  60.8 1.4 pad_maximum_fusion
  62.2 2.0 %gather_fusion.1 = bf16[128,256,32]{1,2,0:T(8,128)(2,1)} fusion(bf16[96,256,32]{1,2,0:T(8,128)(2,1)S(1)} %pad_maximum_fusion, s32[1024]{0:T(1024)S(1)} %pad_clamp_fusion), kind=kCustom, calls=%fused_computation.1 | custom fusion | bytes 4194816 | tf_op jit(solution)/shard_map/gather | solution.py:49
  64.2 7.0 %fusion.32 = f32[128,32,128]{2,1,0:T(8,128)S(1)} fusion(bf16[128,256,32]{1,2,0:T(8,128)(2,1)} %gather_fusion.1, bf16[128,128,256]{2,1,0:T(8,128)(2,1)} %param.7), kind=kOutput, calls=%fused_computation.58 | convolution fusion | flops 268435456 | bytes 12582912 | tf_op jit(solution)/shard_map/fpz,fzg->fpg/dot_general | solution.py:50
  71.2 2.0 %fusion.2 = f32[32,128,32]{1,0,2:T(8,128)S(1)} fusion(f32[128,32,128]{2,1,0:T(8,128)S(1)} %fusion.32, s32[128]{0:T(128)S(1)} %get-tuple-element.4), kind=kOutput, calls=%fused_computation.6 | convolution fusion | flops 201330688 | bytes 2621952 | tf_op jit(solution)/shard_map/id,dpb->ipb/dot_general | solution.py:53
  73.2 1.3 fusion.31
  74.4 7.1 %all_gather.10 = bf16[32,256,32]{1,2,0:T(8,128)(2,1)S(1)} all-gather(bf16[32,128,32]{1,2,0:T(8,128)(2,1)S(1)} %get-tuple-element.6), channel_id=1, replica_groups=mesh['groups'=2,'blk'=4,'basis'=2,'col'=2] {'basis'}, dimensions={1}, use_global_device_ids=true | all-gather | bytes 786432 | tf_op jit(solution)/shard_map/all_gather | solution.py:62
  81.5 0.4 convolution_bitcast_fusion.3
  81.9 2.9 %collective-permute-start.3 = (bf16[32,256,32]{1,2,0:T(8,128)(2,1)S(1)}, bf16[32,256,32]{1,2,0:T(8,128)(2,1)}, u32[]{:S(2)}, u32[]{:S(2)}) collective-permute-start(bf16[32,256,32]{1,2,0:T(8,128)(2,1)S(1)} %all_gather.10), channel_id=1, source_target_pairs={{0,12},{4,0},{8,4},{12,8},{1,13},{5,1},{9,5},{13,9},{2,14},{6,2},{... | collective-permute-start | bytes 1572872 | tf_op jit(solution)/shard_map/ppermute | solution.py:9
  84.8 0.0 collective-permute-start.2
  84.8 16.1 %all-reduce.3 = bf16[32,64,32]{1,2,0:T(8,128)(2,1)S(1)} all-reduce(f32[32,64,32]{1,2,0:T(8,128)S(1)} %convolution_bitcast_fusion.3), channel_id=1, replica_groups=mesh['groups'=2,'blk'=4,'basis'=2,'col'=2] {'basis'}, use_global_device_ids=true, to_apply=%region_1.2 | all-reduce | flops 65536 | bytes 393216 | tf_op jit(solution)/shard_map/psum | solution.py:35
  100.9 25.0 %all_gather.11 = bf16[128,64,32]{1,2,0:T(8,128)(2,1)} all-gather(bf16[32,64,32]{1,2,0:T(8,128)(2,1)S(1)} %all-reduce.3), channel_id=1, replica_groups=mesh['groups'=2,'blk'=4,'basis'=2,'col'=2] {'blk'}, dimensions={0}, use_global_device_ids=true | all-gather | bytes 655360 | tf_op jit(solution)/shard_map/all_gather | solution.py:36
  125.9 3.1 %gather_fusion.2 = bf16[128,64,32]{1,2,0:T(8,128)(2,1)} fusion(bf16[128,64,32]{1,2,0:T(8,128)(2,1)} %all_gather.11, s32[1024]{0:T(1024)S(1)} %pad_clamp_fusion.1), kind=kCustom, calls=%fused_computation.2 | custom fusion | bytes 1049088 | tf_op jit(solution)/shard_map/gather | solution.py:40
  129.0 1.9 %convolution_bitcast_fusion = f32[128,64,32]{1,2,0:T(8,128)S(1)} fusion(bf16[128,64,32]{1,2,0:T(8,128)(2,1)} %gather_fusion.2, bf16[128,64,64]{1,2,0:T(8,128)(2,1)S(1)} %copy-done.2), kind=kOutput, calls=%fused_computation.14 | convolution fusion | flops 33554432 | bytes 2621440 | tf_op jit(solution)/shard_map/pkr,prc->pkc/dot_general | solution.py:37
  130.9 2.0 %fusion.5 = bf16[32,64,32]{1,0,2:T(8,128)(2,1)S(1)} fusion(f32[128,64,32]{1,2,0:T(8,128)S(1)} %convolution_bitcast_fusion, s32[128]{0:T(128)S(1)} %get-tuple-element.2), kind=kOutput, calls=%fused_computation.9 | convolution fusion | flops 100667392 | bytes 1180160 | tf_op jit(solution)/shard_map/np,pkc->nkc/dot_general | solution.py:43
  132.9 1.4 pad_maximum_fusion.1
  134.3 2.0 %gather_fusion.3 = bf16[128,256,32]{1,2,0:T(8,128)(2,1)} fusion(bf16[96,256,32]{1,2,0:T(8,128)(2,1)S(1)} %pad_maximum_fusion.1, s32[1024]{0:T(1024)S(1)} %pad_clamp_fusion), kind=kCustom, calls=%fused_computation.3 | custom fusion | bytes 4194816 | tf_op jit(solution)/shard_map/gather | solution.py:49
  136.3 7.0 %fusion.33 = f32[128,32,128]{2,1,0:T(8,128)S(1)} fusion(bf16[128,256,32]{1,2,0:T(8,128)(2,1)} %gather_fusion.3, bf16[128,128,256]{2,1,0:T(8,128)(2,1)} %param.7), kind=kOutput, calls=%fused_computation.59 | convolution fusion | flops 268435456 | bytes 12582912 | tf_op jit(solution)/shard_map/fpz,fzg->fpg/dot_general | solution.py:50
  143.3 2.0 %fusion = f32[32,128,32]{1,0,2:T(8,128)S(1)} fusion(f32[128,32,128]{2,1,0:T(8,128)S(1)} %fusion.33, s32[128]{0:T(128)S(1)} %get-tuple-element.4), kind=kOutput, calls=%fused_computation.4 | convolution fusion | flops 201330688 | bytes 2621952 | tf_op jit(solution)/shard_map/id,dpb->ipb/dot_general | solution.py:53
  145.3 1.2 fusion.11
  (11 shorter events, 0.0 us)
Async XLA Ops:
  0.6 8.0 %copy-start = (bf16[32,128,64]{1,2,0:T(8,128)(2,1)S(1)}, bf16[32,128,64]{1,2,0:T(8,128)(2,1)}, u32[]{:S(2)}) copy-start(bf16[32,128,64]{1,2,0:T(8,128)(2,1)} %param.9) | copy-start | bytes 1572868
  2.0 58.8 %collective-permute-start.1 = (bf16[32,256,32]{1,2,0:T(8,128)(2,1)S(1)}, bf16[32,256,32]{1,2,0:T(8,128)(2,1)}, u32[]{:S(2)}, u32[]{:S(2)}) collective-permute-start(bf16[32,256,32]{1,2,0:T(8,128)(2,1)S(1)} %convert_element_type.20), channel_id=1, source_target_pairs={{0,12},{4,0},{8,4},{12,8},{1,13},{5,1},{9,5},{13,9},{2,14},{6,2},{... | collective-permute-start | bytes 1572872 | tf_op jit(solution)/shard_map/ppermute | solution.py:9
  7.1 53.7 %collective-permute-start = (bf16[32,256,32]{1,2,0:T(8,128)(2,1)S(1)}, bf16[32,256,32]{1,2,0:T(8,128)(2,1)}, u32[]{:S(2)}, u32[]{:S(2)}) collective-permute-start(bf16[32,256,32]{1,2,0:T(8,128)(2,1)S(1)} %convert_element_type.20), channel_id=1, source_target_pairs={{0,4},{4,8},{8,12},{12,0},{1,5},{5,9},{9,13},{13,1},{2,6},{6,10},{... | collective-permute-start | bytes 1572872 | tf_op jit(solution)/shard_map/ppermute | solution.py:9
  53.2 3.7 %copy-start.1 = (bf16[128,64,64]{1,2,0:T(8,128)(2,1)}, bf16[128,64,64]{1,2,0:T(8,128)(2,1)S(1)}, u32[]{:S(2)}) copy-start(bf16[128,64,64]{1,2,0:T(8,128)(2,1)S(1)} %copy.12) | copy-start | bytes 3145732
  81.9 51.0 %collective-permute-start.3 = (bf16[32,256,32]{1,2,0:T(8,128)(2,1)S(1)}, bf16[32,256,32]{1,2,0:T(8,128)(2,1)}, u32[]{:S(2)}, u32[]{:S(2)}) collective-permute-start(bf16[32,256,32]{1,2,0:T(8,128)(2,1)S(1)} %all_gather.10), channel_id=1, source_target_pairs={{0,12},{4,0},{8,4},{12,8},{1,13},{5,1},{9,5},{13,9},{2,14},{6,2},{... | collective-permute-start | bytes 1572872 | tf_op jit(solution)/shard_map/ppermute | solution.py:9
  84.8 48.1 %collective-permute-start.2 = (bf16[32,256,32]{1,2,0:T(8,128)(2,1)S(1)}, bf16[32,256,32]{1,2,0:T(8,128)(2,1)}, u32[]{:S(2)}, u32[]{:S(2)}) collective-permute-start(bf16[32,256,32]{1,2,0:T(8,128)(2,1)S(1)} %all_gather.10), channel_id=1, source_target_pairs={{0,4},{4,8},{8,12},{12,0},{1,5},{5,9},{9,13},{13,1},{2,6},{6,10},{... | collective-permute-start | bytes 1572872 | tf_op jit(solution)/shard_map/ppermute | solution.py:9
  125.9 3.1 %copy-start.2 = (bf16[128,64,64]{1,2,0:T(8,128)(2,1)S(1)}, bf16[128,64,64]{1,2,0:T(8,128)(2,1)}, u32[]{:S(2)}) copy-start(bf16[128,64,64]{1,2,0:T(8,128)(2,1)} %copy-done.1) | copy-start | bytes 3145732
where the time goes:
time: 147 us
  blocking collectives  87.6 us (60%)
  matrix products  29 us (20%)
  local copies, waits for them, and re-layouts  15.4 us (10%)
  starting transfers between devices  8 us (5%)
  other arithmetic  5.65 us (4%)
    all_gather x2, blocking collectives, apply_operator(): projections_all = lax.all_gather(projected, 'blk', axis=0, tiled=True)  47.8 us
    psum x2, blocking collectives, apply_operator(): projected = lax.psum(partial_sum, 'basis').astype(jnp.bfloat16)  32.8 us
    dot_general x2, matrix products, apply_operator(): jnp.einsum('fpz,fzg->fpg', near_field_blocks, source_vector, preferred_el...  13.9 us
    ppermute x4, starting transfers between devices, from_behind(): lax.ppermute(array, axis, [(i, (i + by) % size) for i in range(size)])  8 us
    all_gather x1, blocking collectives, on_device(): lax.all_gather(krylov_one.astype(jnp.bfloat16), 'basis', axis=1, tiled=True)  7.06 us
    gather x2, local copies, waits for them, and re-layouts, apply_operator(): projections_all[far_list[:, 1]]  6.71 us
    unnamed x7, local copies, waits for them, and re-layouts  4.73 us
    dot_general x2, matrix products, apply_operator(): jnp.einsum('id,dpb->ipb', row_lookup_table, near_field_products, precisio...  4.02 us
  transfers between devices with their start and end apart: 4, of which 0 were waited for; matrix products, arithmetic and copies ran while one was open for 14% of the time, Pallas kernels for 0%

commit v1 on v0

--- a/solution.py
+++ b/solution.py
@@ -1,7 +1,237 @@
+import functools
+
 import jax
 import jax.numpy as jnp
 from jax import lax
+from jax.experimental import pallas as pl
+from jax.experimental.pallas import tpu as pltpu
 from jax.sharding import PartitionSpec as P
+
+UNROLL = 8
+VMEM = pl.BlockSpec(memory_space=pltpu.VMEM)
+SMEM = pl.BlockSpec(memory_space=pltpu.SMEM)
+TRANSPOSED_RHS = (((1,), (1,)), ((), ()))
+PLAIN = (((1,), (0,)), ((), ()))
+
+
+def shifted(array, axis, by):
+    size = lax.axis_size(axis)
+    return lax.ppermute(array, axis, [(i, (i + by) % size) for i in range(size)])
+
+
+def dot(a, b, dims):
+    return lax.dot_general(a, b, dims, preferred_element_type=jnp.float32)
+
+
+def params(vmem=48):
+    return pltpu.CompilerParams(vmem_limit_bytes=vmem << 20)
+
+
+def put_projection(low_ref, offset, width, basis_ref, out_ref):
+    half = out_ref.shape[0]
+    for n in range(half):
+        pair = [
+            dot(low_ref[m, :, pl.ds(offset, width)], basis_ref[m], TRANSPOSED_RHS)
+            for m in (n, n + half)
+        ]
+        out_ref[n] = jnp.concatenate(pair, 1)
+
+
+def start_kernel(place_ref, near_ref, panel_ref, basis_ref, low_ref, mine_ref, proj_ref, plan_ref):
+    clusters = panel_ref.shape[0]
+    slab = basis_ref.shape[2]
+    offset = pl.multiple_of(place_ref[1] * slab, slab)
+    low_ref[...] = panel_ref[...].astype(jnp.bfloat16)
+    mine_ref[...] = low_ref[:, :, pl.ds(offset, slab)]
+    put_projection(low_ref, offset, slab, basis_ref, proj_ref)
+    for kind in range(3):
+        plan_ref[9, kind] = 0
+
+    def sort_entry(t, carry):
+        column = near_ref[1, t]
+        owner = lax.div(column, clusters)
+        kind = lax.rem(owner - place_ref[0] + 1 + place_ref[2], place_ref[2])
+        at = plan_ref[9, kind]
+        plan_ref[kind, at] = t
+        plan_ref[3 + kind, at] = near_ref[0, t] - place_ref[0] * clusters
+        plan_ref[6 + kind, at] = column - owner * clusters
+        plan_ref[9, kind] = at + 1
+        return carry
+
+    lax.fori_loop(0, near_ref.shape[1], sort_entry, 0)
+    for kind in range(3):
+        count = plan_ref[9, kind]
+        for j in range(UNROLL):
+            plan_ref[kind, count + j] = 0
+            plan_ref[3 + kind, count + j] = clusters
+            plan_ref[6 + kind, count + j] = 0
+
+
+def add_near(plan_ref, kind, source_ref, blocks_ref, offset, width, acc_ref):
+    steps = lax.div(plan_ref[9, kind] + UNROLL - 1, UNROLL)
+
+    def step(i, carry):
+        terms = []
+        for j in range(UNROLL):
+            at = i * UNROLL + j
+            block = blocks_ref[plan_ref[kind, at], :, pl.ds(offset, width)]
+            terms.append(dot(source_ref[plan_ref[6 + kind, at]], block, TRANSPOSED_RHS))
+        for j in range(UNROLL):
+            row = plan_ref[3 + kind, i * UNROLL + j]
+            acc_ref[row] = acc_ref[row] + terms[j]
+        return carry
+
+    lax.fori_loop(0, steps, step, 0)
+
+
+def near_kernel(pieces, first, place_ref, plan_ref, *refs):
+    sources, refs = refs[: len(pieces)], refs[len(pieces) :]
+    blocks_ref, refs = refs[0], refs[1:]
+    acc_ref = refs[-1]
+    slab = acc_ref.shape[2]
+    if first:
+        acc_ref[...] = jnp.zeros_like(acc_ref)
+    else:
+        acc_ref[...] = refs[0][...]
+    for (kind, part), source_ref in zip(pieces, sources):
+        width = source_ref.shape[2]
+        if part is None:
+            offset = 0
+        else:
+            offset = pl.multiple_of((place_ref[1] if part == 0 else 1 - place_ref[1]) * slab, slab)
+        add_near(plan_ref, kind, source_ref, blocks_ref, offset, width, acc_ref)
+
+
+def far_kernel(place_ref, far_ref, coupling_ref, *refs):
+    held, out_ref, unpacked, acc = refs[:-3], refs[-3], refs[-2], refs[-1]
+    clusters = out_ref.shape[0]
+    half, columns, _ = held[0].shape
+    rank = coupling_ref.shape[1]
+    for d, packed in enumerate(held):
+        unpacked[d * clusters : d * clusters + half] = packed[:, :, :rank]
+        unpacked[d * clusters + half : (d + 1) * clusters] = packed[:, :, rank:]
+    acc[...] = jnp.zeros_like(acc)
+
+    def step(i, carry):
+        terms = []
+        for j in range(UNROLL):
+            p = i * UNROLL + j
+            column = far_ref[1, p]
+            owner = lax.div(column, clusters)
+            behind = lax.rem(place_ref[0] - owner + place_ref[2], place_ref[2])
+            source = unpacked[behind * clusters + column - owner * clusters]
+            terms.append(dot(source, coupling_ref[p], TRANSPOSED_RHS))
+        for j in range(UNROLL):
+            row = far_ref[0, i * UNROLL + j] - place_ref[0] * clusters
+            acc[row] = acc[row] + terms[j]
+        return carry
+
+    lax.fori_loop(0, coupling_ref.shape[0] // UNROLL, step, 0)
+    out_ref[...] = acc[...].astype(jnp.bfloat16)
+
+
+def finish_kernel(pieces, last, place_ref, plan_ref, *refs):
+    count = len(pieces)
+    sources, blocks_ref, acc_in, far_ref, basis_ref = refs[:count], *refs[count : count + 4]
+    if last:
+        out_ref, acc_ref = refs[count + 4 :]
+    else:
+        out_ref, mine_ref, proj_ref, acc_ref = refs[count + 4 :]
+    near_kernel(pieces, False, place_ref, plan_ref, *sources, blocks_ref, acc_in, acc_ref)
+    clusters = out_ref.shape[0]
+    for n in range(clusters):
+        out_ref[n] = acc_ref[n] + dot(far_ref[n], basis_ref[n], PLAIN)
+    if not last:
+        mine_ref[...] = out_ref[...].astype(jnp.bfloat16)
+        put_projection(mine_ref, 0, mine_ref.shape[2], basis_ref, proj_ref)
+
+
+def tiled_on_device(right_panel, near_field_blocks, near_list, cluster_basis, coupling, far_list):
+    clusters, points, columns = right_panel.shape
+    near_count = near_list.shape[0]
+    slab, rank = cluster_basis.shape[1:]
+    panel = right_panel.transpose(0, 2, 1)
+    basis = cluster_basis.transpose(0, 2, 1)
+    near_list, far_list = near_list.T, far_list.T
+    cycle = lax.axis_size("blk")
+    place = jnp.stack([lax.axis_index("blk"), lax.axis_index("basis"), jnp.int32(cycle)]).astype(jnp.int32)
+    f32, bf16 = jnp.float32, jnp.bfloat16
+    mine_shape = jax.ShapeDtypeStruct((clusters, columns, slab), bf16)
+    proj_shape = jax.ShapeDtypeStruct((clusters // 2, columns, 2 * rank), f32)
+    out_shape = jax.ShapeDtypeStruct((clusters, columns, slab), f32)
+    acc_shape = jax.ShapeDtypeStruct((clusters + 1, columns, slab), f32)
+    plan_shape = jax.ShapeDtypeStruct((10, near_count + UNROLL), jnp.int32)
+
+    low, mine, proj, plan = pl.pallas_call(
+        start_kernel,
+        out_shape=(jax.ShapeDtypeStruct((clusters, columns, points), bf16), mine_shape, proj_shape, plan_shape),
+        in_specs=[SMEM, SMEM, VMEM, VMEM],
+        out_specs=(VMEM, VMEM, VMEM, SMEM),
+        compiler_params=params(),
+        name="start",
+    )(place, near_list, panel, basis)
+
+    def near(pieces, acc, name):
+        tags = tuple(tag for tag, _ in pieces)
+        operands = [array for _, array in pieces] + [near_field_blocks]
+        if acc is not None:
+            operands.append(acc)
+        return pl.pallas_call(
+            functools.partial(near_kernel, tags, acc is None),
+            out_shape=acc_shape,
+            in_specs=[SMEM, SMEM] + [VMEM] * len(operands),
+            out_specs=VMEM,
+            compiler_params=params(),
+            name=name,
+        )(place, plan, *operands)
+
+    def far(held):
+        return pl.pallas_call(
+            far_kernel,
+            out_shape=jax.ShapeDtypeStruct((clusters, columns, rank), bf16),
+            in_specs=[SMEM, SMEM, VMEM] + [VMEM] * len(held),
+            out_specs=VMEM,
+            scratch_shapes=[
+                pltpu.VMEM((cycle * clusters, columns, rank), bf16),
+                pltpu.VMEM((clusters, columns, rank), f32),
+            ],
+            compiler_params=params(),
+            name="far",
+        )(place, far_list, coupling, *held)
+
+    def finish(pieces, acc, far_low, last):
+        tags = tuple(tag for tag, _ in pieces)
+        outs = (out_shape,) if last else (out_shape, mine_shape, proj_shape)
+        operands = [array for _, array in pieces] + [near_field_blocks, acc, far_low, basis]
+        return pl.pallas_call(
+            functools.partial(finish_kernel, tags, last),
+            out_shape=outs,
+            in_specs=[SMEM, SMEM] + [VMEM] * len(operands),
+            out_specs=(VMEM,) * len(outs),
+            scratch_shapes=[pltpu.VMEM(acc_shape.shape, f32)],
+            compiler_params=params(),
+            name="finish",
+        )(place, plan, *operands)
+
+    def projections(proj):
+        other = shifted(proj.astype(bf16), "basis", 1)
+        whole = (proj + other.astype(f32)).astype(bf16)
+        return [whole] + [shifted(whole, "blk", d) for d in range(1, cycle)]
+
+    def apply_operator(mine, proj, own_pieces, last):
+        behind, ahead = shifted(mine, "blk", 1), shifted(mine, "blk", -1)
+        if own_pieces is None:
+            own_pieces = [((1, 0), mine), ((1, 1), shifted(mine, "basis", 1))]
+        held = projections(proj)
+        acc = near(own_pieces, None, "near_own")
+        acc = near([((0, 0), behind), ((2, 0), ahead)], acc, "near_loop")
+        far_low = far(held)
+        others = [((0, 1), shifted(behind, "basis", 1)), ((2, 1), shifted(ahead, "basis", 1))]
+        return finish(others, acc, far_low, last)
+
+    first, mine, proj = apply_operator(mine, proj, [((1, None), low)], False)
+    (second,) = apply_operator(mine, proj, None, True)
+    return first.transpose(0, 2, 1), second.transpose(0, 2, 1)
 
 
 def from_behind(array, axis, by):
@@ -9,7 +239,7 @@
     return lax.ppermute(array, axis, [(i, (i + by) % size) for i in range(size)])
 
 
-def on_device(right_panel, near_field_blocks, near_list, cluster_basis, coupling, far_list):
+def general_on_device(right_panel, near_field_blocks, near_list, cluster_basis, coupling, far_list):
     highest_precision = lax.Precision.HIGHEST
     clusters = right_panel.shape[0]
     slab_rows = cluster_basis.shape[1]
@@ -64,6 +294,12 @@
     return (krylov_one, krylov_two)
 
 
+def on_device(right_panel, near_field_blocks, near_list, cluster_basis, coupling, far_list):
+    tiled = lax.axis_size("basis") == 2 and cluster_basis.shape[1] % 128 == 0
+    run = tiled_on_device if tiled else general_on_device
+    return run(right_panel, near_field_blocks, near_list, cluster_basis, coupling, far_list)
+
+
 def solution(mesh):
     placed = (
         P(("groups", "blk"), None, "col"),

time: 147 us -> 103 us (0.70)
  blocking collectives: 87.6 us -> 0 us
  Pallas kernels: 0 us -> 53.8 us
  matrix products: 29 us -> 0 us
  waiting for transfers between devices: 0.01 us -> 16.4 us
  starting transfers between devices: 8 us -> 23.6 us
  local copies, waits for them, and re-layouts: 15.4 us -> 7.55 us
  other arithmetic: 5.65 us -> 0.18 us
    all_gather x3 -> x0, blocking collectives: 54.9 us -> none  [the longest x2 47.8 us: apply_operator(): projections_all = lax.all_gather(projected, 'blk', axis=0, tiled=True)]
    pallas_call x0 -> x9, Pallas kernels: none -> 53.8 us  [the longest x4 24.2 us: near(): pl.pallas_call(functools.partial(near_kernel, tags, acc is None), out_sha...]
    psum x2 -> x0, blocking collectives: 32.8 us -> none  [apply_operator(): projected = lax.psum(partial_sum, 'basis').astype(jnp.bfloat16)]
    dot_general x12 -> x0, matrix products: 29 us -> none  [the longest x2 13.9 us: apply_operator(): jnp.einsum('fpz,fzg->fpg', near_field_blocks, source_vector, preferred_el...]
    ppermute x4 -> x17, waiting for transfers between devices: 0.01 us -> 16.4 us  [shifted(): lax.ppermute(array, axis, [(i, (i + by) % size) for i in range(size)])]
    ppermute x4 -> x17, starting transfers between devices: 8 us -> 23.6 us  [shifted(): lax.ppermute(array, axis, [(i, (i + by) % size) for i in range(size)])]
    gather x4 -> x0, local copies, waits for them, and re-layouts: 10.7 us -> none  [the longest x2 6.71 us: apply_operator(): projections_all[far_list[:, 1]]]
    unnamed x7 -> x15, local copies, waits for them, and re-layouts: 4.73 us -> 7.55 us
  transfers between devices with their start and end apart: 4 -> 17, of which waited for: 0 -> 4; matrix products, arithmetic and copies ran while one was open for 14% -> 4% of each run, Pallas kernels for 0% -> 32%
where the time goes in v1:
time: 103 us; the launch traced here: 102 us
  Pallas kernels  53.8 us (52%)
  starting transfers between devices  23.6 us (23%)
  waiting for transfers between devices  16.4 us (16%)
  local copies, waits for them, and re-layouts  7.55 us (7%)
    pallas_call x4, Pallas kernels, near(): pl.pallas_call(functools.partial(near_kernel, tags, acc is None), out_sha...  24.2 us
    ppermute x17, starting transfers between devices, shifted(): lax.ppermute(array, axis, [(i, (i + by) % size) for i in range(size)])  23.6 us
    ppermute x17, waiting for transfers between devices, shifted(): lax.ppermute(array, axis, [(i, (i + by) % size) for i in range(size)])  16.4 us
    pallas_call x2, Pallas kernels, finish(): pl.pallas_call(functools.partial(finish_kernel, tags, last), out_shape=ou...  14.7 us
    pallas_call x2, Pallas kernels, far(): pl.pallas_call(far_kernel, out_shape=jax.ShapeDtypeStruct((clusters, colu...  8.45 us
    unnamed x15, local copies, waits for them, and re-layouts  7.55 us
    pallas_call x1, Pallas kernels, tiled_on_device(): pl.pallas_call(start_kernel, out_shape=(jax.ShapeDtypeStruct((clusters, c...  6.42 us
  transfers between devices with their start and end apart: 17, of which 4 were waited for; matrix products, arithmetic and copies ran while one was open for 4% of the time, Pallas kernels for 32%

profile of v1, /device:TPU:0, one launch (start us, length us, event | category | flops | bytes accessed | tf_op | source)
XLA Modules:
  0.0 102.4 jit_solution(15557707049817099848)
XLA Ops:
  0.6 0.1 pad_add_fusion.place_ref
  0.7 1.0 %copy-done = bf16[32,128,64]{1,2,0:T(8,128)(2,1)S(1)} copy-done((bf16[32,128,64]{1,2,0:T(8,128)(2,1)S(1)}, bf16[32,128,64]{1,2,0:T(8,128)(2,1)}, u32[]{:S(2)}) %copy-start) | copy-done | bytes 524312
  1.8 1.2 %copy-done.2 = f32[32,256,32]{1,2,0:T(8,128)S(1)} copy-done((f32[32,256,32]{1,2,0:T(8,128)S(1)}, f32[32,256,32]{1,2,0:T(8,128)}, u32[]{:S(2)}) %copy-start.2) | copy-done | bytes 1048600
  3.0 0.7 copy-done.6
  3.7 6.4 %start.1 = (bf16[32,32,256]{2,1,0:T(8,128)(2,1)S(1)}, bf16[32,32,128]{2,1,0:T(8,128)(2,1)S(1)}, f32[16,32,128]{2,1,0:T(8,128)S(1)}, s32[10,136]{1,0:T(8,128)S(1)}) custom-call(s32[3]{0:T(128)S(1)} %pad_add_fusion.place_ref, s32[2,128]{1,0:T(2,128)S(1)} %bitcast.14, f32[32,32,256]{2,1,0:T(8,128)S(1)} %bitcast.11, bf16[32,64,128]{2,1,0:T(8,128)(2,1)S(1)} %bitcast.8), custom_call_target="tpu_custom_call" | custom-call | tf_op jit(solution)/shard_map/start/pallas_call | solution.py:165
  10.1 5.1 %collective-permute-start.2 = (bf16[32,32,128]{2,1,0:T(8,128)(2,1)S(1)}, bf16[32,32,128]{2,1,0:T(8,128)(2,1)S(1)}, u32[]{:S(2)}, u32[]{:S(2)}) collective-permute-start(bf16[32,32,128]{2,1,0:T(8,128)(2,1)S(1)} %get-tuple-element.10), channel_id=1, source_target_pairs={{0,12},{4,0},{8,4},{12,8},{1,13},{5,1},{9,5},{13,9},{2,14},{6,2},{... | collective-permute-start | bytes 786440 | tf_op jit(solution)/shard_map/ppermute | solution.py:19
  15.2 1.6 %collective-permute-start.4 = (bf16[16,32,128]{2,1,0:T(8,128)(2,1)S(1)}, bf16[16,32,128]{2,1,0:T(8,128)(2,1)S(1)}, u32[]{:S(2)}, u32[]{:S(2)}) collective-permute-start(bf16[16,32,128]{2,1,0:T(8,128)(2,1)S(1)} %convert_element_type.18), channel_id=1, source_target_pairs={{0,2},{2,0},{1,3},{3,1},{4,6},{6,4},{5,7},{7,5},{8,10},{10,8},{9,1... | collective-permute-start | bytes 393224 | tf_op jit(solution)/shard_map/ppermute | solution.py:19
  16.8 5.1 %collective-permute-done.2.refs_1_ = bf16[32,32,128]{2,1,0:T(8,128)(2,1)S(1)} collective-permute-done((bf16[32,32,128]{2,1,0:T(8,128)(2,1)S(1)}, bf16[32,32,128]{2,1,0:T(8,128)(2,1)S(1)}, u32[]{:S(2)}, u32[]{:S(2)}) %collective-permute-start.2) | collective-permute-done | bytes 262176 | tf_op jit(solution)/shard_map/ppermute | solution.py:19
  21.9 1.5 %collective-permute-start.3 = (bf16[32,32,128]{2,1,0:T(8,128)(2,1)S(1)}, bf16[32,32,128]{2,1,0:T(8,128)(2,1)S(1)}, u32[]{:S(2)}, u32[]{:S(2)}) collective-permute-start(bf16[32,32,128]{2,1,0:T(8,128)(2,1)S(1)} %collective-permute-done.2.refs_1_), channel_id=1, source_target_pairs={{0,2},{2,0},{1,3},{3,1},{4,6},{6,4},{5,7},{7,5},{8,10},{10,8},{9,1... | collective-permute-start | bytes 786440 | tf_op jit(solution)/shard_map/ppermute | solution.py:19
  23.4 3.9 %collective-permute-done.refs_0_ = bf16[32,32,128]{2,1,0:T(8,128)(2,1)S(1)} collective-permute-done((bf16[32,32,128]{2,1,0:T(8,128)(2,1)S(1)}, bf16[32,32,128]{2,1,0:T(8,128)(2,1)S(1)}, u32[]{:S(2)}, u32[]{:S(2)}) %collective-permute-start) | collective-permute-done | bytes 262176 | tf_op jit(solution)/shard_map/ppermute | solution.py:19
  27.3 1.5 %collective-permute-start.1 = (bf16[32,32,128]{2,1,0:T(8,128)(2,1)S(1)}, bf16[32,32,128]{2,1,0:T(8,128)(2,1)}, u32[]{:S(2)}, u32[]{:S(2)}) collective-permute-start(bf16[32,32,128]{2,1,0:T(8,128)(2,1)S(1)} %collective-permute-done.refs_0_), channel_id=1, source_target_pairs={{0,2},{2,0},{1,3},{3,1},{4,6},{6,4},{5,7},{7,5},{8,10},{10,8},{9,1... | collective-permute-start | bytes 786440 | tf_op jit(solution)/shard_map/ppermute | solution.py:19
  28.8 1.8 %collective-permute-start.7 = (bf16[16,32,128]{2,1,0:T(8,128)(2,1)S(1)}, bf16[16,32,128]{2,1,0:T(8,128)(2,1)}, u32[]{:S(2)}, u32[]{:S(2)}) collective-permute-start(bf16[16,32,128]{2,1,0:T(8,128)(2,1)S(1)} %add_convert_fusion.1.refs_0_), channel_id=1, source_target_pairs={{0,12},{4,0},{8,4},{12,8},{1,13},{5,1},{9,5},{13,9},{2,14},{6,2},{... | collective-permute-start | bytes 393224 | tf_op jit(solution)/shard_map/ppermute | solution.py:19
  30.6 1.3 %collective-permute-start.6 = (bf16[16,32,128]{2,1,0:T(8,128)(2,1)S(1)}, bf16[16,32,128]{2,1,0:T(8,128)(2,1)}, u32[]{:S(2)}, u32[]{:S(2)}) collective-permute-start(bf16[16,32,128]{2,1,0:T(8,128)(2,1)S(1)} %add_convert_fusion.1.refs_0_), channel_id=1, source_target_pairs={{0,8},{4,12},{8,0},{12,4},{1,9},{5,13},{9,1},{13,5},{2,10},{6,14},... | collective-permute-start | bytes 393224 | tf_op jit(solution)/shard_map/ppermute | solution.py:19
  32.0 3.9 %copy.8.coupling_ref = bf16[128,64,64]{2,1,0:T(8,128)(2,1)S(1)} copy(bf16[128,64,64]{0,2,1:T(8,128)(2,1)} %param.10) | data formatting | bytes 2097152 | tf_op args[4]
  35.9 0.6 copy-done.4
  36.6 5.1 %near_own.2.refs_3_ = f32[33,32,128]{2,1,0:T(8,128)S(1)} custom-call(s32[3]{0:T(128)S(1)} %copy-done.4, s32[10,136]{1,0:T(8,128)S(1)} %get-tuple-element.9.plan_ref, bf16[32,32,256]{2,1,0:T(8,128)(2,1)S(1)} %get-tuple-element.11.refs_0_, bf16[128,128,256]{2,1,0:T(8,128)(2,1)} %refs_2_.9), custom_call_target="tpu_custom_call" | custom-call | tf_op jit(solution)/shard_map/near_own/pallas_call | solution.py:179
  41.7 6.3 %near_loop.2.refs_3_ = f32[33,32,128]{2,1,0:T(8,128)S(1)} custom-call(s32[3]{0:T(128)S(1)} %copy-done.4, s32[10,136]{1,0:T(8,128)S(1)} %get-tuple-element.9.plan_ref, bf16[32,32,128]{2,1,0:T(8,128)(2,1)S(1)} %collective-permute-done.refs_0_, bf16[32,32,128]{2,1,0:T(8,128)(2,1)S(1)} %collective-permute-done.2.refs_1_, bf16[128,128,256]{2,1,0:T(8,128)(2,1)} %refs_2_.9, ...), custom_call_target="tpu_custom_call" | custom-call | tf_op jit(solution)/shard_map/near_loop/pallas_call | solution.py:179
  48.1 4.5 %far.2.refs_4_ = bf16[32,32,64]{2,1,0:T(8,128)(2,1)S(1)} custom-call(s32[3]{0:T(128)S(1)} %copy-done.4, s32[2,128]{1,0:T(2,128)S(1)} %bitcast.12, bf16[128,64,64]{2,1,0:T(8,128)(2,1)S(1)} %copy.8.coupling_ref, bf16[16,32,128]{2,1,0:T(8,128)(2,1)S(1)} %add_convert_fusion.1.refs_0_, bf16[16,32,128]{2,1,0:T(8,128)(2,1)} %collective-permute-done.5.refs_1_, ...), custom_call_target="tpu_custom_call" | custom-call | tf_op jit(solution)/shard_map/far/pallas_call | solution.py:189
  52.6 7.4 %finish.2 = (f32[32,32,128]{2,1,0:T(8,128)}, bf16[32,32,128]{2,1,0:T(8,128)(2,1)S(1)}, f32[16,32,128]{2,1,0:T(8,128)S(1)}) custom-call(s32[3]{0:T(128)S(1)} %copy-done.4, s32[10,136]{1,0:T(8,128)S(1)} %get-tuple-element.9.plan_ref, bf16[32,32,128]{2,1,0:T(8,128)(2,1)} %collective-permute-done.1.refs_0_, ...), custom_call_target="tpu_custom_call" | custom-call | tf_op jit(solution)/shard_map/finish/pallas_call | solution.py:206
  60.0 4.0 %collective-permute-start.10 = (bf16[32,32,128]{2,1,0:T(8,128)(2,1)S(1)}, bf16[32,32,128]{2,1,0:T(8,128)(2,1)S(1)}, u32[]{:S(2)}, u32[]{:S(2)}) collective-permute-start(bf16[32,32,128]{2,1,0:T(8,128)(2,1)S(1)} %get-tuple-element.14.refs_0_), channel_id=1, source_target_pairs={{0,12},{4,0},{8,4},{12,8},{1,13},{5,1},{9,5},{13,9},{2,14},{6,2},{... | collective-permute-start | bytes 786440 | tf_op jit(solution)/shard_map/ppermute | solution.py:19
  64.1 0.6 collective-permute-start.13
  64.7 1.5 %collective-permute-start.12 = (bf16[32,32,128]{2,1,0:T(8,128)(2,1)S(1)}, bf16[32,32,128]{2,1,0:T(8,128)(2,1)S(1)}, u32[]{:S(2)}, u32[]{:S(2)}) collective-permute-start(bf16[32,32,128]{2,1,0:T(8,128)(2,1)S(1)} %get-tuple-element.14.refs_0_), channel_id=1, source_target_pairs={{0,2},{2,0},{1,3},{3,1},{4,6},{6,4},{5,7},{7,5},{8,10},{10,8},{9,1... | collective-permute-start | bytes 786440 | tf_op jit(solution)/shard_map/ppermute | solution.py:19
  66.2 4.4 %collective-permute-done.10.refs_1_ = bf16[32,32,128]{2,1,0:T(8,128)(2,1)S(1)} collective-permute-done((bf16[32,32,128]{2,1,0:T(8,128)(2,1)S(1)}, bf16[32,32,128]{2,1,0:T(8,128)(2,1)S(1)}, u32[]{:S(2)}, u32[]{:S(2)}) %collective-permute-start.10) | collective-permute-done | bytes 262176 | tf_op jit(solution)/shard_map/ppermute | solution.py:19
  70.5 0.5 collective-permute-start.11
  71.1 3.0 %collective-permute-done.8.refs_0_ = bf16[32,32,128]{2,1,0:T(8,128)(2,1)S(1)} collective-permute-done((bf16[32,32,128]{2,1,0:T(8,128)(2,1)S(1)}, bf16[32,32,128]{2,1,0:T(8,128)(2,1)S(1)}, u32[]{:S(2)}, u32[]{:S(2)}) %collective-permute-start.8) | collective-permute-done | bytes 262176 | tf_op jit(solution)/shard_map/ppermute | solution.py:19
  74.1 0.5 collective-permute-start.9
  74.7 2.3 %collective-permute-start.16 = (bf16[16,32,128]{2,1,0:T(8,128)(2,1)S(1)}, bf16[16,32,128]{2,1,0:T(8,128)(2,1)S(1)}, u32[]{:S(2)}, u32[]{:S(2)}) collective-permute-start(bf16[16,32,128]{2,1,0:T(8,128)(2,1)S(1)} %add_convert_fusion.refs_0_), channel_id=1, source_target_pairs={{0,12},{4,0},{8,4},{12,8},{1,13},{5,1},{9,5},{13,9},{2,14},{6,2},{... | collective-permute-start | bytes 393224 | tf_op jit(solution)/shard_map/ppermute | solution.py:19
  77.0 1.3 %collective-permute-start.15 = (bf16[16,32,128]{2,1,0:T(8,128)(2,1)S(1)}, bf16[16,32,128]{2,1,0:T(8,128)(2,1)S(1)}, u32[]{:S(2)}, u32[]{:S(2)}) collective-permute-start(bf16[16,32,128]{2,1,0:T(8,128)(2,1)S(1)} %add_convert_fusion.refs_0_), channel_id=1, source_target_pairs={{0,8},{4,12},{8,0},{12,4},{1,9},{5,13},{9,1},{13,5},{2,10},{6,14},... | collective-permute-start | bytes 393224 | tf_op jit(solution)/shard_map/ppermute | solution.py:19
  78.2 6.5 %near_own.3.refs_3_ = f32[33,32,128]{2,1,0:T(8,128)S(1)} custom-call(s32[3]{0:T(128)S(1)} %copy-done.4, s32[10,136]{1,0:T(8,128)S(1)} %get-tuple-element.9.plan_ref, bf16[32,32,128]{2,1,0:T(8,128)(2,1)S(1)} %get-tuple-element.14.refs_0_, bf16[32,32,128]{2,1,0:T(8,128)(2,1)S(1)} %collective-permute-done.12.refs_1_, bf16[128,128,256]{2,1,0:T(8,128)(2,1)} %refs_2_.9), custom_call_target="tpu_custom_call" | custom-call | tf_op jit(solution)/shard_map/near_own/pallas_call | solution.py:179
  84.8 6.3 %near_loop.3.refs_3_ = f32[33,32,128]{2,1,0:T(8,128)S(1)} custom-call(s32[3]{0:T(128)S(1)} %copy-done.4, s32[10,136]{1,0:T(8,128)S(1)} %get-tuple-element.9.plan_ref, bf16[32,32,128]{2,1,0:T(8,128)(2,1)S(1)} %collective-permute-done.8.refs_0_, bf16[32,32,128]{2,1,0:T(8,128)(2,1)S(1)} %collective-permute-done.10.refs_1_, bf16[128,128,256]{2,1,0:T(8,128)(2,1)} %refs_2_.9, ...), custom_call_target="tpu_custom_call" | custom-call | tf_op jit(solution)/shard_map/near_loop/pallas_call | solution.py:179
  91.1 4.0 %far.3.refs_4_ = bf16[32,32,64]{2,1,0:T(8,128)(2,1)S(1)} custom-call(s32[3]{0:T(128)S(1)} %copy-done.4, s32[2,128]{1,0:T(2,128)S(1)} %bitcast.13, bf16[128,64,64]{2,1,0:T(8,128)(2,1)S(1)} %copy.8.coupling_ref, bf16[16,32,128]{2,1,0:T(8,128)(2,1)S(1)} %add_convert_fusion.refs_0_, bf16[16,32,128]{2,1,0:T(8,128)(2,1)S(1)} %collective-permute-done.14.refs_1_, ...), custom_call_target="tpu_custom_call" | custom-call | tf_op jit(solution)/shard_map/far/pallas_call | solution.py:189
  95.1 7.3 %finish.3 = f32[32,32,128]{2,1,0:T(8,128)} custom-call(s32[3]{0:T(128)S(1)} %copy-done.4, s32[10,136]{1,0:T(8,128)S(1)} %get-tuple-element.9.plan_ref, bf16[32,32,128]{2,1,0:T(8,128)(2,1)S(1)} %collective-permute-done.9.refs_0_, bf16[32,32,128]{2,1,0:T(8,128)(2,1)S(1)} %collective-permute-done.11.refs_1_, bf16[128,128,256]{2,1,0:T(8,128)(2,1)} %refs_2_.9, ...), custom_call_target="tpu_custom_call" | custom-call | tf_op jit(solution)/shard_map/finish/pallas_call | solution.py:206
  (31 shorter events, 0.2 us)
Async XLA Ops:
  0.7 31.2 %copy-start.3 = (s32[3]{0:T(128)}, s32[3]{0:T(128)S(1)}, u32[]{:S(2)}) copy-start(s32[3]{0:T(128)S(1)} %pad_add_fusion.place_ref) | copy-start | bytes 40
  0.7 1.0 %copy-start = (bf16[32,128,64]{1,2,0:T(8,128)(2,1)S(1)}, bf16[32,128,64]{1,2,0:T(8,128)(2,1)}, u32[]{:S(2)}) copy-start(bf16[32,128,64]{1,2,0:T(8,128)(2,1)} %param.9) | copy-start | bytes 1572868
  1.8 1.2 %copy-start.2 = (f32[32,256,32]{1,2,0:T(8,128)S(1)}, f32[32,256,32]{1,2,0:T(8,128)}, u32[]{:S(2)}) copy-start(f32[32,256,32]{1,2,0:T(8,128)} %param.6) | copy-start | bytes 3145732
  3.0 0.7 copy-start.6
  10.1 11.8 %collective-permute-start.2 = (bf16[32,32,128]{2,1,0:T(8,128)(2,1)S(1)}, bf16[32,32,128]{2,1,0:T(8,128)(2,1)S(1)}, u32[]{:S(2)}, u32[]{:S(2)}) collective-permute-start(bf16[32,32,128]{2,1,0:T(8,128)(2,1)S(1)} %get-tuple-element.10), channel_id=1, source_target_pairs={{0,12},{4,0},{8,4},{12,8},{1,13},{5,1},{9,5},{13,9},{2,14},{6,2},{... | collective-permute-start | bytes 786440 | tf_op jit(solution)/shard_map/ppermute | solution.py:19
  15.2 12.1 %collective-permute-start = (bf16[32,32,128]{2,1,0:T(8,128)(2,1)S(1)}, bf16[32,32,128]{2,1,0:T(8,128)(2,1)S(1)}, u32[]{:S(2)}, u32[]{:S(2)}) collective-permute-start(bf16[32,32,128]{2,1,0:T(8,128)(2,1)S(1)} %get-tuple-element.10), channel_id=1, source_target_pairs={{0,4},{4,8},{8,12},{12,0},{1,5},{5,9},{9,13},{13,1},{2,6},{6,10},{... | collective-permute-start | bytes 786440 | tf_op jit(solution)/shard_map/ppermute | solution.py:19
  15.2 13.6 %collective-permute-start.4 = (bf16[16,32,128]{2,1,0:T(8,128)(2,1)S(1)}, bf16[16,32,128]{2,1,0:T(8,128)(2,1)S(1)}, u32[]{:S(2)}, u32[]{:S(2)}) collective-permute-start(bf16[16,32,128]{2,1,0:T(8,128)(2,1)S(1)} %convert_element_type.18), channel_id=1, source_target_pairs={{0,2},{2,0},{1,3},{3,1},{4,6},{6,4},{5,7},{7,5},{8,10},{10,8},{9,1... | collective-permute-start | bytes 393224 | tf_op jit(solution)/shard_map/ppermute | solution.py:19
  21.9 30.7 %collective-permute-start.3 = (bf16[32,32,128]{2,1,0:T(8,128)(2,1)S(1)}, bf16[32,32,128]{2,1,0:T(8,128)(2,1)S(1)}, u32[]{:S(2)}, u32[]{:S(2)}) collective-permute-start(bf16[32,32,128]{2,1,0:T(8,128)(2,1)S(1)} %collective-permute-done.2.refs_1_), channel_id=1, source_target_pairs={{0,2},{2,0},{1,3},{3,1},{4,6},{6,4},{5,7},{7,5},{8,10},{10,8},{9,1... | collective-permute-start | bytes 786440 | tf_op jit(solution)/shard_map/ppermute | solution.py:19
  27.3 25.3 %collective-permute-start.1 = (bf16[32,32,128]{2,1,0:T(8,128)(2,1)S(1)}, bf16[32,32,128]{2,1,0:T(8,128)(2,1)}, u32[]{:S(2)}, u32[]{:S(2)}) collective-permute-start(bf16[32,32,128]{2,1,0:T(8,128)(2,1)S(1)} %collective-permute-done.refs_0_), channel_id=1, source_target_pairs={{0,2},{2,0},{1,3},{3,1},{4,6},{6,4},{5,7},{7,5},{8,10},{10,8},{9,1... | collective-permute-start | bytes 786440 | tf_op jit(solution)/shard_map/ppermute | solution.py:19
  28.8 19.2 %collective-permute-start.7 = (bf16[16,32,128]{2,1,0:T(8,128)(2,1)S(1)}, bf16[16,32,128]{2,1,0:T(8,128)(2,1)}, u32[]{:S(2)}, u32[]{:S(2)}) collective-permute-start(bf16[16,32,128]{2,1,0:T(8,128)(2,1)S(1)} %add_convert_fusion.1.refs_0_), channel_id=1, source_target_pairs={{0,12},{4,0},{8,4},{12,8},{1,13},{5,1},{9,5},{13,9},{2,14},{6,2},{... | collective-permute-start | bytes 393224 | tf_op jit(solution)/shard_map/ppermute | solution.py:19
  30.6 17.4 %collective-permute-start.6 = (bf16[16,32,128]{2,1,0:T(8,128)(2,1)S(1)}, bf16[16,32,128]{2,1,0:T(8,128)(2,1)}, u32[]{:S(2)}, u32[]{:S(2)}) collective-permute-start(bf16[16,32,128]{2,1,0:T(8,128)(2,1)S(1)} %add_convert_fusion.1.refs_0_), channel_id=1, source_target_pairs={{0,8},{4,12},{8,0},{12,4},{1,9},{5,13},{9,1},{13,5},{2,10},{6,14},... | collective-permute-start | bytes 393224 | tf_op jit(solution)/shard_map/ppermute | solution.py:19
  32.0 16.1 %collective-permute-start.5 = (bf16[16,32,128]{2,1,0:T(8,128)(2,1)S(1)}, bf16[16,32,128]{2,1,0:T(8,128)(2,1)}, u32[]{:S(2)}, u32[]{:S(2)}) collective-permute-start(bf16[16,32,128]{2,1,0:T(8,128)(2,1)S(1)} %add_convert_fusion.1.refs_0_), channel_id=1, source_target_pairs={{0,4},{4,8},{8,12},{12,0},{1,5},{5,9},{9,13},{13,1},{2,6},{6,10},{... | collective-permute-start | bytes 393224 | tf_op jit(solution)/shard_map/ppermute | solution.py:19
  35.9 0.7 copy-start.4
  36.6 11.5 %copy-start.5 = (s32[128,2]{0,1:T(2,128)S(1)}, s32[128,2]{0,1:T(2,128)}, u32[]{:S(2)}) copy-start(s32[128,2]{0,1:T(2,128)} %param.11) | copy-start | bytes 3076
  41.7 10.9 %copy-start.1 = (bf16[32,128,64]{1,2,0:T(8,128)(2,1)S(1)}, bf16[32,128,64]{1,2,0:T(8,128)(2,1)}, u32[]{:S(2)}) copy-start(bf16[32,128,64]{1,2,0:T(8,128)(2,1)} %param.9) | copy-start | bytes 1572868
  60.0 10.5 %collective-permute-start.10 = (bf16[32,32,128]{2,1,0:T(8,128)(2,1)S(1)}, bf16[32,32,128]{2,1,0:T(8,128)(2,1)S(1)}, u32[]{:S(2)}, u32[]{:S(2)}) collective-permute-start(bf16[32,32,128]{2,1,0:T(8,128)(2,1)S(1)} %get-tuple-element.14.refs_0_), channel_id=1, source_target_pairs={{0,12},{4,0},{8,4},{12,8},{1,13},{5,1},{9,5},{13,9},{2,14},{6,2},{... | collective-permute-start | bytes 786440 | tf_op jit(solution)/shard_map/ppermute | solution.py:19
  64.1 10.0 %collective-permute-start.8 = (bf16[32,32,128]{2,1,0:T(8,128)(2,1)S(1)}, bf16[32,32,128]{2,1,0:T(8,128)(2,1)S(1)}, u32[]{:S(2)}, u32[]{:S(2)}) collective-permute-start(bf16[32,32,128]{2,1,0:T(8,128)(2,1)S(1)} %get-tuple-element.14.refs_0_), channel_id=1, source_target_pairs={{0,4},{4,8},{8,12},{12,0},{1,5},{5,9},{9,13},{13,1},{2,6},{6,10},{... | collective-permute-start | bytes 786440 | tf_op jit(solution)/shard_map/ppermute | solution.py:19
  64.1 10.5 %collective-permute-start.13 = (bf16[16,32,128]{2,1,0:T(8,128)(2,1)S(1)}, bf16[16,32,128]{2,1,0:T(8,128)(2,1)S(1)}, u32[]{:S(2)}, u32[]{:S(2)}) collective-permute-start(bf16[16,32,128]{2,1,0:T(8,128)(2,1)S(1)} %convert_element_type.21), channel_id=1, source_target_pairs={{0,2},{2,0},{1,3},{3,1},{4,6},{6,4},{5,7},{7,5},{8,10},{10,8},{9,1... | collective-permute-start | bytes 393224 | tf_op jit(solution)/shard_map/ppermute | solution.py:19
  64.7 13.6 %collective-permute-start.12 = (bf16[32,32,128]{2,1,0:T(8,128)(2,1)S(1)}, bf16[32,32,128]{2,1,0:T(8,128)(2,1)S(1)}, u32[]{:S(2)}, u32[]{:S(2)}) collective-permute-start(bf16[32,32,128]{2,1,0:T(8,128)(2,1)S(1)} %get-tuple-element.14.refs_0_), channel_id=1, source_target_pairs={{0,2},{2,0},{1,3},{3,1},{4,6},{6,4},{5,7},{7,5},{8,10},{10,8},{9,1... | collective-permute-start | bytes 786440 | tf_op jit(solution)/shard_map/ppermute | solution.py:19
  70.5 24.5 %collective-permute-start.11 = (bf16[32,32,128]{2,1,0:T(8,128)(2,1)S(1)}, bf16[32,32,128]{2,1,0:T(8,128)(2,1)S(1)}, u32[]{:S(2)}, u32[]{:S(2)}) collective-permute-start(bf16[32,32,128]{2,1,0:T(8,128)(2,1)S(1)} %collective-permute-done.10.refs_1_), channel_id=1, source_target_pairs={{0,2},{2,0},{1,3},{3,1},{4,6},{6,4},{5,7},{7,5},{8,10},{10,8},{9,1... | collective-permute-start | bytes 786440 | tf_op jit(solution)/shard_map/ppermute | solution.py:19
  74.1 21.0 %collective-permute-start.9 = (bf16[32,32,128]{2,1,0:T(8,128)(2,1)S(1)}, bf16[32,32,128]{2,1,0:T(8,128)(2,1)S(1)}, u32[]{:S(2)}, u32[]{:S(2)}) collective-permute-start(bf16[32,32,128]{2,1,0:T(8,128)(2,1)S(1)} %collective-permute-done.8.refs_0_), channel_id=1, source_target_pairs={{0,2},{2,0},{1,3},{3,1},{4,6},{6,4},{5,7},{7,5},{8,10},{10,8},{9,1... | collective-permute-start | bytes 786440 | tf_op jit(solution)/shard_map/ppermute | solution.py:19
  74.7 16.4 %collective-permute-start.16 = (bf16[16,32,128]{2,1,0:T(8,128)(2,1)S(1)}, bf16[16,32,128]{2,1,0:T(8,128)(2,1)S(1)}, u32[]{:S(2)}, u32[]{:S(2)}) collective-permute-start(bf16[16,32,128]{2,1,0:T(8,128)(2,1)S(1)} %add_convert_fusion.refs_0_), channel_id=1, source_target_pairs={{0,12},{4,0},{8,4},{12,8},{1,13},{5,1},{9,5},{13,9},{2,14},{6,2},{... | collective-permute-start | bytes 393224 | tf_op jit(solution)/shard_map/ppermute | solution.py:19
  77.0 14.1 %collective-permute-start.15 = (bf16[16,32,128]{2,1,0:T(8,128)(2,1)S(1)}, bf16[16,32,128]{2,1,0:T(8,128)(2,1)S(1)}, u32[]{:S(2)}, u32[]{:S(2)}) collective-permute-start(bf16[16,32,128]{2,1,0:T(8,128)(2,1)S(1)} %add_convert_fusion.refs_0_), channel_id=1, source_target_pairs={{0,8},{4,12},{8,0},{12,4},{1,9},{5,13},{9,1},{13,5},{2,10},{6,14},... | collective-permute-start | bytes 393224 | tf_op jit(solution)/shard_map/ppermute | solution.py:19
  78.2 12.8 %collective-permute-start.14 = (bf16[16,32,128]{2,1,0:T(8,128)(2,1)S(1)}, bf16[16,32,128]{2,1,0:T(8,128)(2,1)S(1)}, u32[]{:S(2)}, u32[]{:S(2)}) collective-permute-start(bf16[16,32,128]{2,1,0:T(8,128)(2,1)S(1)} %add_convert_fusion.refs_0_), channel_id=1, source_target_pairs={{0,4},{4,8},{8,12},{12,0},{1,5},{5,9},{9,13},{13,1},{2,6},{6,10},{... | collective-permute-start | bytes 393224 | tf_op jit(solution)/shard_map/ppermute | solution.py:19

commit v2 on v0

--- a/solution.py
+++ b/solution.py
@@ -1,7 +1,370 @@
+import functools
+
 import jax
 import jax.numpy as jnp
 from jax import lax
+from jax.experimental import pallas as pl
+from jax.experimental.pallas import tpu as pltpu
 from jax.sharding import PartitionSpec as P
+
+UNROLL = 16
+FIELD = 9
+FAR_UNROLL = 32
+VMEM = pl.BlockSpec(memory_space=pltpu.VMEM)
+ANY = pl.BlockSpec(memory_space=pl.ANY)
+HBM = pl.BlockSpec(memory_space=pltpu.HBM)
+SMEM = pl.BlockSpec(memory_space=pltpu.SMEM)
+TRANSPOSED_RHS = (((1,), (1,)), ((), ()))
+PLAIN = (((1,), (0,)), ((), ()))
+
+
+def swapped(array, axis, partner):
+    return lax.ppermute(array, axis, [(i, partner(i)) for i in range(lax.axis_size(axis))])
+
+
+def dot(a, b, dims):
+    return lax.dot_general(a, b, dims, preferred_element_type=jnp.float32)
+
+
+def params(mebibytes=14):
+    return pltpu.CompilerParams(vmem_limit_bytes=mebibytes << 20)
+
+
+def in_hbm(array):
+    return pltpu.with_memory_space_constraint(array, pltpu.HBM)
+
+
+def cost(microseconds):
+    return pl.CostEstimate(flops=0, transcendentals=0, bytes_accessed=int(microseconds * 3.69e6))
+
+
+def put_projection(place_ref, low_ref, basis_ref, keep_ref, send_ref, at, parts):
+    quarter = keep_ref.shape[0]
+    for part in range(2):
+        for n in range(quarter):
+            m = 2 * part * quarter + n
+            pair = [dot(low_ref[i], basis_ref[i], TRANSPOSED_RHS) for i in (m, m + quarter)]
+            parts[part, n] = jnp.concatenate(pair, 1)
+    keep_ref[...] = parts[place_ref[1]]
+    send_ref[at:] = parts[1 - place_ref[1]].astype(jnp.bfloat16)
+
+
+def start_kernel(place_ref, panel_hbm, basis_hbm, mine_ref, basis_ref, keep_ref, send_ref, panel, parts, arrived):
+    slab = basis_ref.shape[2]
+    offset = pl.multiple_of(place_ref[1] * slab, slab)
+    pieces = arrived.shape[0] // 2
+    size = panel.shape[0] // pieces
+    for i in range(pieces):
+        rows = pl.ds(i * size, size)
+        pltpu.make_async_copy(panel_hbm.at[rows, :, pl.ds(offset, slab)], panel.at[rows], arrived.at[i]).start()
+        pltpu.make_async_copy(basis_hbm.at[rows], basis_ref.at[rows], arrived.at[pieces + i]).start()
+    for i in range(pieces):
+        rows = pl.ds(i * size, size)
+        pltpu.make_async_copy(panel_hbm.at[rows, :, pl.ds(offset, slab)], panel.at[rows], arrived.at[i]).wait()
+        mine_ref[rows] = panel[rows].astype(jnp.bfloat16)
+    for i in range(pieces):
+        rows = pl.ds(i * size, size)
+        pltpu.make_async_copy(basis_hbm.at[rows], basis_ref.at[rows], arrived.at[pieces + i]).wait()
+    put_projection(place_ref, mine_ref, basis_ref, keep_ref, send_ref, 0, parts)
+
+
+def put_sorted(words_ref, kinds, nothing, plan_ref):
+    count, width = words_ref.shape[1], plan_ref.shape[1]
+    across = jnp.broadcast_to(words_ref[...], (count, count))
+    down = across.T
+    kind_across, kind_down = lax.shift_right_logical(across, 3 * FIELD), lax.shift_right_logical(down, 3 * FIELD)
+    t = lax.broadcasted_iota(jnp.int32, (count, count), 1)
+    s = lax.broadcasted_iota(jnp.int32, (count, count), 0)
+    before = jnp.sum(((kind_across == kind_down) & (t < s)).astype(jnp.float32), 1, keepdims=True).astype(jnp.int32)
+    word = down[:, :1]
+    place = lax.broadcasted_iota(jnp.int32, (count, width), 1)
+    slot = lax.broadcasted_iota(jnp.int32, (1, width), 1)
+    totals = jnp.zeros((1, width), jnp.int32)
+    for kind in range(kinds):
+        of_kind = kind_down[:, :1] == kind
+        total = jnp.sum(of_kind.astype(jnp.float32), 0, keepdims=True).astype(jnp.int32)
+        row = jnp.sum(jnp.where(of_kind & (before == place), word, 0), 0, keepdims=True)
+        plan_ref[kind : kind + 1] = jnp.where(slot < total, row, nothing)
+        totals = jnp.where(slot == kind, total, totals)
+    plan_ref[kinds : kinds + 1] = totals
+
+
+def plan_kernel(nothing, near_ref, far_ref, near_plan_ref, far_plan_ref):
+    put_sorted(near_ref, 3, nothing, near_plan_ref)
+    put_sorted(far_ref, 2, nothing, far_plan_ref)
+
+
+def prepare_kernel(far_plan_ref, blocks_hbm, coupling_hbm, blocks_ref, pairs_ref, coupling, turned, arrived):
+    pieces = arrived.shape[0] - 1
+    size = blocks_ref.shape[0] // pieces
+    first = pltpu.make_async_copy(coupling_hbm, coupling, arrived.at[pieces])
+    first.start()
+    copies = [
+        pltpu.make_async_copy(
+            blocks_hbm.at[pl.ds(i * size, size)], blocks_ref.at[pl.ds(i * size, size)], arrived.at[i]
+        )
+        for i in range(pieces)
+    ]
+    for copy in copies:
+        copy.start()
+    first.wait()
+    rank, _, count = coupling.shape
+    for k in range(rank):
+        turned[k * count : (k + 1) * count] = coupling[k].astype(jnp.float32).T
+
+    def step(i, carry):
+        for j in range(FAR_UNROLL):
+            at = i * FAR_UNROLL + j
+            pair = lax.shift_right_logical(far_plan_ref[0, at], 2 * FIELD) & ((1 << FIELD) - 1)
+            pairs_ref[at] = turned[pl.ds(pair, rank, stride=count)].astype(jnp.bfloat16)
+        return carry
+
+    lax.fori_loop(0, lax.div(far_plan_ref[2, 0] + FAR_UNROLL - 1, FAR_UNROLL), step, 0)
+    for copy in copies:
+        copy.wait()
+
+
+def add_near(plan_ref, kind, source_ref, blocks_ref, acc_ref):
+    mask = (1 << FIELD) - 1
+
+    def step(i, carry):
+        words = [plan_ref[kind, i * UNROLL + j] for j in range(UNROLL)]
+        terms = []
+        for word in words:
+            block = blocks_ref[lax.shift_right_logical(word, 2 * FIELD) & mask]
+            terms.append(dot(source_ref[word & mask], block, TRANSPOSED_RHS))
+        for word, term in zip(words, terms):
+            row = lax.shift_right_logical(word, FIELD) & mask
+            acc_ref[row] = acc_ref[row] + term
+        return carry
+
+    lax.fori_loop(0, lax.div(plan_ref[3, kind] + UNROLL - 1, UNROLL), step, 0)
+
+
+def near_own_kernel(plan_ref, panel_hbm, blocks_ref, acc_ref, panel, low, arrived):
+    copy = pltpu.make_async_copy(panel_hbm, panel, arrived)
+    copy.start()
+    acc_ref[...] = jnp.zeros_like(acc_ref)
+    copy.wait()
+    low[...] = panel[...].astype(jnp.bfloat16)
+    add_near(plan_ref, 0, low, blocks_ref, acc_ref)
+
+
+def put_whole(place_ref, same_ref, other_ref, whole):
+    slab = same_ref.shape[2]
+    first = place_ref[1] == 0
+    same, other = same_ref[...], other_ref[: same_ref.shape[0]]
+    whole[:, :, :slab] = jnp.where(first, same, other)
+    whole[:, :, slab:] = jnp.where(first, other, same)
+
+
+def near_halves_kernel(kind, place_ref, plan_ref, same_ref, other_ref, blocks_ref, *refs):
+    acc_ref, whole = refs[-2:]
+    put_whole(place_ref, same_ref, other_ref, whole)
+    acc_ref[...] = refs[0][...] if len(refs) == 3 else jnp.zeros_like(acc_ref)
+    add_near(plan_ref, kind, whole, blocks_ref, acc_ref)
+
+
+def far_kernel(plan_ref, pairs_ref, *refs):
+    held, keep_ref, send_ref, unpacked, acc = refs[:-4], *refs[-4:]
+    clusters = keep_ref.shape[0]
+    quarter = held[0].shape[0]
+    rank = pairs_ref.shape[1]
+    mask = (1 << FIELD) - 1
+    for d, packed in enumerate(held):
+        unpacked[2 * d * quarter : (2 * d + 1) * quarter] = packed[:, :, :rank]
+        unpacked[(2 * d + 1) * quarter : (2 * d + 2) * quarter] = packed[:, :, rank:]
+    acc[...] = jnp.zeros_like(acc)
+
+    def step(i, carry):
+        words = [plan_ref[0, i * FAR_UNROLL + j] for j in range(FAR_UNROLL)]
+        terms = []
+        for j, word in enumerate(words):
+            terms.append(dot(unpacked[word & mask], pairs_ref[i * FAR_UNROLL + j], TRANSPOSED_RHS))
+        for word, term in zip(words, terms):
+            row = lax.shift_right_logical(word, FIELD) & mask
+            acc[row] = acc[row] + term
+        return carry
+
+    lax.fori_loop(0, lax.div(plan_ref[2, 0] + FAR_UNROLL - 1, FAR_UNROLL), step, 0)
+    half = clusters // 2
+    for n in range(half):
+        keep_ref[n] = acc[n]
+        keep_ref[n + half] = acc[n + half]
+        send_ref[n] = jnp.concatenate([acc[n], acc[n + half]], 1).astype(jnp.bfloat16)
+
+
+def finish_kernel(place_ref, plan_ref, same_ref, other_ref, blocks_ref, acc_in, far_ref, far_other_ref, basis_ref, *refs):
+    out_ref, (acc_ref, whole) = refs[0], refs[-2:]
+    near_halves_kernel(2, place_ref, plan_ref, same_ref, other_ref, blocks_ref, acc_in, acc_ref, whole)
+    half, _, wide = far_other_ref.shape
+    rank = wide // 2
+    for n in range(half):
+        for m, other in ((n, far_other_ref[n, :, :rank]), (n + half, far_other_ref[n, :, rank:])):
+            far_low = (far_ref[m] + other.astype(jnp.float32)).astype(jnp.bfloat16)
+            out_ref[m] = acc_ref[m] + dot(far_low, basis_ref[m], PLAIN)
+    if len(refs) == 7:
+        mine_ref, keep_ref, send_ref, parts = refs[1:5]
+        low = out_ref[...].astype(jnp.bfloat16)
+        mine_ref[...] = low
+        send_ref[: 2 * half] = low
+        put_projection(place_ref, mine_ref, basis_ref, keep_ref, send_ref, 2 * half, parts)
+
+
+def tiled_on_device(right_panel, near_field_blocks, near_list, cluster_basis, coupling, far_list):
+    clusters, points, columns = right_panel.shape
+    near_count = near_list.shape[0]
+    slab, rank = cluster_basis.shape[1:]
+    panel = right_panel.transpose(0, 2, 1)
+    basis = cluster_basis.transpose(0, 2, 1)
+    cycle = lax.axis_size("blk")
+    place = jnp.stack([lax.axis_index("blk"), lax.axis_index("basis")]).astype(jnp.int32)
+    half, quarter = clusters // 2, clusters // 4
+    near_owner, far_owner = near_list[:, 1] // clusters, far_list[:, 1] // clusters
+    words = jnp.where(near_owner == place[0], 0, jnp.where(near_owner == place[0] ^ 1, 1, 2))
+    words = words << FIELD | jnp.arange(near_count, dtype=jnp.int32)
+    words = words << FIELD | near_list[:, 0] - place[0] * clusters
+    words = words << FIELD | near_list[:, 1] % clusters
+    far_source = far_list[:, 1] % clusters
+    far_words = (far_source // half != place[1]).astype(jnp.int32)
+    far_words = far_words << FIELD | jnp.arange(far_list.shape[0], dtype=jnp.int32)
+    far_words = far_words << FIELD | far_list[:, 0] - place[0] * clusters
+    far_words = far_words << FIELD | (place[0] ^ far_owner) * half + far_source % half
+    f32, bf16 = jnp.float32, jnp.bfloat16
+    mine_shape = jax.ShapeDtypeStruct((clusters, columns, slab), bf16)
+    keep_shape = jax.ShapeDtypeStruct((quarter, columns, 2 * rank), f32)
+    send_shape = jax.ShapeDtypeStruct((quarter, columns, 2 * rank), bf16)
+    both_shape = jax.ShapeDtypeStruct((clusters + quarter, columns, slab), bf16)
+    parts = pltpu.VMEM((2, quarter, columns, 2 * rank), f32)
+    out_shape = jax.ShapeDtypeStruct((clusters, columns, slab), f32)
+    acc_shape = jax.ShapeDtypeStruct((clusters + 1, columns, slab), f32)
+    near_plan_shape = jax.ShapeDtypeStruct((4, near_count + UNROLL), jnp.int32)
+    far_plan_shape = jax.ShapeDtypeStruct((3, far_list.shape[0] + FAR_UNROLL), jnp.int32)
+
+    low_shape = jax.ShapeDtypeStruct((clusters, columns, points), bf16)
+    pieces = 4
+    mine, basis, keep, send = pl.pallas_call(
+        start_kernel,
+        out_shape=(mine_shape, jax.ShapeDtypeStruct(basis.shape, bf16), keep_shape, send_shape),
+        in_specs=[SMEM, HBM, HBM],
+        out_specs=(VMEM,) * 4,
+        scratch_shapes=[pltpu.VMEM(mine_shape.shape, f32), parts, pltpu.SemaphoreType.DMA((2 * pieces,))],
+        compiler_params=params(),
+        cost_estimate=cost(2),
+        name="start",
+    )(place, in_hbm(panel), in_hbm(basis))
+    near_plan, far_plan = pl.pallas_call(
+        functools.partial(plan_kernel, clusters << FIELD),
+        out_shape=(near_plan_shape, far_plan_shape),
+        in_specs=[VMEM, VMEM],
+        out_specs=(VMEM, VMEM),
+        compiler_params=params(),
+        cost_estimate=cost(1),
+        name="plan",
+    )(words[None], far_words[None])
+    blocks, pairs = pl.pallas_call(
+        prepare_kernel,
+        out_shape=(
+            pltpu.VMEM(near_field_blocks.shape, bf16),
+            pltpu.VMEM((coupling.shape[0] + FAR_UNROLL, rank, rank), bf16),
+        ),
+        in_specs=[SMEM, HBM, HBM],
+        out_specs=(VMEM, VMEM),
+        scratch_shapes=[
+            pltpu.VMEM((rank, rank, coupling.shape[0]), bf16),
+            pltpu.VMEM((rank * coupling.shape[0], rank), f32),
+            pltpu.SemaphoreType.DMA((9,)),
+        ],
+        compiler_params=params(20),
+        cost_estimate=cost(4),
+        name="prepare",
+    )(far_plan, in_hbm(near_field_blocks), in_hbm(coupling.transpose(1, 2, 0)))
+
+    def near_own(plan, blocks):
+        return pl.pallas_call(
+            near_own_kernel,
+            out_shape=acc_shape,
+            in_specs=[SMEM, HBM, VMEM],
+            out_specs=VMEM,
+            scratch_shapes=[
+                pltpu.VMEM(panel.shape, f32),
+                pltpu.VMEM(low_shape.shape, bf16),
+                pltpu.SemaphoreType.DMA,
+            ],
+            compiler_params=params(),
+            cost_estimate=cost(3),
+            name="near_own",
+        )(plan, panel, blocks)
+
+    def near_halves(plan, blocks, kind, same, other, *acc):
+        return pl.pallas_call(
+            functools.partial(near_halves_kernel, kind),
+            out_shape=acc_shape,
+            in_specs=[SMEM, SMEM] + [VMEM] * (3 + len(acc)),
+            out_specs=VMEM,
+            scratch_shapes=[pltpu.VMEM(low_shape.shape, bf16)],
+            compiler_params=params(),
+            cost_estimate=cost(2),
+            name="near_halves",
+        )(place, plan, same, other, blocks, *acc)
+
+    def far(plan, held):
+        return pl.pallas_call(
+            far_kernel,
+            out_shape=(
+                jax.ShapeDtypeStruct((clusters, columns, rank), f32),
+                jax.ShapeDtypeStruct((half, columns, 2 * rank), bf16),
+            ),
+            in_specs=[SMEM, VMEM] + [VMEM] * len(held),
+            out_specs=(VMEM, VMEM),
+            scratch_shapes=[
+                pltpu.VMEM((cycle * half, columns, rank), bf16),
+                pltpu.VMEM((clusters + 1, columns, rank), f32),
+            ],
+            compiler_params=params(),
+            cost_estimate=cost(3),
+            name="far",
+        )(plan, pairs, *held)
+
+    def finish(plan, blocks, same, other, acc, far_sum, far_other, last):
+        outs = (out_shape,) if last else (out_shape, mine_shape, keep_shape, both_shape)
+        return pl.pallas_call(
+            finish_kernel,
+            out_shape=outs,
+            in_specs=[SMEM, SMEM] + [VMEM] * 7,
+            out_specs=(VMEM,) * len(outs),
+            scratch_shapes=([] if last else [parts])
+            + [pltpu.VMEM(acc_shape.shape, f32), pltpu.VMEM(low_shape.shape, bf16)],
+            compiler_params=params(),
+            cost_estimate=cost(4),
+            name="finish",
+        )(place, plan, same, other, blocks, acc, far_sum, far_other, basis)
+
+    def other_basis(array):
+        return swapped(array, "basis", lambda i: 1 - i)
+
+    def apply_operator(mine, keep, send, near_plan, last):
+        between = swapped(mine, "blk", lambda i: (((i + 1) % cycle ^ 1) - 1) % cycle)
+        paired = swapped(mine, "blk", lambda i: i ^ 1)
+        received = other_basis(send)
+        if last:
+            acc = near_halves(near_plan, blocks, 0, mine, received)
+        else:
+            acc = near_own(near_plan, blocks)
+        held = [(keep + received[-quarter:].astype(f32)).astype(bf16)]
+        held += [swapped(held[0], "blk", lambda i, d=d: i ^ d) for d in range(1, cycle)]
+        paired, acc = lax.optimization_barrier((paired, acc))
+        between, *held = lax.optimization_barrier((between, *held))
+        paired_other = other_basis(paired)
+        between_other = other_basis(between)
+        far_sum, far_send = far(far_plan, held)
+        far_other = other_basis(far_send)
+        acc = near_halves(near_plan, blocks, 1, paired, paired_other, acc)
+        return finish(near_plan, blocks, between, between_other, acc, far_sum, far_other, last), near_plan
+
+    (first, mine, keep, send), near_plan = apply_operator(mine, keep, send, near_plan, False)
+    (second,), _ = apply_operator(mine, keep, send, near_plan, True)
+    return first.transpose(0, 2, 1), second.transpose(0, 2, 1)
 
 
 def from_behind(array, axis, by):
@@ -9,7 +372,7 @@
     return lax.ppermute(array, axis, [(i, (i + by) % size) for i in range(size)])
 
 
-def on_device(right_panel, near_field_blocks, near_list, cluster_basis, coupling, far_list):
+def general_on_device(right_panel, near_field_blocks, near_list, cluster_basis, coupling, far_list):
     highest_precision = lax.Precision.HIGHEST
     clusters = right_panel.shape[0]
     slab_rows = cluster_basis.shape[1]
@@ -64,6 +427,13 @@
     return (krylov_one, krylov_two)
 
 
+def on_device(right_panel, near_field_blocks, near_list, cluster_basis, coupling, far_list):
+    cycle = lax.axis_size("blk")
+    tiled = lax.axis_size("basis") == 2 and cluster_basis.shape[1] % 128 == 0 and cycle & (cycle - 1) == 0
+    run = tiled_on_device if tiled else general_on_device
+    return run(right_panel, near_field_blocks, near_list, cluster_basis, coupling, far_list)
+
+
 def solution(mesh):
     placed = (
         P(("groups", "blk"), None, "col"),

time: 147 us -> 74.4 us (0.51)
  blocking collectives: 87.6 us -> 0 us
  matrix products: 29 us -> 0 us
  Pallas kernels: 0 us -> 28.1 us
  waiting for transfers between devices: 0.01 us -> 20.9 us
  starting transfers between devices: 8 us -> 23.9 us
  local copies, waits for them, and re-layouts: 15.4 us -> 0.01 us
  other arithmetic: 5.65 us -> 0.9 us
    all_gather x3 -> x0, blocking collectives: 54.9 us -> none  [the longest x2 47.8 us: apply_operator(): projections_all = lax.all_gather(projected, 'blk', axis=0, tiled=True)]
    psum x2 -> x0, blocking collectives: 32.8 us -> none  [apply_operator(): projected = lax.psum(partial_sum, 'basis').astype(jnp.bfloat16)]
    dot_general x12 -> x0, matrix products: 29 us -> none  [the longest x2 13.9 us: apply_operator(): jnp.einsum('fpz,fzg->fpg', near_field_blocks, source_vector, preferred_el...]
    pallas_call x0 -> x11, Pallas kernels: none -> 28.1 us  [the longest x2 6.78 us: finish(): pl.pallas_call(finish_kernel, out_shape=outs, in_specs=[SMEM, SMEM] + [VM...]
    ppermute x4 -> x18, waiting for transfers between devices: 0.01 us -> 20.9 us  [swapped(): lax.ppermute(array, axis, [(i, partner(i)) for i in range(lax.axis_size(a...]
    ppermute x4 -> x18, starting transfers between devices: 8 us -> 23.9 us  [swapped(): lax.ppermute(array, axis, [(i, partner(i)) for i in range(lax.axis_size(a...]
    gather x4 -> x0, local copies, waits for them, and re-layouts: 10.7 us -> none  [the longest x2 6.71 us: apply_operator(): projections_all[far_list[:, 1]]]
    unnamed x7 -> x2, local copies, waits for them, and re-layouts: 4.73 us -> 0.01 us
  transfers between devices with their start and end apart: 4 -> 18, of which waited for: 0 -> 8; matrix products, arithmetic and copies ran while one was open for 14% -> 1% of each run, Pallas kernels for 0% -> 25%
where the time goes in v2:
time: 74.4 us; the launch traced here: 74.6 us
  Pallas kernels  28.1 us (38%)
  starting transfers between devices  23.9 us (32%)
  waiting for transfers between devices  20.9 us (28%)
  other arithmetic  0.9 us (1%)
  between operations  0.76 us (1%)
    ppermute x18, starting transfers between devices, swapped(): lax.ppermute(array, axis, [(i, partner(i)) for i in range(lax.axis_size(a...  23.9 us
    ppermute x18, waiting for transfers between devices, swapped(): lax.ppermute(array, axis, [(i, partner(i)) for i in range(lax.axis_size(a...  20.9 us
    pallas_call x2, Pallas kernels, finish(): pl.pallas_call(finish_kernel, out_shape=outs, in_specs=[SMEM, SMEM] + [VM...  6.78 us
    pallas_call x3, Pallas kernels, near_halves(): pl.pallas_call(functools.partial(near_halves_kernel, kind), out_shape=acc...  6.34 us
    pallas_call x1, Pallas kernels, tiled_on_device(): pl.pallas_call(prepare_kernel, out_shape=(pltpu.VMEM(near_field_blocks.sh...  5.8 us
    pallas_call x2, Pallas kernels, far(): pl.pallas_call(far_kernel, out_shape=(jax.ShapeDtypeStruct((clusters, col...  4.19 us
    pallas_call x1, Pallas kernels, tiled_on_device(): pl.pallas_call(start_kernel, out_shape=(mine_shape, jax.ShapeDtypeStruct(...  2.37 us
    pallas_call x1, Pallas kernels, near_own(): pl.pallas_call(near_own_kernel, out_shape=acc_shape, in_specs=[SMEM, HBM,...  2.16 us
  transfers between devices with their start and end apart: 18, of which 8 were waited for; matrix products, arithmetic and copies ran while one was open for 1% of the time, Pallas kernels for 25%

profile of v2, /device:TPU:0, one launch (start us, length us, event | category | flops | bytes accessed | tf_op | source)
XLA Modules:
  0.0 74.6 jit_solution(12379073940144502910)
XLA Ops:
  0.7 2.4 %start.1 = (bf16[32,32,128]{2,1,0:T(8,128)(2,1)S(1)}, bf16[32,64,128]{2,1,0:T(8,128)(2,1)S(1)}, f32[8,32,128]{2,1,0:T(8,128)S(1)}, bf16[8,32,128]{2,1,0:T(8,128)(2,1)S(1)}) custom-call(s32[2]{0:T(128)S(1)} %pad_add_fusion.place_ref, f32[32,32,256]{2,1,0:T(8,128)} %bitcast.45, bf16[32,64,128]{2,1,0:T(8,128)(2,1)} %bitcast.48), custom_call_target="tpu_custom_call" | custom-call | bytes 7380000 | tf_op jit(solution)/shard_map/start/pallas_call | solution.py:246
  3.1 3.0 %collective-permute-start.1 = (bf16[8,32,128]{2,1,0:T(8,128)(2,1)S(1)}, bf16[8,32,128]{2,1,0:T(8,128)(2,1)S(1)}, u32[]{:S(2)}, u32[]{:S(2)}) collective-permute-start(bf16[8,32,128]{2,1,0:T(8,128)(2,1)S(1)} %get-tuple-element.35), channel_id=1, source_target_pairs={{0,2},{2,0},{1,3},{3,1},{4,6},{6,4},{5,7},{7,5},{8,10},{10,8},{9,1... | collective-permute-start | bytes 196616 | tf_op jit(solution)/shard_map/ppermute | solution.py:22
  6.1 1.6 %collective-permute-start.6 = (bf16[32,32,128]{2,1,0:T(8,128)(2,1)S(1)}, bf16[32,32,128]{2,1,0:T(8,128)(2,1)S(1)}, u32[]{:S(2)}, u32[]{:S(2)}) collective-permute-start(bf16[32,32,128]{2,1,0:T(8,128)(2,1)S(1)} %get-tuple-element.33), channel_id=1, source_target_pairs={{0,4},{4,0},{8,12},{12,8},{1,5},{5,1},{9,13},{13,9},{2,6},{6,2},{1... | collective-permute-start | bytes 786440 | tf_op jit(solution)/shard_map/ppermute | solution.py:22
  7.7 2.5 %collective-permute-start = (bf16[32,32,128]{2,1,0:T(8,128)(2,1)S(1)}, bf16[32,32,128]{2,1,0:T(8,128)(2,1)S(1)}, u32[]{:S(2)}, u32[]{:S(2)}) collective-permute-start(bf16[32,32,128]{2,1,0:T(8,128)(2,1)S(1)} %get-tuple-element.33), channel_id=1, source_target_pairs={{0,12},{4,8},{8,4},{12,0},{1,13},{5,9},{9,5},{13,1},{2,14},{6,10},... | collective-permute-start | bytes 786440 | tf_op jit(solution)/shard_map/ppermute | solution.py:22
  10.2 2.4 %collective-permute-start.4 = (bf16[8,32,128]{2,1,0:T(8,128)(2,1)S(1)}, bf16[8,32,128]{2,1,0:T(8,128)(2,1)S(1)}, u32[]{:S(2)}, u32[]{:S(2)}) collective-permute-start(bf16[8,32,128]{2,1,0:T(8,128)(2,1)S(1)} %add_convert_fusion.1.refs_0_), channel_id=1, source_target_pairs={{0,12},{4,8},{8,4},{12,0},{1,13},{5,9},{9,5},{13,1},{2,14},{6,10},... | collective-permute-start | bytes 196616 | tf_op jit(solution)/shard_map/ppermute | solution.py:22
  12.6 2.1 %collective-permute-start.2 = (bf16[8,32,128]{2,1,0:T(8,128)(2,1)S(1)}, bf16[8,32,128]{2,1,0:T(8,128)(2,1)S(1)}, u32[]{:S(2)}, u32[]{:S(2)}) collective-permute-start(bf16[8,32,128]{2,1,0:T(8,128)(2,1)S(1)} %add_convert_fusion.1.refs_0_), channel_id=1, source_target_pairs={{0,4},{4,0},{8,12},{12,8},{1,5},{5,1},{9,13},{13,9},{2,6},{6,2},{1... | collective-permute-start | bytes 196616 | tf_op jit(solution)/shard_map/ppermute | solution.py:22
  14.6 0.8 %fusion = (s32[1,128]{1,0:T(1,128)S(1)}, s32[1,128]{1,0:T(1,128)S(1)}) fusion(s32[128,2]{0,1:T(2,128)} %param.8, s32[]{:T(128)S(6)} %mul.15, s32[]{:T(128)S(6)} %xor.14, s32[]{:T(128)} %axis_index.25, s32[128,2]{0,1:T(2,128)} %param.11, s32[]{:T(128)} %axis_index.28), kind=kLoop, calls=%fused_computation.20 | loop fusion | flops 10240 | bytes 3088 | tf_op jit(solution)/shard_map/or | solution.py:227
  15.4 0.4 plan.1
  15.9 5.8 %prepare.1 = (bf16[128,128,256]{2,1,0:T(8,128)(2,1)S(1)}, bf16[160,64,64]{2,1,0:T(8,128)(2,1)S(1)}) custom-call(s32[3,160]{1,0:T(4,128)S(1)} %get-tuple-element.37.far_plan_ref.plan_ref, bf16[128,128,256]{2,1,0:T(8,128)(2,1)} %blocks_hbm.1, bf16[64,64,128]{2,1,0:T(8,128)(2,1)} %bitcast.47), custom_call_target="tpu_custom_call" | custom-call | bytes 14760000 | tf_op jit(solution)/shard_map/prepare/pallas_call | solution.py:265
  21.7 2.2 %near_own.1.refs_0_ = f32[33,32,128]{2,1,0:T(8,128)S(1)} custom-call(s32[4,144]{1,0:T(4,128)S(1)} %get-tuple-element.32.plan_ref, f32[32,32,256]{2,1,0:T(8,128)S(1)} %bitcast.46, bf16[128,128,256]{2,1,0:T(8,128)(2,1)S(1)} %get-tuple-element.38.blocks_ref), custom_call_target="tpu_custom_call" | custom-call | bytes 11070000 | tf_op jit(solution)/shard_map/near_own/pallas_call | solution.py:284
  23.9 0.4 collective-permute-done.4.refs_3_
  24.4 2.9 %collective-permute-done.3.refs_2_ = bf16[8,32,128]{2,1,0:T(8,128)(2,1)S(1)} collective-permute-done((bf16[8,32,128]{2,1,0:T(8,128)(2,1)S(1)}, bf16[8,32,128]{2,1,0:T(8,128)(2,1)S(1)}, u32[]{:S(2)}, u32[]{:S(2)}) %collective-permute-start.3) | collective-permute-done | bytes 65568 | tf_op jit(solution)/shard_map/ppermute | solution.py:22
  27.3 0.5 collective-permute-start.5
  27.8 2.1 %far.2 = (f32[32,32,64]{2,1,0:T(8,128)S(1)}, bf16[16,32,128]{2,1,0:T(8,128)(2,1)S(1)}) custom-call(s32[3,160]{1,0:T(4,128)S(1)} %get-tuple-element.37.far_plan_ref.plan_ref, bf16[160,64,64]{2,1,0:T(8,128)(2,1)S(1)} %get-tuple-element.41.pairs_ref, bf16[8,32,128]{2,1,0:T(8,128)(2,1)S(1)} %add_convert_fusion.1.refs_0_, ...), custom_call_target="tpu_custom_call" | custom-call | bytes 11070000 | tf_op jit(solution)/shard_map/far/pallas_call | solution.py:312
  29.9 1.2 %collective-permute-start.8 = (bf16[16,32,128]{2,1,0:T(8,128)(2,1)S(1)}, bf16[16,32,128]{2,1,0:T(8,128)(2,1)S(1)}, u32[]{:S(2)}, u32[]{:S(2)}) collective-permute-start(bf16[16,32,128]{2,1,0:T(8,128)(2,1)S(1)} %get-tuple-element.47), channel_id=1, source_target_pairs={{0,2},{2,0},{1,3},{3,1},{4,6},{6,4},{5,7},{7,5},{8,10},{10,8},{9,1... | collective-permute-start | bytes 393224 | tf_op jit(solution)/shard_map/ppermute | solution.py:22
  31.1 1.4 %collective-permute-done.7.other_ref = bf16[32,32,128]{2,1,0:T(8,128)(2,1)S(1)} collective-permute-done((bf16[32,32,128]{2,1,0:T(8,128)(2,1)S(1)}, bf16[32,32,128]{2,1,0:T(8,128)(2,1)S(1)}, u32[]{:S(2)}, u32[]{:S(2)}) %collective-permute-start.7) | collective-permute-done | bytes 262176 | tf_op jit(solution)/shard_map/ppermute | solution.py:22
  32.4 2.1 %near_halves.3.acc_in = f32[33,32,128]{2,1,0:T(8,128)S(1)} custom-call(s32[2]{0:T(128)S(1)} %pad_add_fusion.place_ref, s32[4,144]{1,0:T(4,128)S(1)} %get-tuple-element.32.plan_ref, bf16[32,32,128]{2,1,0:T(8,128)(2,1)S(1)} %collective-permute-done.6.same_ref, bf16[32,32,128]{2,1,0:T(8,128)(2,1)S(1)} %collective-permute-done.7.other_ref, ...), custom_call_target="tpu_custom_call" | custom-call | bytes 7380000 | tf_op jit(solution)/shard_map/near_halves/pallas_call | solution.py:300
  34.6 4.2 %collective-permute-done.8.far_other_ref = bf16[16,32,128]{2,1,0:T(8,128)(2,1)S(1)} collective-permute-done((bf16[16,32,128]{2,1,0:T(8,128)(2,1)S(1)}, bf16[16,32,128]{2,1,0:T(8,128)(2,1)S(1)}, u32[]{:S(2)}, u32[]{:S(2)}) %collective-permute-start.8) | collective-permute-done | bytes 131104 | tf_op jit(solution)/shard_map/ppermute | solution.py:22
  38.7 3.5 %finish.2 = (f32[32,32,128]{2,1,0:T(8,128)}, bf16[32,32,128]{2,1,0:T(8,128)(2,1)S(1)}, f32[8,32,128]{2,1,0:T(8,128)S(1)}, bf16[40,32,128]{2,1,0:T(8,128)(2,1)S(1)}) custom-call(s32[2]{0:T(128)S(1)} %pad_add_fusion.place_ref, s32[4,144]{1,0:T(4,128)S(1)} %get-tuple-element.32.plan_ref, bf16[32,32,128]{2,1,0:T(8,128)(2,1)S(1)} %collective-permute-done.same_ref, ...), custom_call_target="tpu_custom_call" | custom-call | bytes 14760000 | tf_op jit(solution)/shard_map/finish/pallas_call | solution.py:331
  42.8 3.2 %collective-permute-start.9 = (bf16[32,32,128]{2,1,0:T(8,128)(2,1)S(1)}, bf16[32,32,128]{2,1,0:T(8,128)(2,1)S(1)}, u32[]{:S(2)}, u32[]{:S(2)}) collective-permute-start(bf16[32,32,128]{2,1,0:T(8,128)(2,1)S(1)} %get-tuple-element.50.same_ref), channel_id=1, source_target_pairs={{0,12},{4,8},{8,4},{12,0},{1,13},{5,9},{9,5},{13,1},{2,14},{6,10},... | collective-permute-start | bytes 786440 | tf_op jit(solution)/shard_map/ppermute | solution.py:22
  46.0 3.8 %collective-permute-done.10.other_ref = bf16[40,32,128]{2,1,0:T(8,128)(2,1)S(1)} collective-permute-done((bf16[40,32,128]{2,1,0:T(8,128)(2,1)S(1)}, bf16[40,32,128]{2,1,0:T(8,128)(2,1)S(1)}, u32[]{:S(2)}, u32[]{:S(2)}) %collective-permute-start.10) | collective-permute-done | bytes 327712 | tf_op jit(solution)/shard_map/ppermute | solution.py:22
  49.9 2.4 %collective-permute-start.13 = (bf16[8,32,128]{2,1,0:T(8,128)(2,1)S(1)}, bf16[8,32,128]{2,1,0:T(8,128)(2,1)S(1)}, u32[]{:S(2)}, u32[]{:S(2)}) collective-permute-start(bf16[8,32,128]{2,1,0:T(8,128)(2,1)S(1)} %add_convert_fusion.refs_0_), channel_id=1, source_target_pairs={{0,12},{4,8},{8,4},{12,0},{1,13},{5,9},{9,5},{13,1},{2,14},{6,10},... | collective-permute-start | bytes 196616 | tf_op jit(solution)/shard_map/ppermute | solution.py:22
  52.3 2.0 %collective-permute-start.11 = (bf16[8,32,128]{2,1,0:T(8,128)(2,1)S(1)}, bf16[8,32,128]{2,1,0:T(8,128)(2,1)S(1)}, u32[]{:S(2)}, u32[]{:S(2)}) collective-permute-start(bf16[8,32,128]{2,1,0:T(8,128)(2,1)S(1)} %add_convert_fusion.refs_0_), channel_id=1, source_target_pairs={{0,4},{4,0},{8,12},{12,8},{1,5},{5,1},{9,13},{13,9},{2,6},{6,2},{1... | collective-permute-start | bytes 196616 | tf_op jit(solution)/shard_map/ppermute | solution.py:22
  54.3 2.1 %near_halves.4.refs_0_ = f32[33,32,128]{2,1,0:T(8,128)S(1)} custom-call(s32[2]{0:T(128)S(1)} %pad_add_fusion.place_ref, s32[4,144]{1,0:T(4,128)S(1)} %get-tuple-element.32.plan_ref, bf16[32,32,128]{2,1,0:T(8,128)(2,1)S(1)} %get-tuple-element.50.same_ref, bf16[40,32,128]{2,1,0:T(8,128)(2,1)S(1)} %collective-permute-done.10.other_ref, ...), custom_call_target="tpu_custom_call" | custom-call | bytes 7380000 | tf_op jit(solution)/shard_map/near_halves/pallas_call | solution.py:300
  56.4 0.7 collective-permute-start.16
  57.2 0.7 collective-permute-done.13.refs_3_
  57.9 3.3 %collective-permute-done.12.refs_2_ = bf16[8,32,128]{2,1,0:T(8,128)(2,1)S(1)} collective-permute-done((bf16[8,32,128]{2,1,0:T(8,128)(2,1)S(1)}, bf16[8,32,128]{2,1,0:T(8,128)(2,1)S(1)}, u32[]{:S(2)}, u32[]{:S(2)}) %collective-permute-start.12) | collective-permute-done | bytes 65568 | tf_op jit(solution)/shard_map/ppermute | solution.py:22
  61.2 1.4 %collective-permute-start.14 = (bf16[32,32,128]{2,1,0:T(8,128)(2,1)S(1)}, bf16[32,32,128]{2,1,0:T(8,128)(2,1)S(1)}, u32[]{:S(2)}, u32[]{:S(2)}) collective-permute-start(bf16[32,32,128]{2,1,0:T(8,128)(2,1)S(1)} %collective-permute-done.9.same_ref), channel_id=1, source_target_pairs={{0,2},{2,0},{1,3},{3,1},{4,6},{6,4},{5,7},{7,5},{8,10},{10,8},{9,1... | collective-permute-start | bytes 786440 | tf_op jit(solution)/shard_map/ppermute | solution.py:22
  62.6 2.1 %far.3 = (f32[32,32,64]{2,1,0:T(8,128)S(1)}, bf16[16,32,128]{2,1,0:T(8,128)(2,1)S(1)}) custom-call(s32[3,160]{1,0:T(4,128)S(1)} %get-tuple-element.37.far_plan_ref.plan_ref, bf16[160,64,64]{2,1,0:T(8,128)(2,1)S(1)} %get-tuple-element.41.pairs_ref, bf16[8,32,128]{2,1,0:T(8,128)(2,1)S(1)} %add_convert_fusion.refs_0_, ...), custom_call_target="tpu_custom_call" | custom-call | bytes 11070000 | tf_op jit(solution)/shard_map/far/pallas_call | solution.py:312
  65.0 2.1 %near_halves.5.acc_in = f32[33,32,128]{2,1,0:T(8,128)S(1)} custom-call(s32[2]{0:T(128)S(1)} %pad_add_fusion.place_ref, s32[4,144]{1,0:T(4,128)S(1)} %get-tuple-element.32.plan_ref, bf16[32,32,128]{2,1,0:T(8,128)(2,1)S(1)} %collective-permute-done.15.same_ref, bf16[32,32,128]{2,1,0:T(8,128)(2,1)S(1)} %collective-permute-done.16.other_ref, ...), custom_call_target="tpu_custom_call" | custom-call | bytes 7380000 | tf_op jit(solution)/shard_map/near_halves/pallas_call | solution.py:300
  67.1 4.2 %collective-permute-done.17.far_other_ref = bf16[16,32,128]{2,1,0:T(8,128)(2,1)S(1)} collective-permute-done((bf16[16,32,128]{2,1,0:T(8,128)(2,1)S(1)}, bf16[16,32,128]{2,1,0:T(8,128)(2,1)S(1)}, u32[]{:S(2)}, u32[]{:S(2)}) %collective-permute-start.17) | collective-permute-done | bytes 131104 | tf_op jit(solution)/shard_map/ppermute | solution.py:22
  71.3 3.2 %finish.3 = f32[32,32,128]{2,1,0:T(8,128)} custom-call(s32[2]{0:T(128)S(1)} %pad_add_fusion.place_ref, s32[4,144]{1,0:T(4,128)S(1)} %get-tuple-element.32.plan_ref, bf16[32,32,128]{2,1,0:T(8,128)(2,1)S(1)} %collective-permute-done.9.same_ref, bf16[32,32,128]{2,1,0:T(8,128)(2,1)S(1)} %collective-permute-done.14.other_ref, ...), custom_call_target="tpu_custom_call" | custom-call | bytes 14760000 | tf_op jit(solution)/shard_map/finish/pallas_call | solution.py:331
  (21 shorter events, 1.1 us)
Async XLA Ops:
  0.6 21.0 %copy-start = (f32[32,256,32]{1,2,0:T(8,128)S(1)}, f32[32,256,32]{1,2,0:T(8,128)}, u32[]{:S(2)}) copy-start(f32[32,256,32]{1,2,0:T(8,128)} %param.6) | copy-start | bytes 3145732
  3.1 7.1 %collective-permute-start.1 = (bf16[8,32,128]{2,1,0:T(8,128)(2,1)S(1)}, bf16[8,32,128]{2,1,0:T(8,128)(2,1)S(1)}, u32[]{:S(2)}, u32[]{:S(2)}) collective-permute-start(bf16[8,32,128]{2,1,0:T(8,128)(2,1)S(1)} %get-tuple-element.35), channel_id=1, source_target_pairs={{0,2},{2,0},{1,3},{3,1},{4,6},{6,4},{5,7},{7,5},{8,10},{10,8},{9,1... | collective-permute-start | bytes 196616 | tf_op jit(solution)/shard_map/ppermute | solution.py:22
  6.1 17.7 %collective-permute-start.6 = (bf16[32,32,128]{2,1,0:T(8,128)(2,1)S(1)}, bf16[32,32,128]{2,1,0:T(8,128)(2,1)S(1)}, u32[]{:S(2)}, u32[]{:S(2)}) collective-permute-start(bf16[32,32,128]{2,1,0:T(8,128)(2,1)S(1)} %get-tuple-element.33), channel_id=1, source_target_pairs={{0,4},{4,0},{8,12},{12,8},{1,5},{5,1},{9,13},{13,9},{2,6},{6,2},{1... | collective-permute-start | bytes 786440 | tf_op jit(solution)/shard_map/ppermute | solution.py:22
  7.7 19.6 %collective-permute-start = (bf16[32,32,128]{2,1,0:T(8,128)(2,1)S(1)}, bf16[32,32,128]{2,1,0:T(8,128)(2,1)S(1)}, u32[]{:S(2)}, u32[]{:S(2)}) collective-permute-start(bf16[32,32,128]{2,1,0:T(8,128)(2,1)S(1)} %get-tuple-element.33), channel_id=1, source_target_pairs={{0,12},{4,8},{8,4},{12,0},{1,13},{5,9},{9,5},{13,1},{2,14},{6,10},... | collective-permute-start | bytes 786440 | tf_op jit(solution)/shard_map/ppermute | solution.py:22
  10.2 14.2 %collective-permute-start.4 = (bf16[8,32,128]{2,1,0:T(8,128)(2,1)S(1)}, bf16[8,32,128]{2,1,0:T(8,128)(2,1)S(1)}, u32[]{:S(2)}, u32[]{:S(2)}) collective-permute-start(bf16[8,32,128]{2,1,0:T(8,128)(2,1)S(1)} %add_convert_fusion.1.refs_0_), channel_id=1, source_target_pairs={{0,12},{4,8},{8,4},{12,0},{1,13},{5,9},{9,5},{13,1},{2,14},{6,10},... | collective-permute-start | bytes 196616 | tf_op jit(solution)/shard_map/ppermute | solution.py:22
  12.6 14.7 %collective-permute-start.3 = (bf16[8,32,128]{2,1,0:T(8,128)(2,1)S(1)}, bf16[8,32,128]{2,1,0:T(8,128)(2,1)S(1)}, u32[]{:S(2)}, u32[]{:S(2)}) collective-permute-start(bf16[8,32,128]{2,1,0:T(8,128)(2,1)S(1)} %add_convert_fusion.1.refs_0_), channel_id=1, source_target_pairs={{0,8},{4,12},{8,0},{12,4},{1,9},{5,13},{9,1},{13,5},{2,10},{6,14},... | collective-permute-start | bytes 196616 | tf_op jit(solution)/shard_map/ppermute | solution.py:22
  12.6 14.7 %collective-permute-start.2 = (bf16[8,32,128]{2,1,0:T(8,128)(2,1)S(1)}, bf16[8,32,128]{2,1,0:T(8,128)(2,1)S(1)}, u32[]{:S(2)}, u32[]{:S(2)}) collective-permute-start(bf16[8,32,128]{2,1,0:T(8,128)(2,1)S(1)} %add_convert_fusion.1.refs_0_), channel_id=1, source_target_pairs={{0,4},{4,0},{8,12},{12,8},{1,5},{5,1},{9,13},{13,9},{2,6},{6,2},{1... | collective-permute-start | bytes 196616 | tf_op jit(solution)/shard_map/ppermute | solution.py:22
  23.9 8.6 %collective-permute-start.7 = (bf16[32,32,128]{2,1,0:T(8,128)(2,1)S(1)}, bf16[32,32,128]{2,1,0:T(8,128)(2,1)S(1)}, u32[]{:S(2)}, u32[]{:S(2)}) collective-permute-start(bf16[32,32,128]{2,1,0:T(8,128)(2,1)S(1)} %collective-permute-done.6.same_ref), channel_id=1, source_target_pairs={{0,2},{2,0},{1,3},{3,1},{4,6},{6,4},{5,7},{7,5},{8,10},{10,8},{9,1... | collective-permute-start | bytes 786440 | tf_op jit(solution)/shard_map/ppermute | solution.py:22
  27.3 11.5 %collective-permute-start.5 = (bf16[32,32,128]{2,1,0:T(8,128)(2,1)S(1)}, bf16[32,32,128]{2,1,0:T(8,128)(2,1)S(1)}, u32[]{:S(2)}, u32[]{:S(2)}) collective-permute-start(bf16[32,32,128]{2,1,0:T(8,128)(2,1)S(1)} %collective-permute-done.same_ref), channel_id=1, source_target_pairs={{0,2},{2,0},{1,3},{3,1},{4,6},{6,4},{5,7},{7,5},{8,10},{10,8},{9,1... | collective-permute-start | bytes 786440 | tf_op jit(solution)/shard_map/ppermute | solution.py:22
  29.9 8.8 %collective-permute-start.8 = (bf16[16,32,128]{2,1,0:T(8,128)(2,1)S(1)}, bf16[16,32,128]{2,1,0:T(8,128)(2,1)S(1)}, u32[]{:S(2)}, u32[]{:S(2)}) collective-permute-start(bf16[16,32,128]{2,1,0:T(8,128)(2,1)S(1)} %get-tuple-element.47), channel_id=1, source_target_pairs={{0,2},{2,0},{1,3},{3,1},{4,6},{6,4},{5,7},{7,5},{8,10},{10,8},{9,1... | collective-permute-start | bytes 393224 | tf_op jit(solution)/shard_map/ppermute | solution.py:22
  42.3 7.6 %collective-permute-start.10 = (bf16[40,32,128]{2,1,0:T(8,128)(2,1)S(1)}, bf16[40,32,128]{2,1,0:T(8,128)(2,1)S(1)}, u32[]{:S(2)}, u32[]{:S(2)}) collective-permute-start(bf16[40,32,128]{2,1,0:T(8,128)(2,1)S(1)} %get-tuple-element.52), channel_id=1, source_target_pairs={{0,2},{2,0},{1,3},{3,1},{4,6},{6,4},{5,7},{7,5},{8,10},{10,8},{9,1... | collective-permute-start | bytes 983048 | tf_op jit(solution)/shard_map/ppermute | solution.py:22
  42.5 13.9 %collective-permute-start.15 = (bf16[32,32,128]{2,1,0:T(8,128)(2,1)S(1)}, bf16[32,32,128]{2,1,0:T(8,128)(2,1)S(1)}, u32[]{:S(2)}, u32[]{:S(2)}) collective-permute-start(bf16[32,32,128]{2,1,0:T(8,128)(2,1)S(1)} %get-tuple-element.50.same_ref), channel_id=1, source_target_pairs={{0,4},{4,0},{8,12},{12,8},{1,5},{5,1},{9,13},{13,9},{2,6},{6,2},{1... | collective-permute-start | bytes 786440 | tf_op jit(solution)/shard_map/ppermute | solution.py:22
  42.8 14.3 %collective-permute-start.9 = (bf16[32,32,128]{2,1,0:T(8,128)(2,1)S(1)}, bf16[32,32,128]{2,1,0:T(8,128)(2,1)S(1)}, u32[]{:S(2)}, u32[]{:S(2)}) collective-permute-start(bf16[32,32,128]{2,1,0:T(8,128)(2,1)S(1)} %get-tuple-element.50.same_ref), channel_id=1, source_target_pairs={{0,12},{4,8},{8,4},{12,0},{1,13},{5,9},{9,5},{13,1},{2,14},{6,10},... | collective-permute-start | bytes 786440 | tf_op jit(solution)/shard_map/ppermute | solution.py:22
  49.9 8.0 %collective-permute-start.13 = (bf16[8,32,128]{2,1,0:T(8,128)(2,1)S(1)}, bf16[8,32,128]{2,1,0:T(8,128)(2,1)S(1)}, u32[]{:S(2)}, u32[]{:S(2)}) collective-permute-start(bf16[8,32,128]{2,1,0:T(8,128)(2,1)S(1)} %add_convert_fusion.refs_0_), channel_id=1, source_target_pairs={{0,12},{4,8},{8,4},{12,0},{1,13},{5,9},{9,5},{13,1},{2,14},{6,10},... | collective-permute-start | bytes 196616 | tf_op jit(solution)/shard_map/ppermute | solution.py:22
  52.3 8.9 %collective-permute-start.12 = (bf16[8,32,128]{2,1,0:T(8,128)(2,1)S(1)}, bf16[8,32,128]{2,1,0:T(8,128)(2,1)S(1)}, u32[]{:S(2)}, u32[]{:S(2)}) collective-permute-start(bf16[8,32,128]{2,1,0:T(8,128)(2,1)S(1)} %add_convert_fusion.refs_0_), channel_id=1, source_target_pairs={{0,8},{4,12},{8,0},{12,4},{1,9},{5,13},{9,1},{13,5},{2,10},{6,14},... | collective-permute-start | bytes 196616 | tf_op jit(solution)/shard_map/ppermute | solution.py:22
  52.3 8.9 %collective-permute-start.11 = (bf16[8,32,128]{2,1,0:T(8,128)(2,1)S(1)}, bf16[8,32,128]{2,1,0:T(8,128)(2,1)S(1)}, u32[]{:S(2)}, u32[]{:S(2)}) collective-permute-start(bf16[8,32,128]{2,1,0:T(8,128)(2,1)S(1)} %add_convert_fusion.refs_0_), channel_id=1, source_target_pairs={{0,4},{4,0},{8,12},{12,8},{1,5},{5,1},{9,13},{13,9},{2,6},{6,2},{1... | collective-permute-start | bytes 196616 | tf_op jit(solution)/shard_map/ppermute | solution.py:22
  56.4 8.6 %collective-permute-start.16 = (bf16[32,32,128]{2,1,0:T(8,128)(2,1)S(1)}, bf16[32,32,128]{2,1,0:T(8,128)(2,1)S(1)}, u32[]{:S(2)}, u32[]{:S(2)}) collective-permute-start(bf16[32,32,128]{2,1,0:T(8,128)(2,1)S(1)} %collective-permute-done.15.same_ref), channel_id=1, source_target_pairs={{0,2},{2,0},{1,3},{3,1},{4,6},{6,4},{5,7},{7,5},{8,10},{10,8},{9,1... | collective-permute-start | bytes 786440 | tf_op jit(solution)/shard_map/ppermute | solution.py:22
  61.2 10.1 %collective-permute-start.14 = (bf16[32,32,128]{2,1,0:T(8,128)(2,1)S(1)}, bf16[32,32,128]{2,1,0:T(8,128)(2,1)S(1)}, u32[]{:S(2)}, u32[]{:S(2)}) collective-permute-start(bf16[32,32,128]{2,1,0:T(8,128)(2,1)S(1)} %collective-permute-done.9.same_ref), channel_id=1, source_target_pairs={{0,2},{2,0},{1,3},{3,1},{4,6},{6,4},{5,7},{7,5},{8,10},{10,8},{9,1... | collective-permute-start | bytes 786440 | tf_op jit(solution)/shard_map/ppermute | solution.py:22
  64.7 6.6 %collective-permute-start.17 = (bf16[16,32,128]{2,1,0:T(8,128)(2,1)S(1)}, bf16[16,32,128]{2,1,0:T(8,128)(2,1)S(1)}, u32[]{:S(2)}, u32[]{:S(2)}) collective-permute-start(bf16[16,32,128]{2,1,0:T(8,128)(2,1)S(1)} %get-tuple-element.61), channel_id=1, source_target_pairs={{0,2},{2,0},{1,3},{3,1},{4,6},{6,4},{5,7},{7,5},{8,10},{10,8},{9,1... | collective-permute-start | bytes 393224 | tf_op jit(solution)/shard_map/ppermute | solution.py:22

commit v3 on v2

--- a/solution.py
+++ b/solution.py
@@ -30,6 +30,10 @@
     return pltpu.CompilerParams(vmem_limit_bytes=mebibytes << 20)
 
 
+def in_smem(array):
+    return pltpu.with_memory_space_constraint(array, pltpu.SMEM)
+
+
 def in_hbm(array):
     return pltpu.with_memory_space_constraint(array, pltpu.HBM)
 
@@ -38,20 +42,20 @@
     return pl.CostEstimate(flops=0, transcendentals=0, bytes_accessed=int(microseconds * 3.69e6))
 
 
-def put_projection(place_ref, low_ref, basis_ref, keep_ref, send_ref, at, parts):
+def put_projection(low_ref, basis_ref, keep_ref, send_ref, at, parts):
     quarter = keep_ref.shape[0]
     for part in range(2):
         for n in range(quarter):
             m = 2 * part * quarter + n
             pair = [dot(low_ref[i], basis_ref[i], TRANSPOSED_RHS) for i in (m, m + quarter)]
             parts[part, n] = jnp.concatenate(pair, 1)
-    keep_ref[...] = parts[place_ref[1]]
-    send_ref[at:] = parts[1 - place_ref[1]].astype(jnp.bfloat16)
-
-
-def start_kernel(place_ref, panel_hbm, basis_hbm, mine_ref, basis_ref, keep_ref, send_ref, panel, parts, arrived):
+    keep_ref[...] = parts[lax.axis_index("basis")]
+    send_ref[at:] = parts[1 - lax.axis_index("basis")].astype(jnp.bfloat16)
+
+
+def start_kernel(panel_hbm, basis_hbm, mine_ref, basis_ref, keep_ref, send_ref, panel, parts, arrived):
     slab = basis_ref.shape[2]
-    offset = pl.multiple_of(place_ref[1] * slab, slab)
+    offset = pl.multiple_of(lax.axis_index("basis") * slab, slab)
     pieces = arrived.shape[0] // 2
     size = panel.shape[0] // pieces
     for i in range(pieces):
@@ -65,7 +69,7 @@
     for i in range(pieces):
         rows = pl.ds(i * size, size)
         pltpu.make_async_copy(basis_hbm.at[rows], basis_ref.at[rows], arrived.at[pieces + i]).wait()
-    put_projection(place_ref, mine_ref, basis_ref, keep_ref, send_ref, 0, parts)
+    put_projection(mine_ref, basis_ref, keep_ref, send_ref, 0, parts)
 
 
 def put_sorted(words_ref, kinds, nothing, plan_ref):
@@ -89,9 +93,15 @@
     plan_ref[kinds : kinds + 1] = totals
 
 
-def plan_kernel(nothing, near_ref, far_ref, near_plan_ref, far_plan_ref):
-    put_sorted(near_ref, 3, nothing, near_plan_ref)
-    put_sorted(far_ref, 2, nothing, far_plan_ref)
+def plan_kernel(nothing, near_ref, far_ref, near_plan_ref, far_plan_ref, near_plan, far_plan, sent):
+    put_sorted(near_ref, 3, nothing, near_plan)
+    put_sorted(far_ref, 2, nothing, far_plan)
+    near_copy = pltpu.make_async_copy(near_plan, near_plan_ref, sent.at[0])
+    far_copy = pltpu.make_async_copy(far_plan, far_plan_ref, sent.at[1])
+    near_copy.start()
+    far_copy.start()
+    near_copy.wait()
+    far_copy.wait()
 
 
 def prepare_kernel(far_plan_ref, blocks_hbm, coupling_hbm, blocks_ref, pairs_ref, coupling, turned, arrived):
@@ -150,17 +160,17 @@
     add_near(plan_ref, 0, low, blocks_ref, acc_ref)
 
 
-def put_whole(place_ref, same_ref, other_ref, whole):
+def put_whole(same_ref, other_ref, whole):
     slab = same_ref.shape[2]
-    first = place_ref[1] == 0
+    first = lax.axis_index("basis") == 0
     same, other = same_ref[...], other_ref[: same_ref.shape[0]]
     whole[:, :, :slab] = jnp.where(first, same, other)
     whole[:, :, slab:] = jnp.where(first, other, same)
 
 
-def near_halves_kernel(kind, place_ref, plan_ref, same_ref, other_ref, blocks_ref, *refs):
+def near_halves_kernel(kind, plan_ref, same_ref, other_ref, blocks_ref, *refs):
     acc_ref, whole = refs[-2:]
-    put_whole(place_ref, same_ref, other_ref, whole)
+    put_whole(same_ref, other_ref, whole)
     acc_ref[...] = refs[0][...] if len(refs) == 3 else jnp.zeros_like(acc_ref)
     add_near(plan_ref, kind, whole, blocks_ref, acc_ref)
 
@@ -194,9 +204,9 @@
         send_ref[n] = jnp.concatenate([acc[n], acc[n + half]], 1).astype(jnp.bfloat16)
 
 
-def finish_kernel(place_ref, plan_ref, same_ref, other_ref, blocks_ref, acc_in, far_ref, far_other_ref, basis_ref, *refs):
+def finish_kernel(plan_ref, same_ref, other_ref, blocks_ref, acc_in, far_ref, far_other_ref, basis_ref, *refs):
     out_ref, (acc_ref, whole) = refs[0], refs[-2:]
-    near_halves_kernel(2, place_ref, plan_ref, same_ref, other_ref, blocks_ref, acc_in, acc_ref, whole)
+    near_halves_kernel(2, plan_ref, same_ref, other_ref, blocks_ref, acc_in, acc_ref, whole)
     half, _, wide = far_other_ref.shape
     rank = wide // 2
     for n in range(half):
@@ -208,7 +218,7 @@
         low = out_ref[...].astype(jnp.bfloat16)
         mine_ref[...] = low
         send_ref[: 2 * half] = low
-        put_projection(place_ref, mine_ref, basis_ref, keep_ref, send_ref, 2 * half, parts)
+        put_projection(mine_ref, basis_ref, keep_ref, send_ref, 2 * half, parts)
 
 
 def tiled_on_device(right_panel, near_field_blocks, near_list, cluster_basis, coupling, far_list):
@@ -221,7 +231,7 @@
     place = jnp.stack([lax.axis_index("blk"), lax.axis_index("basis")]).astype(jnp.int32)
     half, quarter = clusters // 2, clusters // 4
     near_owner, far_owner = near_list[:, 1] // clusters, far_list[:, 1] // clusters
-    words = jnp.where(near_owner == place[0], 0, jnp.where(near_owner == place[0] ^ 1, 1, 2))
+    words = jnp.where(near_owner == place[0], 0, jnp.where(near_owner == place[0] ^ 1, 2, 1))
     words = words << FIELD | jnp.arange(near_count, dtype=jnp.int32)
     words = words << FIELD | near_list[:, 0] - place[0] * clusters
     words = words << FIELD | near_list[:, 1] % clusters
@@ -246,18 +256,26 @@
     mine, basis, keep, send = pl.pallas_call(
         start_kernel,
         out_shape=(mine_shape, jax.ShapeDtypeStruct(basis.shape, bf16), keep_shape, send_shape),
-        in_specs=[SMEM, HBM, HBM],
+        in_specs=[HBM, HBM],
         out_specs=(VMEM,) * 4,
         scratch_shapes=[pltpu.VMEM(mine_shape.shape, f32), parts, pltpu.SemaphoreType.DMA((2 * pieces,))],
         compiler_params=params(),
         cost_estimate=cost(2),
         name="start",
-    )(place, in_hbm(panel), in_hbm(basis))
+    )(in_hbm(panel), in_hbm(basis))
     near_plan, far_plan = pl.pallas_call(
         functools.partial(plan_kernel, clusters << FIELD),
-        out_shape=(near_plan_shape, far_plan_shape),
+        out_shape=(
+            pltpu.SMEM(near_plan_shape.shape, jnp.int32),
+            pltpu.SMEM(far_plan_shape.shape, jnp.int32),
+        ),
         in_specs=[VMEM, VMEM],
-        out_specs=(VMEM, VMEM),
+        out_specs=(SMEM, SMEM),
+        scratch_shapes=[
+            pltpu.VMEM(near_plan_shape.shape, jnp.int32),
+            pltpu.VMEM(far_plan_shape.shape, jnp.int32),
+            pltpu.SemaphoreType.DMA((2,)),
+        ],
         compiler_params=params(),
         cost_estimate=cost(1),
         name="plan",
@@ -278,7 +296,7 @@
         compiler_params=params(20),
         cost_estimate=cost(4),
         name="prepare",
-    )(far_plan, in_hbm(near_field_blocks), in_hbm(coupling.transpose(1, 2, 0)))
+    )(in_smem(far_plan), in_hbm(near_field_blocks), in_hbm(coupling.transpose(1, 2, 0)))
 
     def near_own(plan, blocks):
         return pl.pallas_call(
@@ -294,19 +312,19 @@
             compiler_params=params(),
             cost_estimate=cost(3),
             name="near_own",
-        )(plan, panel, blocks)
+        )(in_smem(plan), panel, blocks)
 
     def near_halves(plan, blocks, kind, same, other, *acc):
         return pl.pallas_call(
             functools.partial(near_halves_kernel, kind),
             out_shape=acc_shape,
-            in_specs=[SMEM, SMEM] + [VMEM] * (3 + len(acc)),
+            in_specs=[SMEM] + [VMEM] * (3 + len(acc)),
             out_specs=VMEM,
             scratch_shapes=[pltpu.VMEM(low_shape.shape, bf16)],
             compiler_params=params(),
             cost_estimate=cost(2),
             name="near_halves",
-        )(place, plan, same, other, blocks, *acc)
+        )(in_smem(plan), same, other, blocks, *acc)
 
     def far(plan, held):
         return pl.pallas_call(
@@ -324,28 +342,28 @@
             compiler_params=params(),
             cost_estimate=cost(3),
             name="far",
-        )(plan, pairs, *held)
+        )(in_smem(plan), pairs, *held)
 
     def finish(plan, blocks, same, other, acc, far_sum, far_other, last):
         outs = (out_shape,) if last else (out_shape, mine_shape, keep_shape, both_shape)
         return pl.pallas_call(
             finish_kernel,
             out_shape=outs,
-            in_specs=[SMEM, SMEM] + [VMEM] * 7,
+            in_specs=[SMEM] + [VMEM] * 7,
             out_specs=(VMEM,) * len(outs),
             scratch_shapes=([] if last else [parts])
             + [pltpu.VMEM(acc_shape.shape, f32), pltpu.VMEM(low_shape.shape, bf16)],
             compiler_params=params(),
             cost_estimate=cost(4),
             name="finish",
-        )(place, plan, same, other, blocks, acc, far_sum, far_other, basis)
+        )(in_smem(plan), same, other, blocks, acc, far_sum, far_other, basis)
 
     def other_basis(array):
         return swapped(array, "basis", lambda i: 1 - i)
 
     def apply_operator(mine, keep, send, near_plan, last):
-        between = swapped(mine, "blk", lambda i: (((i + 1) % cycle ^ 1) - 1) % cycle)
-        paired = swapped(mine, "blk", lambda i: i ^ 1)
+        paired = swapped(mine, "blk", lambda i: (((i + 1) % cycle ^ 1) - 1) % cycle)
+        between = swapped(mine, "blk", lambda i: i ^ 1)
         received = other_basis(send)
         if last:
             acc = near_halves(near_plan, blocks, 0, mine, received)
@@ -353,8 +371,7 @@
             acc = near_own(near_plan, blocks)
         held = [(keep + received[-quarter:].astype(f32)).astype(bf16)]
         held += [swapped(held[0], "blk", lambda i, d=d: i ^ d) for d in range(1, cycle)]
-        paired, acc = lax.optimization_barrier((paired, acc))
-        between, *held = lax.optimization_barrier((between, *held))
+        between, acc, *held = lax.optimization_barrier((between, acc, *held))
         paired_other = other_basis(paired)
         between_other = other_basis(between)
         far_sum, far_send = far(far_plan, held)

time: 74.4 us -> 71.2 us (0.957)
  Pallas kernels: 28.1 us -> 20.8 us
  waiting for transfers between devices: 20.9 us -> 25 us
    ppermute x18, waiting for transfers between devices: 20.9 us -> 25 us  [swapped(): lax.ppermute(array, axis, [(i, partner(i)) for i in range(lax.axis_size(a...]
    pallas_call x3, Pallas kernels: 6.34 us -> 3.62 us  [near_halves(): pl.pallas_call(functools.partial(near_halves_kernel, kind), out_shape=acc...]
    pallas_call x2, Pallas kernels: 4.19 us -> 2.18 us  [far(): pl.pallas_call(far_kernel, out_shape=(jax.ShapeDtypeStruct((clusters, col...]
    pallas_call x1, Pallas kernels: 5.8 us -> 4.11 us  [tiled_on_device(): pl.pallas_call(prepare_kernel, out_shape=(pltpu.VMEM(near_field_blocks.sh...]
    ppermute x18, starting transfers between devices: 23.9 us -> 24.6 us  [swapped(): lax.ppermute(array, axis, [(i, partner(i)) for i in range(lax.axis_size(a...]
  transfers between devices with their start and end apart: 18 -> 18, of which waited for: 8 -> 7; matrix products, arithmetic and copies ran while one was open for 1% -> 1% of each run, Pallas kernels for 25% -> 17%
where the time goes in v3:
time: 71.2 us; the launch traced here: 72 us
  waiting for transfers between devices  25 us (35%)
  starting transfers between devices  24.6 us (35%)
  Pallas kernels  20.8 us (29%)
  other arithmetic  0.82 us (1%)
  between operations  0.76 us (1%)
    ppermute x18, waiting for transfers between devices, swapped(): lax.ppermute(array, axis, [(i, partner(i)) for i in range(lax.axis_size(a...  25 us
    ppermute x18, starting transfers between devices, swapped(): lax.ppermute(array, axis, [(i, partner(i)) for i in range(lax.axis_size(a...  24.6 us
    pallas_call x2, Pallas kernels, finish(): pl.pallas_call(finish_kernel, out_shape=outs, in_specs=[SMEM] + [VMEM] *...  6.36 us
    pallas_call x1, Pallas kernels, tiled_on_device(): pl.pallas_call(prepare_kernel, out_shape=(pltpu.VMEM(near_field_blocks.sh...  4.11 us
    pallas_call x3, Pallas kernels, near_halves(): pl.pallas_call(functools.partial(near_halves_kernel, kind), out_shape=acc...  3.62 us
    pallas_call x2, Pallas kernels, far(): pl.pallas_call(far_kernel, out_shape=(jax.ShapeDtypeStruct((clusters, col...  2.18 us
    pallas_call x1, Pallas kernels, tiled_on_device(): pl.pallas_call(start_kernel, out_shape=(mine_shape, jax.ShapeDtypeStruct(...  1.9 us
    pallas_call x1, Pallas kernels, near_own(): pl.pallas_call(near_own_kernel, out_shape=acc_shape, in_specs=[SMEM, HBM,...  1.56 us
  transfers between devices with their start and end apart: 18, of which 7 were waited for; matrix products, arithmetic and copies ran while one was open for 1% of the time, Pallas kernels for 17%

profile of v3, /device:TPU:0, one launch (start us, length us, event | category | flops | bytes accessed | tf_op | source)
XLA Modules:
  0.0 72.0 jit_solution(11624441588270728046)
XLA Ops:
  0.6 1.9 %start.1 = (bf16[32,32,128]{2,1,0:T(8,128)(2,1)S(1)}, bf16[32,64,128]{2,1,0:T(8,128)(2,1)S(1)}, f32[8,32,128]{2,1,0:T(8,128)S(1)}, bf16[8,32,128]{2,1,0:T(8,128)(2,1)S(1)}) custom-call(f32[32,32,256]{2,1,0:T(8,128)} %bitcast.43, bf16[32,64,128]{2,1,0:T(8,128)(2,1)} %bitcast.46), custom_call_target="tpu_custom_call" | custom-call | bytes 7380000 | tf_op jit(solution)/shard_map/start/pallas_call | solution.py:256
  2.6 3.0 %collective-permute-start.1 = (bf16[8,32,128]{2,1,0:T(8,128)(2,1)S(1)}, bf16[8,32,128]{2,1,0:T(8,128)(2,1)S(1)}, u32[]{:S(2)}, u32[]{:S(2)}) collective-permute-start(bf16[8,32,128]{2,1,0:T(8,128)(2,1)S(1)} %get-tuple-element.35), channel_id=1, source_target_pairs={{0,2},{2,0},{1,3},{3,1},{4,6},{6,4},{5,7},{7,5},{8,10},{10,8},{9,1... | collective-permute-start | bytes 196616 | tf_op jit(solution)/shard_map/ppermute | solution.py:22
  5.6 3.6 %collective-permute-start.6 = (bf16[32,32,128]{2,1,0:T(8,128)(2,1)S(1)}, bf16[32,32,128]{2,1,0:T(8,128)(2,1)S(1)}, u32[]{:S(2)}, u32[]{:S(2)}) collective-permute-start(bf16[32,32,128]{2,1,0:T(8,128)(2,1)S(1)} %get-tuple-element.31), channel_id=1, source_target_pairs={{0,12},{4,8},{8,4},{12,0},{1,13},{5,9},{9,5},{13,1},{2,14},{6,10},... | collective-permute-start | bytes 786440 | tf_op jit(solution)/shard_map/ppermute | solution.py:22
  9.2 2.8 %collective-permute-start.4 = (bf16[8,32,128]{2,1,0:T(8,128)(2,1)S(1)}, bf16[8,32,128]{2,1,0:T(8,128)(2,1)S(1)}, u32[]{:S(2)}, u32[]{:S(2)}) collective-permute-start(bf16[8,32,128]{2,1,0:T(8,128)(2,1)S(1)} %add_convert_fusion.1.refs_0_), channel_id=1, source_target_pairs={{0,12},{4,8},{8,4},{12,0},{1,13},{5,9},{9,5},{13,1},{2,14},{6,10},... | collective-permute-start | bytes 196616 | tf_op jit(solution)/shard_map/ppermute | solution.py:22
  12.0 0.7 collective-permute-start.3
  12.7 0.9 %collective-permute-start.2 = (bf16[8,32,128]{2,1,0:T(8,128)(2,1)S(1)}, bf16[8,32,128]{2,1,0:T(8,128)(2,1)S(1)}, u32[]{:S(2)}, u32[]{:S(2)}) collective-permute-start(bf16[8,32,128]{2,1,0:T(8,128)(2,1)S(1)} %add_convert_fusion.1.refs_0_), channel_id=1, source_target_pairs={{0,4},{4,0},{8,12},{12,8},{1,5},{5,1},{9,13},{13,9},{2,6},{6,2},{1... | collective-permute-start | bytes 196616 | tf_op jit(solution)/shard_map/ppermute | solution.py:22
  13.6 0.8 %fusion = (s32[1,128]{1,0:T(1,128)S(1)}, s32[1,128]{1,0:T(1,128)S(1)}) fusion(s32[128,2]{0,1:T(2,128)} %param.8, s32[]{:T(128)S(6)} %mul.15, s32[]{:T(128)S(6)} %xor.14, s32[]{:T(128)S(6)} %axis_index.25, s32[128,2]{0,1:T(2,128)} %param.11, s32[]{:T(128)S(6)} %axis_index.28), kind=kLoop, calls=%fused_computation.20 | loop fusion | flops 10240 | bytes 3088 | tf_op jit(solution)/shard_map/or | solution.py:237
  14.4 1.1 %plan.1 = (s32[4,144]{1,0:T(4,128)S(4)}, s32[3,160]{1,0:T(4,128)S(4)}) custom-call(s32[1,128]{1,0:T(1,128)S(1)} %get-tuple-element.58.near_ref, s32[1,128]{1,0:T(1,128)S(1)} %get-tuple-element.59.far_ref), custom_call_target="tpu_custom_call" | custom-call | bytes 3690000 | tf_op jit(solution)/shard_map/plan/pallas_call | solution.py:266
  15.5 4.1 %prepare.1 = (bf16[128,128,256]{2,1,0:T(8,128)(2,1)S(1)}, bf16[160,64,64]{2,1,0:T(8,128)(2,1)S(1)}) custom-call(s32[3,160]{1,0:T(4,128)S(4)} %get-tuple-element.32.far_plan_ref.plan_ref, bf16[128,128,256]{2,1,0:T(8,128)(2,1)} %blocks_hbm.1, bf16[64,64,128]{2,1,0:T(8,128)(2,1)} %bitcast.45), custom_call_target="tpu_custom_call" | custom-call | bytes 14760000 | tf_op jit(solution)/shard_map/prepare/pallas_call | solution.py:283
  19.6 1.6 %near_own.1.refs_0_ = f32[33,32,128]{2,1,0:T(8,128)S(1)} custom-call(s32[4,144]{1,0:T(4,128)S(4)} %get-tuple-element.30.plan_ref, f32[32,32,256]{2,1,0:T(8,128)S(1)} %bitcast.44, bf16[128,128,256]{2,1,0:T(8,128)(2,1)S(1)} %get-tuple-element.33.blocks_ref), custom_call_target="tpu_custom_call" | custom-call | bytes 11070000 | tf_op jit(solution)/shard_map/near_own/pallas_call | solution.py:302
  21.2 0.7 %collective-permute-start.7 = (bf16[32,32,128]{2,1,0:T(8,128)(2,1)S(1)}, bf16[32,32,128]{2,1,0:T(8,128)(2,1)S(1)}, u32[]{:S(2)}, u32[]{:S(2)}) collective-permute-start(bf16[32,32,128]{2,1,0:T(8,128)(2,1)S(1)} %collective-permute-done.6.same_ref), channel_id=1, source_target_pairs={{0,2},{2,0},{1,3},{3,1},{4,6},{6,4},{5,7},{7,5},{8,10},{10,8},{9,1... | collective-permute-start | bytes 786440 | tf_op jit(solution)/shard_map/ppermute | solution.py:22
  21.9 1.7 %collective-permute-done.4.refs_3_ = bf16[8,32,128]{2,1,0:T(8,128)(2,1)S(1)} collective-permute-done((bf16[8,32,128]{2,1,0:T(8,128)(2,1)S(1)}, bf16[8,32,128]{2,1,0:T(8,128)(2,1)S(1)}, u32[]{:S(2)}, u32[]{:S(2)}) %collective-permute-start.4) | collective-permute-done | bytes 65568 | tf_op jit(solution)/shard_map/ppermute | solution.py:22
  23.6 1.9 %collective-permute-done.3.refs_2_ = bf16[8,32,128]{2,1,0:T(8,128)(2,1)S(1)} collective-permute-done((bf16[8,32,128]{2,1,0:T(8,128)(2,1)S(1)}, bf16[8,32,128]{2,1,0:T(8,128)(2,1)S(1)}, u32[]{:S(2)}, u32[]{:S(2)}) %collective-permute-start.3) | collective-permute-done | bytes 65568 | tf_op jit(solution)/shard_map/ppermute | solution.py:22
  26.1 1.1 %far.2 = (f32[32,32,64]{2,1,0:T(8,128)S(1)}, bf16[16,32,128]{2,1,0:T(8,128)(2,1)S(1)}) custom-call(s32[3,160]{1,0:T(4,128)S(4)} %get-tuple-element.32.far_plan_ref.plan_ref, bf16[160,64,64]{2,1,0:T(8,128)(2,1)S(1)} %get-tuple-element.38.pairs_ref, bf16[8,32,128]{2,1,0:T(8,128)(2,1)S(1)} %add_convert_fusion.1.refs_0_, ...), custom_call_target="tpu_custom_call" | custom-call | bytes 11070000 | tf_op jit(solution)/shard_map/far/pallas_call | solution.py:330
  27.2 1.6 %collective-permute-start.8 = (bf16[16,32,128]{2,1,0:T(8,128)(2,1)S(1)}, bf16[16,32,128]{2,1,0:T(8,128)(2,1)S(1)}, u32[]{:S(2)}, u32[]{:S(2)}) collective-permute-start(bf16[16,32,128]{2,1,0:T(8,128)(2,1)S(1)} %get-tuple-element.44), channel_id=1, source_target_pairs={{0,2},{2,0},{1,3},{3,1},{4,6},{6,4},{5,7},{7,5},{8,10},{10,8},{9,1... | collective-permute-start | bytes 393224 | tf_op jit(solution)/shard_map/ppermute | solution.py:22
  28.8 1.1 %near_halves.3.acc_in = f32[33,32,128]{2,1,0:T(8,128)S(1)} custom-call(s32[4,144]{1,0:T(4,128)S(4)} %get-tuple-element.30.plan_ref, bf16[32,32,128]{2,1,0:T(8,128)(2,1)S(1)} %collective-permute-done.6.same_ref, bf16[32,32,128]{2,1,0:T(8,128)(2,1)S(1)} %collective-permute-done.7.other_ref, bf16[128,128,256]{2,1,0:T(8,128)(2,1)S(1)} %get-tuple-element.33.blocks_ref, ...), custom_call_target="tpu_custom_call" | custom-call | bytes 7380000 | tf_op jit(solution)/shard_map/near_halves/pallas_call | solution.py:318
  29.8 6.5 %collective-permute-done.8.far_other_ref = bf16[16,32,128]{2,1,0:T(8,128)(2,1)S(1)} collective-permute-done((bf16[16,32,128]{2,1,0:T(8,128)(2,1)S(1)}, bf16[16,32,128]{2,1,0:T(8,128)(2,1)S(1)}, u32[]{:S(2)}, u32[]{:S(2)}) %collective-permute-start.8) | collective-permute-done | bytes 131104 | tf_op jit(solution)/shard_map/ppermute | solution.py:22
  36.3 3.3 %finish.2 = (f32[32,32,128]{2,1,0:T(8,128)}, bf16[32,32,128]{2,1,0:T(8,128)(2,1)S(1)}, f32[8,32,128]{2,1,0:T(8,128)S(1)}, bf16[40,32,128]{2,1,0:T(8,128)(2,1)S(1)}) custom-call(s32[4,144]{1,0:T(4,128)S(4)} %get-tuple-element.30.plan_ref, bf16[32,32,128]{2,1,0:T(8,128)(2,1)S(1)} %collective-permute-done.same_ref, ...), custom_call_target="tpu_custom_call" | custom-call | bytes 14760000 | tf_op jit(solution)/shard_map/finish/pallas_call | solution.py:349
  40.1 2.7 %collective-permute-start.15 = (bf16[32,32,128]{2,1,0:T(8,128)(2,1)S(1)}, bf16[32,32,128]{2,1,0:T(8,128)(2,1)S(1)}, u32[]{:S(2)}, u32[]{:S(2)}) collective-permute-start(bf16[32,32,128]{2,1,0:T(8,128)(2,1)S(1)} %get-tuple-element.47.same_ref), channel_id=1, source_target_pairs={{0,12},{4,8},{8,4},{12,0},{1,13},{5,9},{9,5},{13,1},{2,14},{6,10},... | collective-permute-start | bytes 786440 | tf_op jit(solution)/shard_map/ppermute | solution.py:22
  43.3 4.7 %collective-permute-done.10.other_ref = bf16[40,32,128]{2,1,0:T(8,128)(2,1)S(1)} collective-permute-done((bf16[40,32,128]{2,1,0:T(8,128)(2,1)S(1)}, bf16[40,32,128]{2,1,0:T(8,128)(2,1)S(1)}, u32[]{:S(2)}, u32[]{:S(2)}) %collective-permute-start.10) | collective-permute-done | bytes 327712 | tf_op jit(solution)/shard_map/ppermute | solution.py:22
  48.0 1.5 %collective-permute-start.13 = (bf16[8,32,128]{2,1,0:T(8,128)(2,1)S(1)}, bf16[8,32,128]{2,1,0:T(8,128)(2,1)S(1)}, u32[]{:S(2)}, u32[]{:S(2)}) collective-permute-start(bf16[8,32,128]{2,1,0:T(8,128)(2,1)S(1)} %add_convert_fusion.refs_0_), channel_id=1, source_target_pairs={{0,12},{4,8},{8,4},{12,0},{1,13},{5,9},{9,5},{13,1},{2,14},{6,10},... | collective-permute-start | bytes 196616 | tf_op jit(solution)/shard_map/ppermute | solution.py:22
  49.6 1.5 %collective-permute-start.12 = (bf16[8,32,128]{2,1,0:T(8,128)(2,1)S(1)}, bf16[8,32,128]{2,1,0:T(8,128)(2,1)S(1)}, u32[]{:S(2)}, u32[]{:S(2)}) collective-permute-start(bf16[8,32,128]{2,1,0:T(8,128)(2,1)S(1)} %add_convert_fusion.refs_0_), channel_id=1, source_target_pairs={{0,8},{4,12},{8,0},{12,4},{1,9},{5,13},{9,1},{13,5},{2,10},{6,14},... | collective-permute-start | bytes 196616 | tf_op jit(solution)/shard_map/ppermute | solution.py:22
  51.0 1.5 %collective-permute-start.11 = (bf16[8,32,128]{2,1,0:T(8,128)(2,1)S(1)}, bf16[8,32,128]{2,1,0:T(8,128)(2,1)S(1)}, u32[]{:S(2)}, u32[]{:S(2)}) collective-permute-start(bf16[8,32,128]{2,1,0:T(8,128)(2,1)S(1)} %add_convert_fusion.refs_0_), channel_id=1, source_target_pairs={{0,4},{4,0},{8,12},{12,8},{1,5},{5,1},{9,13},{13,9},{2,6},{6,2},{1... | collective-permute-start | bytes 196616 | tf_op jit(solution)/shard_map/ppermute | solution.py:22
  53.0 1.5 %near_halves.4.refs_0_ = f32[33,32,128]{2,1,0:T(8,128)S(1)} custom-call(s32[4,144]{1,0:T(4,128)S(4)} %get-tuple-element.30.plan_ref, bf16[32,32,128]{2,1,0:T(8,128)(2,1)S(1)} %get-tuple-element.47.same_ref, bf16[40,32,128]{2,1,0:T(8,128)(2,1)S(1)} %collective-permute-done.10.other_ref, bf16[128,128,256]{2,1,0:T(8,128)(2,1)S(1)} %get-tuple-element.33.blocks_ref), custom_call_target="tpu_custom_call" | custom-call | bytes 7380000 | tf_op jit(solution)/shard_map/near_halves/pallas_call | solution.py:318
  54.6 2.7 %collective-permute-done.13.refs_3_ = bf16[8,32,128]{2,1,0:T(8,128)(2,1)S(1)} collective-permute-done((bf16[8,32,128]{2,1,0:T(8,128)(2,1)S(1)}, bf16[8,32,128]{2,1,0:T(8,128)(2,1)S(1)}, u32[]{:S(2)}, u32[]{:S(2)}) %collective-permute-start.13) | collective-permute-done | bytes 65568 | tf_op jit(solution)/shard_map/ppermute | solution.py:22
  57.2 1.8 %collective-permute-done.12.refs_2_ = bf16[8,32,128]{2,1,0:T(8,128)(2,1)S(1)} collective-permute-done((bf16[8,32,128]{2,1,0:T(8,128)(2,1)S(1)}, bf16[8,32,128]{2,1,0:T(8,128)(2,1)S(1)}, u32[]{:S(2)}, u32[]{:S(2)}) %collective-permute-start.12) | collective-permute-done | bytes 65568 | tf_op jit(solution)/shard_map/ppermute | solution.py:22
  59.1 1.4 %collective-permute-start.14 = (bf16[32,32,128]{2,1,0:T(8,128)(2,1)S(1)}, bf16[32,32,128]{2,1,0:T(8,128)(2,1)S(1)}, u32[]{:S(2)}, u32[]{:S(2)}) collective-permute-start(bf16[32,32,128]{2,1,0:T(8,128)(2,1)S(1)} %collective-permute-done.9.same_ref), channel_id=1, source_target_pairs={{0,2},{2,0},{1,3},{3,1},{4,6},{6,4},{5,7},{7,5},{8,10},{10,8},{9,1... | collective-permute-start | bytes 786440 | tf_op jit(solution)/shard_map/ppermute | solution.py:22
  60.5 1.1 %far.3 = (f32[32,32,64]{2,1,0:T(8,128)S(1)}, bf16[16,32,128]{2,1,0:T(8,128)(2,1)S(1)}) custom-call(s32[3,160]{1,0:T(4,128)S(4)} %get-tuple-element.32.far_plan_ref.plan_ref, bf16[160,64,64]{2,1,0:T(8,128)(2,1)S(1)} %get-tuple-element.38.pairs_ref, bf16[8,32,128]{2,1,0:T(8,128)(2,1)S(1)} %add_convert_fusion.refs_0_, ...), custom_call_target="tpu_custom_call" | custom-call | bytes 11070000 | tf_op jit(solution)/shard_map/far/pallas_call | solution.py:330
  61.6 0.7 collective-permute-start.17
  62.3 1.1 %near_halves.5.acc_in = f32[33,32,128]{2,1,0:T(8,128)S(1)} custom-call(s32[4,144]{1,0:T(4,128)S(4)} %get-tuple-element.30.plan_ref, bf16[32,32,128]{2,1,0:T(8,128)(2,1)S(1)} %collective-permute-done.15.same_ref, bf16[32,32,128]{2,1,0:T(8,128)(2,1)S(1)} %collective-permute-done.16.other_ref, bf16[128,128,256]{2,1,0:T(8,128)(2,1)S(1)} %get-tuple-element.33.blocks_ref, ...), custom_call_target="tpu_custom_call" | custom-call | bytes 7380000 | tf_op jit(solution)/shard_map/near_halves/pallas_call | solution.py:318
  63.3 5.6 %collective-permute-done.17.far_other_ref = bf16[16,32,128]{2,1,0:T(8,128)(2,1)S(1)} collective-permute-done((bf16[16,32,128]{2,1,0:T(8,128)(2,1)S(1)}, bf16[16,32,128]{2,1,0:T(8,128)(2,1)S(1)}, u32[]{:S(2)}, u32[]{:S(2)}) %collective-permute-start.17) | collective-permute-done | bytes 131104 | tf_op jit(solution)/shard_map/ppermute | solution.py:22
  68.9 3.1 %finish.3 = f32[32,32,128]{2,1,0:T(8,128)} custom-call(s32[4,144]{1,0:T(4,128)S(4)} %get-tuple-element.30.plan_ref, bf16[32,32,128]{2,1,0:T(8,128)(2,1)S(1)} %collective-permute-done.9.same_ref, bf16[32,32,128]{2,1,0:T(8,128)(2,1)S(1)} %collective-permute-done.14.other_ref, bf16[128,128,256]{2,1,0:T(8,128)(2,1)S(1)} %get-tuple-element.33.blocks_ref, ...), custom_call_target="tpu_custom_call" | custom-call | bytes 14760000 | tf_op jit(solution)/shard_map/finish/pallas_call | solution.py:349
  (20 shorter events, 2.2 us)
Async XLA Ops:
  0.6 19.0 %copy-start = (f32[32,256,32]{1,2,0:T(8,128)S(1)}, f32[32,256,32]{1,2,0:T(8,128)}, u32[]{:S(2)}) copy-start(f32[32,256,32]{1,2,0:T(8,128)} %param.6) | copy-start | bytes 3145732
  2.6 6.6 %collective-permute-start.1 = (bf16[8,32,128]{2,1,0:T(8,128)(2,1)S(1)}, bf16[8,32,128]{2,1,0:T(8,128)(2,1)S(1)}, u32[]{:S(2)}, u32[]{:S(2)}) collective-permute-start(bf16[8,32,128]{2,1,0:T(8,128)(2,1)S(1)} %get-tuple-element.35), channel_id=1, source_target_pairs={{0,2},{2,0},{1,3},{3,1},{4,6},{6,4},{5,7},{7,5},{8,10},{10,8},{9,1... | collective-permute-start | bytes 196616 | tf_op jit(solution)/shard_map/ppermute | solution.py:22
  5.6 15.6 %collective-permute-start.6 = (bf16[32,32,128]{2,1,0:T(8,128)(2,1)S(1)}, bf16[32,32,128]{2,1,0:T(8,128)(2,1)S(1)}, u32[]{:S(2)}, u32[]{:S(2)}) collective-permute-start(bf16[32,32,128]{2,1,0:T(8,128)(2,1)S(1)} %get-tuple-element.31), channel_id=1, source_target_pairs={{0,12},{4,8},{8,4},{12,0},{1,13},{5,9},{9,5},{13,1},{2,14},{6,10},... | collective-permute-start | bytes 786440 | tf_op jit(solution)/shard_map/ppermute | solution.py:22
  9.2 16.4 %collective-permute-start = (bf16[32,32,128]{2,1,0:T(8,128)(2,1)S(1)}, bf16[32,32,128]{2,1,0:T(8,128)(2,1)S(1)}, u32[]{:S(2)}, u32[]{:S(2)}) collective-permute-start(bf16[32,32,128]{2,1,0:T(8,128)(2,1)S(1)} %get-tuple-element.31), channel_id=1, source_target_pairs={{0,4},{4,0},{8,12},{12,8},{1,5},{5,1},{9,13},{13,9},{2,6},{6,2},{1... | collective-permute-start | bytes 786440 | tf_op jit(solution)/shard_map/ppermute | solution.py:22
  9.2 14.5 %collective-permute-start.4 = (bf16[8,32,128]{2,1,0:T(8,128)(2,1)S(1)}, bf16[8,32,128]{2,1,0:T(8,128)(2,1)S(1)}, u32[]{:S(2)}, u32[]{:S(2)}) collective-permute-start(bf16[8,32,128]{2,1,0:T(8,128)(2,1)S(1)} %add_convert_fusion.1.refs_0_), channel_id=1, source_target_pairs={{0,12},{4,8},{8,4},{12,0},{1,13},{5,9},{9,5},{13,1},{2,14},{6,10},... | collective-permute-start | bytes 196616 | tf_op jit(solution)/shard_map/ppermute | solution.py:22
  12.0 13.6 %collective-permute-start.3 = (bf16[8,32,128]{2,1,0:T(8,128)(2,1)S(1)}, bf16[8,32,128]{2,1,0:T(8,128)(2,1)S(1)}, u32[]{:S(2)}, u32[]{:S(2)}) collective-permute-start(bf16[8,32,128]{2,1,0:T(8,128)(2,1)S(1)} %add_convert_fusion.1.refs_0_), channel_id=1, source_target_pairs={{0,8},{4,12},{8,0},{12,4},{1,9},{5,13},{9,1},{13,5},{2,10},{6,14},... | collective-permute-start | bytes 196616 | tf_op jit(solution)/shard_map/ppermute | solution.py:22
  12.7 12.8 %collective-permute-start.2 = (bf16[8,32,128]{2,1,0:T(8,128)(2,1)S(1)}, bf16[8,32,128]{2,1,0:T(8,128)(2,1)S(1)}, u32[]{:S(2)}, u32[]{:S(2)}) collective-permute-start(bf16[8,32,128]{2,1,0:T(8,128)(2,1)S(1)} %add_convert_fusion.1.refs_0_), channel_id=1, source_target_pairs={{0,4},{4,0},{8,12},{12,8},{1,5},{5,1},{9,13},{13,9},{2,6},{6,2},{1... | collective-permute-start | bytes 196616 | tf_op jit(solution)/shard_map/ppermute | solution.py:22
  21.2 7.6 %collective-permute-start.7 = (bf16[32,32,128]{2,1,0:T(8,128)(2,1)S(1)}, bf16[32,32,128]{2,1,0:T(8,128)(2,1)S(1)}, u32[]{:S(2)}, u32[]{:S(2)}) collective-permute-start(bf16[32,32,128]{2,1,0:T(8,128)(2,1)S(1)} %collective-permute-done.6.same_ref), channel_id=1, source_target_pairs={{0,2},{2,0},{1,3},{3,1},{4,6},{6,4},{5,7},{7,5},{8,10},{10,8},{9,1... | collective-permute-start | bytes 786440 | tf_op jit(solution)/shard_map/ppermute | solution.py:22
  25.6 10.8 %collective-permute-start.5 = (bf16[32,32,128]{2,1,0:T(8,128)(2,1)S(1)}, bf16[32,32,128]{2,1,0:T(8,128)(2,1)S(1)}, u32[]{:S(2)}, u32[]{:S(2)}) collective-permute-start(bf16[32,32,128]{2,1,0:T(8,128)(2,1)S(1)} %collective-permute-done.same_ref), channel_id=1, source_target_pairs={{0,2},{2,0},{1,3},{3,1},{4,6},{6,4},{5,7},{7,5},{8,10},{10,8},{9,1... | collective-permute-start | bytes 786440 | tf_op jit(solution)/shard_map/ppermute | solution.py:22
  27.2 9.1 %collective-permute-start.8 = (bf16[16,32,128]{2,1,0:T(8,128)(2,1)S(1)}, bf16[16,32,128]{2,1,0:T(8,128)(2,1)S(1)}, u32[]{:S(2)}, u32[]{:S(2)}) collective-permute-start(bf16[16,32,128]{2,1,0:T(8,128)(2,1)S(1)} %get-tuple-element.44), channel_id=1, source_target_pairs={{0,2},{2,0},{1,3},{3,1},{4,6},{6,4},{5,7},{7,5},{8,10},{10,8},{9,1... | collective-permute-start | bytes 393224 | tf_op jit(solution)/shard_map/ppermute | solution.py:22
  39.6 8.4 %collective-permute-start.10 = (bf16[40,32,128]{2,1,0:T(8,128)(2,1)S(1)}, bf16[40,32,128]{2,1,0:T(8,128)(2,1)S(1)}, u32[]{:S(2)}, u32[]{:S(2)}) collective-permute-start(bf16[40,32,128]{2,1,0:T(8,128)(2,1)S(1)} %get-tuple-element.48), channel_id=1, source_target_pairs={{0,2},{2,0},{1,3},{3,1},{4,6},{6,4},{5,7},{7,5},{8,10},{10,8},{9,1... | collective-permute-start | bytes 983048 | tf_op jit(solution)/shard_map/ppermute | solution.py:22
  40.1 12.4 %collective-permute-start.15 = (bf16[32,32,128]{2,1,0:T(8,128)(2,1)S(1)}, bf16[32,32,128]{2,1,0:T(8,128)(2,1)S(1)}, u32[]{:S(2)}, u32[]{:S(2)}) collective-permute-start(bf16[32,32,128]{2,1,0:T(8,128)(2,1)S(1)} %get-tuple-element.47.same_ref), channel_id=1, source_target_pairs={{0,12},{4,8},{8,4},{12,0},{1,13},{5,9},{9,5},{13,1},{2,14},{6,10},... | collective-permute-start | bytes 786440 | tf_op jit(solution)/shard_map/ppermute | solution.py:22
  42.8 11.8 %collective-permute-start.9 = (bf16[32,32,128]{2,1,0:T(8,128)(2,1)S(1)}, bf16[32,32,128]{2,1,0:T(8,128)(2,1)S(1)}, u32[]{:S(2)}, u32[]{:S(2)}) collective-permute-start(bf16[32,32,128]{2,1,0:T(8,128)(2,1)S(1)} %get-tuple-element.47.same_ref), channel_id=1, source_target_pairs={{0,4},{4,0},{8,12},{12,8},{1,5},{5,1},{9,13},{13,9},{2,6},{6,2},{1... | collective-permute-start | bytes 786440 | tf_op jit(solution)/shard_map/ppermute | solution.py:22
  48.0 9.2 %collective-permute-start.13 = (bf16[8,32,128]{2,1,0:T(8,128)(2,1)S(1)}, bf16[8,32,128]{2,1,0:T(8,128)(2,1)S(1)}, u32[]{:S(2)}, u32[]{:S(2)}) collective-permute-start(bf16[8,32,128]{2,1,0:T(8,128)(2,1)S(1)} %add_convert_fusion.refs_0_), channel_id=1, source_target_pairs={{0,12},{4,8},{8,4},{12,0},{1,13},{5,9},{9,5},{13,1},{2,14},{6,10},... | collective-permute-start | bytes 196616 | tf_op jit(solution)/shard_map/ppermute | solution.py:22
  49.6 9.5 %collective-permute-start.12 = (bf16[8,32,128]{2,1,0:T(8,128)(2,1)S(1)}, bf16[8,32,128]{2,1,0:T(8,128)(2,1)S(1)}, u32[]{:S(2)}, u32[]{:S(2)}) collective-permute-start(bf16[8,32,128]{2,1,0:T(8,128)(2,1)S(1)} %add_convert_fusion.refs_0_), channel_id=1, source_target_pairs={{0,8},{4,12},{8,0},{12,4},{1,9},{5,13},{9,1},{13,5},{2,10},{6,14},... | collective-permute-start | bytes 196616 | tf_op jit(solution)/shard_map/ppermute | solution.py:22
  51.0 8.0 %collective-permute-start.11 = (bf16[8,32,128]{2,1,0:T(8,128)(2,1)S(1)}, bf16[8,32,128]{2,1,0:T(8,128)(2,1)S(1)}, u32[]{:S(2)}, u32[]{:S(2)}) collective-permute-start(bf16[8,32,128]{2,1,0:T(8,128)(2,1)S(1)} %add_convert_fusion.refs_0_), channel_id=1, source_target_pairs={{0,4},{4,0},{8,12},{12,8},{1,5},{5,1},{9,13},{13,9},{2,6},{6,2},{1... | collective-permute-start | bytes 196616 | tf_op jit(solution)/shard_map/ppermute | solution.py:22
  52.5 9.8 %collective-permute-start.16 = (bf16[32,32,128]{2,1,0:T(8,128)(2,1)S(1)}, bf16[32,32,128]{2,1,0:T(8,128)(2,1)S(1)}, u32[]{:S(2)}, u32[]{:S(2)}) collective-permute-start(bf16[32,32,128]{2,1,0:T(8,128)(2,1)S(1)} %collective-permute-done.15.same_ref), channel_id=1, source_target_pairs={{0,2},{2,0},{1,3},{3,1},{4,6},{6,4},{5,7},{7,5},{8,10},{10,8},{9,1... | collective-permute-start | bytes 786440 | tf_op jit(solution)/shard_map/ppermute | solution.py:22
  59.1 9.9 %collective-permute-start.14 = (bf16[32,32,128]{2,1,0:T(8,128)(2,1)S(1)}, bf16[32,32,128]{2,1,0:T(8,128)(2,1)S(1)}, u32[]{:S(2)}, u32[]{:S(2)}) collective-permute-start(bf16[32,32,128]{2,1,0:T(8,128)(2,1)S(1)} %collective-permute-done.9.same_ref), channel_id=1, source_target_pairs={{0,2},{2,0},{1,3},{3,1},{4,6},{6,4},{5,7},{7,5},{8,10},{10,8},{9,1... | collective-permute-start | bytes 786440 | tf_op jit(solution)/shard_map/ppermute | solution.py:22
  61.6 7.3 %collective-permute-start.17 = (bf16[16,32,128]{2,1,0:T(8,128)(2,1)S(1)}, bf16[16,32,128]{2,1,0:T(8,128)(2,1)S(1)}, u32[]{:S(2)}, u32[]{:S(2)}) collective-permute-start(bf16[16,32,128]{2,1,0:T(8,128)(2,1)S(1)} %get-tuple-element.57), channel_id=1, source_target_pairs={{0,2},{2,0},{1,3},{3,1},{4,6},{6,4},{5,7},{7,5},{8,10},{10,8},{9,1... | collective-permute-start | bytes 393224 | tf_op jit(solution)/shard_map/ppermute | solution.py:22

commit v4 on v3

--- a/solution.py
+++ b/solution.py
@@ -205,20 +205,29 @@
 
 
 def finish_kernel(plan_ref, same_ref, other_ref, blocks_ref, acc_in, far_ref, far_other_ref, basis_ref, *refs):
-    out_ref, (acc_ref, whole) = refs[0], refs[-2:]
+    out_hbm, (acc_ref, whole, out_ref, sent) = refs[0], refs[-4:]
     near_halves_kernel(2, plan_ref, same_ref, other_ref, blocks_ref, acc_in, acc_ref, whole)
     half, _, wide = far_other_ref.shape
     rank = wide // 2
-    for n in range(half):
-        for m, other in ((n, far_other_ref[n, :, :rank]), (n + half, far_other_ref[n, :, rank:])):
-            far_low = (far_ref[m] + other.astype(jnp.float32)).astype(jnp.bfloat16)
-            out_ref[m] = acc_ref[m] + dot(far_low, basis_ref[m], PLAIN)
-    if len(refs) == 7:
+    pieces = sent.shape[0]
+    size = 2 * half // pieces
+    copies = []
+    for n in range(2 * half):
+        other = far_other_ref[n, :, :rank] if n < half else far_other_ref[n - half, :, rank:]
+        far_low = (far_ref[n] + other.astype(jnp.float32)).astype(jnp.bfloat16)
+        out_ref[n] = acc_ref[n] + dot(far_low, basis_ref[n], PLAIN)
+        if (n + 1) % size == 0:
+            rows = pl.ds(n + 1 - size, size)
+            copies.append(pltpu.make_async_copy(out_ref.at[rows], out_hbm.at[rows], sent.at[n // size]))
+            copies[-1].start()
+    if len(refs) == 9:
         mine_ref, keep_ref, send_ref, parts = refs[1:5]
         low = out_ref[...].astype(jnp.bfloat16)
         mine_ref[...] = low
         send_ref[: 2 * half] = low
         put_projection(mine_ref, basis_ref, keep_ref, send_ref, 2 * half, parts)
+    for copy in copies:
+        copy.wait()
 
 
 def tiled_on_device(right_panel, near_field_blocks, near_list, cluster_basis, coupling, far_list):
@@ -350,9 +359,10 @@
             finish_kernel,
             out_shape=outs,
             in_specs=[SMEM] + [VMEM] * 7,
-            out_specs=(VMEM,) * len(outs),
+            out_specs=(HBM,) + (VMEM,) * (len(outs) - 1),
             scratch_shapes=([] if last else [parts])
-            + [pltpu.VMEM(acc_shape.shape, f32), pltpu.VMEM(low_shape.shape, bf16)],
+            + [pltpu.VMEM(acc_shape.shape, f32), pltpu.VMEM(low_shape.shape, bf16)]
+            + [pltpu.VMEM(out_shape.shape, f32), pltpu.SemaphoreType.DMA((4,))],
             compiler_params=params(),
             cost_estimate=cost(4),
             name="finish",

time: 71.2 us -> 70 us (0.983); the launches traced: 72 us -> 69.7 us
  waiting for transfers between devices: 25 us -> 22 us
  Pallas kernels: 20.8 us -> 22.4 us
  starting transfers between devices: 24.6 us -> 23.7 us
    ppermute x18, waiting for transfers between devices: 25 us -> 22 us  [swapped(): lax.ppermute(array, axis, [(i, partner(i)) for i in range(lax.axis_size(a...]
    pallas_call x2, Pallas kernels: 6.36 us -> 5.16 us  [finish(): pl.pallas_call(finish_kernel, out_shape=outs, in_specs=[SMEM] + [VMEM] *...]
    pallas_call x1, Pallas kernels: 4.11 us -> 5.2 us  [tiled_on_device(): pl.pallas_call(prepare_kernel, out_shape=(pltpu.VMEM(near_field_blocks.sh...]
    ppermute x18, starting transfers between devices: 24.6 us -> 23.7 us  [swapped(): lax.ppermute(array, axis, [(i, partner(i)) for i in range(lax.axis_size(a...]
    pallas_call x3, Pallas kernels: 3.62 us -> 4.55 us  [near_halves(): pl.pallas_call(functools.partial(near_halves_kernel, kind), out_shape=acc...]
    pallas_call x2, Pallas kernels: 2.18 us -> 2.98 us  [far(): pl.pallas_call(far_kernel, out_shape=(jax.ShapeDtypeStruct((clusters, col...]
  transfers between devices with their start and end apart: 18 -> 18, of which waited for: 7 -> 9; matrix products, arithmetic and copies ran while one was open for 1% -> 1% of each run, Pallas kernels for 17% -> 22%
where the time goes in v4:
time: 70 us; the launch traced here: 69.7 us
  starting transfers between devices  23.7 us (34%)
  Pallas kernels  22.4 us (32%)
  waiting for transfers between devices  22 us (31%)
  other arithmetic  0.82 us (1%)
  between operations  0.76 us (1%)
    ppermute x18, starting transfers between devices, swapped(): lax.ppermute(array, axis, [(i, partner(i)) for i in range(lax.axis_size(a...  23.7 us
    ppermute x18, waiting for transfers between devices, swapped(): lax.ppermute(array, axis, [(i, partner(i)) for i in range(lax.axis_size(a...  22 us
    pallas_call x1, Pallas kernels, tiled_on_device(): pl.pallas_call(prepare_kernel, out_shape=(pltpu.VMEM(near_field_blocks.sh...  5.2 us
    pallas_call x2, Pallas kernels, finish(): pl.pallas_call(finish_kernel, out_shape=outs, in_specs=[SMEM] + [VMEM] *...  5.16 us
    pallas_call x3, Pallas kernels, near_halves(): pl.pallas_call(functools.partial(near_halves_kernel, kind), out_shape=acc...  4.55 us
    pallas_call x2, Pallas kernels, far(): pl.pallas_call(far_kernel, out_shape=(jax.ShapeDtypeStruct((clusters, col...  2.98 us
    pallas_call x1, Pallas kernels, tiled_on_device(): pl.pallas_call(start_kernel, out_shape=(mine_shape, jax.ShapeDtypeStruct(...  1.9 us
    pallas_call x1, Pallas kernels, near_own(): pl.pallas_call(near_own_kernel, out_shape=acc_shape, in_specs=[SMEM, HBM,...  1.55 us
  transfers between devices with their start and end apart: 18, of which 9 were waited for; matrix products, arithmetic and copies ran while one was open for 1% of the time, Pallas kernels for 22%

profile of v4, /device:TPU:0, one launch (start us, length us, event | category | flops | bytes accessed | tf_op | source)
XLA Modules:
  0.0 69.7 jit_solution(4776090626059882110)
XLA Ops:
  0.6 1.9 %start.1 = (bf16[32,32,128]{2,1,0:T(8,128)(2,1)S(1)}, bf16[32,64,128]{2,1,0:T(8,128)(2,1)S(1)}, f32[8,32,128]{2,1,0:T(8,128)S(1)}, bf16[8,32,128]{2,1,0:T(8,128)(2,1)S(1)}) custom-call(f32[32,32,256]{2,1,0:T(8,128)} %bitcast.43, bf16[32,64,128]{2,1,0:T(8,128)(2,1)} %bitcast.46), custom_call_target="tpu_custom_call" | custom-call | bytes 7380000 | tf_op jit(solution)/shard_map/start/pallas_call | solution.py:265
  2.6 3.0 %collective-permute-start.1 = (bf16[8,32,128]{2,1,0:T(8,128)(2,1)S(1)}, bf16[8,32,128]{2,1,0:T(8,128)(2,1)S(1)}, u32[]{:S(2)}, u32[]{:S(2)}) collective-permute-start(bf16[8,32,128]{2,1,0:T(8,128)(2,1)S(1)} %get-tuple-element.35), channel_id=1, source_target_pairs={{0,2},{2,0},{1,3},{3,1},{4,6},{6,4},{5,7},{7,5},{8,10},{10,8},{9,1... | collective-permute-start | bytes 196616 | tf_op jit(solution)/shard_map/ppermute | solution.py:22
  5.6 3.6 %collective-permute-start.6 = (bf16[32,32,128]{2,1,0:T(8,128)(2,1)S(1)}, bf16[32,32,128]{2,1,0:T(8,128)(2,1)S(1)}, u32[]{:S(2)}, u32[]{:S(2)}) collective-permute-start(bf16[32,32,128]{2,1,0:T(8,128)(2,1)S(1)} %get-tuple-element.31), channel_id=1, source_target_pairs={{0,12},{4,8},{8,4},{12,0},{1,13},{5,9},{9,5},{13,1},{2,14},{6,10},... | collective-permute-start | bytes 786440 | tf_op jit(solution)/shard_map/ppermute | solution.py:22
  9.2 2.8 %collective-permute-start.4 = (bf16[8,32,128]{2,1,0:T(8,128)(2,1)S(1)}, bf16[8,32,128]{2,1,0:T(8,128)(2,1)S(1)}, u32[]{:S(2)}, u32[]{:S(2)}) collective-permute-start(bf16[8,32,128]{2,1,0:T(8,128)(2,1)S(1)} %add_convert_fusion.1.refs_0_), channel_id=1, source_target_pairs={{0,12},{4,8},{8,4},{12,0},{1,13},{5,9},{9,5},{13,1},{2,14},{6,10},... | collective-permute-start | bytes 196616 | tf_op jit(solution)/shard_map/ppermute | solution.py:22
  12.7 0.9 %collective-permute-start.2 = (bf16[8,32,128]{2,1,0:T(8,128)(2,1)S(1)}, bf16[8,32,128]{2,1,0:T(8,128)(2,1)S(1)}, u32[]{:S(2)}, u32[]{:S(2)}) collective-permute-start(bf16[8,32,128]{2,1,0:T(8,128)(2,1)S(1)} %add_convert_fusion.1.refs_0_), channel_id=1, source_target_pairs={{0,4},{4,0},{8,12},{12,8},{1,5},{5,1},{9,13},{13,9},{2,6},{6,2},{1... | collective-permute-start | bytes 196616 | tf_op jit(solution)/shard_map/ppermute | solution.py:22
  13.6 0.8 %fusion = (s32[1,128]{1,0:T(1,128)S(1)}, s32[1,128]{1,0:T(1,128)S(1)}) fusion(s32[128,2]{0,1:T(2,128)} %param.8, s32[]{:T(128)S(6)} %mul.15, s32[]{:T(128)S(6)} %xor.14, s32[]{:T(128)S(6)} %axis_index.25, s32[128,2]{0,1:T(2,128)} %param.11, s32[]{:T(128)S(6)} %axis_index.28), kind=kLoop, calls=%fused_computation.20 | loop fusion | flops 10240 | bytes 3088 | tf_op jit(solution)/shard_map/or | solution.py:246
  14.4 1.1 %plan.1 = (s32[4,144]{1,0:T(4,128)S(4)}, s32[3,160]{1,0:T(4,128)S(4)}) custom-call(s32[1,128]{1,0:T(1,128)S(1)} %get-tuple-element.58.near_ref, s32[1,128]{1,0:T(1,128)S(1)} %get-tuple-element.59.far_ref), custom_call_target="tpu_custom_call" | custom-call | bytes 3690000 | tf_op jit(solution)/shard_map/plan/pallas_call | solution.py:275
  15.5 5.2 %prepare.1 = (bf16[128,128,256]{2,1,0:T(8,128)(2,1)S(1)}, bf16[160,64,64]{2,1,0:T(8,128)(2,1)S(1)}) custom-call(s32[3,160]{1,0:T(4,128)S(4)} %get-tuple-element.32.far_plan_ref.plan_ref, bf16[128,128,256]{2,1,0:T(8,128)(2,1)} %blocks_hbm.1, bf16[64,64,128]{2,1,0:T(8,128)(2,1)} %bitcast.45), custom_call_target="tpu_custom_call" | custom-call | bytes 14760000 | tf_op jit(solution)/shard_map/prepare/pallas_call | solution.py:292
  20.7 1.6 %near_own.1.refs_0_ = f32[33,32,128]{2,1,0:T(8,128)S(1)} custom-call(s32[4,144]{1,0:T(4,128)S(4)} %get-tuple-element.30.plan_ref, f32[32,32,256]{2,1,0:T(8,128)S(1)} %bitcast.44, bf16[128,128,256]{2,1,0:T(8,128)(2,1)S(1)} %get-tuple-element.33.blocks_ref), custom_call_target="tpu_custom_call" | custom-call | bytes 11070000 | tf_op jit(solution)/shard_map/near_own/pallas_call | solution.py:311
  22.4 1.3 %collective-permute-done.4.refs_3_ = bf16[8,32,128]{2,1,0:T(8,128)(2,1)S(1)} collective-permute-done((bf16[8,32,128]{2,1,0:T(8,128)(2,1)S(1)}, bf16[8,32,128]{2,1,0:T(8,128)(2,1)S(1)}, u32[]{:S(2)}, u32[]{:S(2)}) %collective-permute-start.4) | collective-permute-done | bytes 65568 | tf_op jit(solution)/shard_map/ppermute | solution.py:22
  23.6 1.9 %collective-permute-done.3.refs_2_ = bf16[8,32,128]{2,1,0:T(8,128)(2,1)S(1)} collective-permute-done((bf16[8,32,128]{2,1,0:T(8,128)(2,1)S(1)}, bf16[8,32,128]{2,1,0:T(8,128)(2,1)S(1)}, u32[]{:S(2)}, u32[]{:S(2)}) %collective-permute-start.3) | collective-permute-done | bytes 65568 | tf_op jit(solution)/shard_map/ppermute | solution.py:22
  26.1 1.5 %far.2 = (f32[32,32,64]{2,1,0:T(8,128)S(1)}, bf16[16,32,128]{2,1,0:T(8,128)(2,1)S(1)}) custom-call(s32[3,160]{1,0:T(4,128)S(4)} %get-tuple-element.32.far_plan_ref.plan_ref, bf16[160,64,64]{2,1,0:T(8,128)(2,1)S(1)} %get-tuple-element.38.pairs_ref, bf16[8,32,128]{2,1,0:T(8,128)(2,1)S(1)} %add_convert_fusion.1.refs_0_, ...), custom_call_target="tpu_custom_call" | custom-call | bytes 11070000 | tf_op jit(solution)/shard_map/far/pallas_call | solution.py:339
  27.6 1.2 %collective-permute-start.8 = (bf16[16,32,128]{2,1,0:T(8,128)(2,1)S(1)}, bf16[16,32,128]{2,1,0:T(8,128)(2,1)S(1)}, u32[]{:S(2)}, u32[]{:S(2)}) collective-permute-start(bf16[16,32,128]{2,1,0:T(8,128)(2,1)S(1)} %get-tuple-element.44), channel_id=1, source_target_pairs={{0,2},{2,0},{1,3},{3,1},{4,6},{6,4},{5,7},{7,5},{8,10},{10,8},{9,1... | collective-permute-start | bytes 393224 | tf_op jit(solution)/shard_map/ppermute | solution.py:22
  28.8 2.2 %collective-permute-done.7.other_ref = bf16[32,32,128]{2,1,0:T(8,128)(2,1)S(1)} collective-permute-done((bf16[32,32,128]{2,1,0:T(8,128)(2,1)S(1)}, bf16[32,32,128]{2,1,0:T(8,128)(2,1)S(1)}, u32[]{:S(2)}, u32[]{:S(2)}) %collective-permute-start.7) | collective-permute-done | bytes 262176 | tf_op jit(solution)/shard_map/ppermute | solution.py:22
  31.0 1.5 %near_halves.3.acc_in = f32[33,32,128]{2,1,0:T(8,128)S(1)} custom-call(s32[4,144]{1,0:T(4,128)S(4)} %get-tuple-element.30.plan_ref, bf16[32,32,128]{2,1,0:T(8,128)(2,1)S(1)} %collective-permute-done.6.same_ref, bf16[32,32,128]{2,1,0:T(8,128)(2,1)S(1)} %collective-permute-done.7.other_ref, bf16[128,128,256]{2,1,0:T(8,128)(2,1)S(1)} %get-tuple-element.33.blocks_ref, ...), custom_call_target="tpu_custom_call" | custom-call | bytes 7380000 | tf_op jit(solution)/shard_map/near_halves/pallas_call | solution.py:327
  32.5 4.9 %collective-permute-done.8.far_other_ref = bf16[16,32,128]{2,1,0:T(8,128)(2,1)S(1)} collective-permute-done((bf16[16,32,128]{2,1,0:T(8,128)(2,1)S(1)}, bf16[16,32,128]{2,1,0:T(8,128)(2,1)S(1)}, u32[]{:S(2)}, u32[]{:S(2)}) %collective-permute-start.8) | collective-permute-done | bytes 131104 | tf_op jit(solution)/shard_map/ppermute | solution.py:22
  37.4 2.7 %finish.2 = (f32[32,32,128]{2,1,0:T(8,128)}, bf16[32,32,128]{2,1,0:T(8,128)(2,1)S(1)}, f32[8,32,128]{2,1,0:T(8,128)S(1)}, bf16[40,32,128]{2,1,0:T(8,128)(2,1)S(1)}) custom-call(s32[4,144]{1,0:T(4,128)S(4)} %get-tuple-element.30.plan_ref, bf16[32,32,128]{2,1,0:T(8,128)(2,1)S(1)} %collective-permute-done.same_ref, ...), custom_call_target="tpu_custom_call" | custom-call | bytes 14760000 | tf_op jit(solution)/shard_map/finish/pallas_call | solution.py:358
  40.4 3.4 %collective-permute-start.15 = (bf16[32,32,128]{2,1,0:T(8,128)(2,1)S(1)}, bf16[32,32,128]{2,1,0:T(8,128)(2,1)S(1)}, u32[]{:S(2)}, u32[]{:S(2)}) collective-permute-start(bf16[32,32,128]{2,1,0:T(8,128)(2,1)S(1)} %get-tuple-element.47.same_ref), channel_id=1, source_target_pairs={{0,12},{4,8},{8,4},{12,0},{1,13},{5,9},{9,5},{13,1},{2,14},{6,10},... | collective-permute-start | bytes 786440 | tf_op jit(solution)/shard_map/ppermute | solution.py:22
  43.8 4.1 %collective-permute-done.10.other_ref = bf16[40,32,128]{2,1,0:T(8,128)(2,1)S(1)} collective-permute-done((bf16[40,32,128]{2,1,0:T(8,128)(2,1)S(1)}, bf16[40,32,128]{2,1,0:T(8,128)(2,1)S(1)}, u32[]{:S(2)}, u32[]{:S(2)}) %collective-permute-start.10) | collective-permute-done | bytes 327712 | tf_op jit(solution)/shard_map/ppermute | solution.py:22
  47.9 1.3 %collective-permute-start.13 = (bf16[8,32,128]{2,1,0:T(8,128)(2,1)S(1)}, bf16[8,32,128]{2,1,0:T(8,128)(2,1)S(1)}, u32[]{:S(2)}, u32[]{:S(2)}) collective-permute-start(bf16[8,32,128]{2,1,0:T(8,128)(2,1)S(1)} %add_convert_fusion.refs_0_), channel_id=1, source_target_pairs={{0,12},{4,8},{8,4},{12,0},{1,13},{5,9},{9,5},{13,1},{2,14},{6,10},... | collective-permute-start | bytes 196616 | tf_op jit(solution)/shard_map/ppermute | solution.py:22
  49.2 1.3 %collective-permute-start.12 = (bf16[8,32,128]{2,1,0:T(8,128)(2,1)S(1)}, bf16[8,32,128]{2,1,0:T(8,128)(2,1)S(1)}, u32[]{:S(2)}, u32[]{:S(2)}) collective-permute-start(bf16[8,32,128]{2,1,0:T(8,128)(2,1)S(1)} %add_convert_fusion.refs_0_), channel_id=1, source_target_pairs={{0,8},{4,12},{8,0},{12,4},{1,9},{5,13},{9,1},{13,5},{2,10},{6,14},... | collective-permute-start | bytes 196616 | tf_op jit(solution)/shard_map/ppermute | solution.py:22
  50.5 1.9 %collective-permute-start.11 = (bf16[8,32,128]{2,1,0:T(8,128)(2,1)S(1)}, bf16[8,32,128]{2,1,0:T(8,128)(2,1)S(1)}, u32[]{:S(2)}, u32[]{:S(2)}) collective-permute-start(bf16[8,32,128]{2,1,0:T(8,128)(2,1)S(1)} %add_convert_fusion.refs_0_), channel_id=1, source_target_pairs={{0,4},{4,0},{8,12},{12,8},{1,5},{5,1},{9,13},{13,9},{2,6},{6,2},{1... | collective-permute-start | bytes 196616 | tf_op jit(solution)/shard_map/ppermute | solution.py:22
  52.4 0.9 %collective-permute-start.16 = (bf16[32,32,128]{2,1,0:T(8,128)(2,1)S(1)}, bf16[32,32,128]{2,1,0:T(8,128)(2,1)S(1)}, u32[]{:S(2)}, u32[]{:S(2)}) collective-permute-start(bf16[32,32,128]{2,1,0:T(8,128)(2,1)S(1)} %collective-permute-done.15.same_ref), channel_id=1, source_target_pairs={{0,2},{2,0},{1,3},{3,1},{4,6},{6,4},{5,7},{7,5},{8,10},{10,8},{9,1... | collective-permute-start | bytes 786440 | tf_op jit(solution)/shard_map/ppermute | solution.py:22
  53.3 1.5 %near_halves.4.refs_0_ = f32[33,32,128]{2,1,0:T(8,128)S(1)} custom-call(s32[4,144]{1,0:T(4,128)S(4)} %get-tuple-element.30.plan_ref, bf16[32,32,128]{2,1,0:T(8,128)(2,1)S(1)} %get-tuple-element.47.same_ref, bf16[40,32,128]{2,1,0:T(8,128)(2,1)S(1)} %collective-permute-done.10.other_ref, bf16[128,128,256]{2,1,0:T(8,128)(2,1)S(1)} %get-tuple-element.33.blocks_ref), custom_call_target="tpu_custom_call" | custom-call | bytes 7380000 | tf_op jit(solution)/shard_map/near_halves/pallas_call | solution.py:327
  54.8 1.3 %collective-permute-done.9.same_ref = bf16[32,32,128]{2,1,0:T(8,128)(2,1)S(1)} collective-permute-done((bf16[32,32,128]{2,1,0:T(8,128)(2,1)S(1)}, bf16[32,32,128]{2,1,0:T(8,128)(2,1)S(1)}, u32[]{:S(2)}, u32[]{:S(2)}) %collective-permute-start.9) | collective-permute-done | bytes 262176 | tf_op jit(solution)/shard_map/ppermute | solution.py:22
  56.1 1.1 %collective-permute-done.13.refs_3_ = bf16[8,32,128]{2,1,0:T(8,128)(2,1)S(1)} collective-permute-done((bf16[8,32,128]{2,1,0:T(8,128)(2,1)S(1)}, bf16[8,32,128]{2,1,0:T(8,128)(2,1)S(1)}, u32[]{:S(2)}, u32[]{:S(2)}) %collective-permute-start.13) | collective-permute-done | bytes 65568 | tf_op jit(solution)/shard_map/ppermute | solution.py:22
  57.3 1.2 %collective-permute-done.12.refs_2_ = bf16[8,32,128]{2,1,0:T(8,128)(2,1)S(1)} collective-permute-done((bf16[8,32,128]{2,1,0:T(8,128)(2,1)S(1)}, bf16[8,32,128]{2,1,0:T(8,128)(2,1)S(1)}, u32[]{:S(2)}, u32[]{:S(2)}) %collective-permute-start.12) | collective-permute-done | bytes 65568 | tf_op jit(solution)/shard_map/ppermute | solution.py:22
  58.5 1.5 %collective-permute-start.14 = (bf16[32,32,128]{2,1,0:T(8,128)(2,1)S(1)}, bf16[32,32,128]{2,1,0:T(8,128)(2,1)S(1)}, u32[]{:S(2)}, u32[]{:S(2)}) collective-permute-start(bf16[32,32,128]{2,1,0:T(8,128)(2,1)S(1)} %collective-permute-done.9.same_ref), channel_id=1, source_target_pairs={{0,2},{2,0},{1,3},{3,1},{4,6},{6,4},{5,7},{7,5},{8,10},{10,8},{9,1... | collective-permute-start | bytes 786440 | tf_op jit(solution)/shard_map/ppermute | solution.py:22
  60.0 1.5 %far.3 = (f32[32,32,64]{2,1,0:T(8,128)S(1)}, bf16[16,32,128]{2,1,0:T(8,128)(2,1)S(1)}) custom-call(s32[3,160]{1,0:T(4,128)S(4)} %get-tuple-element.32.far_plan_ref.plan_ref, bf16[160,64,64]{2,1,0:T(8,128)(2,1)S(1)} %get-tuple-element.38.pairs_ref, bf16[8,32,128]{2,1,0:T(8,128)(2,1)S(1)} %add_convert_fusion.refs_0_, ...), custom_call_target="tpu_custom_call" | custom-call | bytes 11070000 | tf_op jit(solution)/shard_map/far/pallas_call | solution.py:339
  61.7 1.5 %near_halves.5.acc_in = f32[33,32,128]{2,1,0:T(8,128)S(1)} custom-call(s32[4,144]{1,0:T(4,128)S(4)} %get-tuple-element.30.plan_ref, bf16[32,32,128]{2,1,0:T(8,128)(2,1)S(1)} %collective-permute-done.15.same_ref, bf16[32,32,128]{2,1,0:T(8,128)(2,1)S(1)} %collective-permute-done.16.other_ref, bf16[128,128,256]{2,1,0:T(8,128)(2,1)S(1)} %get-tuple-element.33.blocks_ref, ...), custom_call_target="tpu_custom_call" | custom-call | bytes 7380000 | tf_op jit(solution)/shard_map/near_halves/pallas_call | solution.py:327
  63.2 4.0 %collective-permute-done.17.far_other_ref = bf16[16,32,128]{2,1,0:T(8,128)(2,1)S(1)} collective-permute-done((bf16[16,32,128]{2,1,0:T(8,128)(2,1)S(1)}, bf16[16,32,128]{2,1,0:T(8,128)(2,1)S(1)}, u32[]{:S(2)}, u32[]{:S(2)}) %collective-permute-start.17) | collective-permute-done | bytes 131104 | tf_op jit(solution)/shard_map/ppermute | solution.py:22
  67.2 2.5 %finish.3 = f32[32,32,128]{2,1,0:T(8,128)} custom-call(s32[4,144]{1,0:T(4,128)S(4)} %get-tuple-element.30.plan_ref, bf16[32,32,128]{2,1,0:T(8,128)(2,1)S(1)} %collective-permute-done.9.same_ref, bf16[32,32,128]{2,1,0:T(8,128)(2,1)S(1)} %collective-permute-done.14.other_ref, bf16[128,128,256]{2,1,0:T(8,128)(2,1)S(1)} %get-tuple-element.33.blocks_ref, ...), custom_call_target="tpu_custom_call" | custom-call | bytes 14760000 | tf_op jit(solution)/shard_map/finish/pallas_call | solution.py:358
  (20 shorter events, 1.9 us)
Async XLA Ops:
  0.6 20.1 %copy-start = (f32[32,256,32]{1,2,0:T(8,128)S(1)}, f32[32,256,32]{1,2,0:T(8,128)}, u32[]{:S(2)}) copy-start(f32[32,256,32]{1,2,0:T(8,128)} %param.6) | copy-start | bytes 3145732
  2.6 6.6 %collective-permute-start.1 = (bf16[8,32,128]{2,1,0:T(8,128)(2,1)S(1)}, bf16[8,32,128]{2,1,0:T(8,128)(2,1)S(1)}, u32[]{:S(2)}, u32[]{:S(2)}) collective-permute-start(bf16[8,32,128]{2,1,0:T(8,128)(2,1)S(1)} %get-tuple-element.35), channel_id=1, source_target_pairs={{0,2},{2,0},{1,3},{3,1},{4,6},{6,4},{5,7},{7,5},{8,10},{10,8},{9,1... | collective-permute-start | bytes 196616 | tf_op jit(solution)/shard_map/ppermute | solution.py:22
  5.6 16.7 %collective-permute-start.6 = (bf16[32,32,128]{2,1,0:T(8,128)(2,1)S(1)}, bf16[32,32,128]{2,1,0:T(8,128)(2,1)S(1)}, u32[]{:S(2)}, u32[]{:S(2)}) collective-permute-start(bf16[32,32,128]{2,1,0:T(8,128)(2,1)S(1)} %get-tuple-element.31), channel_id=1, source_target_pairs={{0,12},{4,8},{8,4},{12,0},{1,13},{5,9},{9,5},{13,1},{2,14},{6,10},... | collective-permute-start | bytes 786440 | tf_op jit(solution)/shard_map/ppermute | solution.py:22
  9.2 16.4 %collective-permute-start = (bf16[32,32,128]{2,1,0:T(8,128)(2,1)S(1)}, bf16[32,32,128]{2,1,0:T(8,128)(2,1)S(1)}, u32[]{:S(2)}, u32[]{:S(2)}) collective-permute-start(bf16[32,32,128]{2,1,0:T(8,128)(2,1)S(1)} %get-tuple-element.31), channel_id=1, source_target_pairs={{0,4},{4,0},{8,12},{12,8},{1,5},{5,1},{9,13},{13,9},{2,6},{6,2},{1... | collective-permute-start | bytes 786440 | tf_op jit(solution)/shard_map/ppermute | solution.py:22
  9.2 14.5 %collective-permute-start.4 = (bf16[8,32,128]{2,1,0:T(8,128)(2,1)S(1)}, bf16[8,32,128]{2,1,0:T(8,128)(2,1)S(1)}, u32[]{:S(2)}, u32[]{:S(2)}) collective-permute-start(bf16[8,32,128]{2,1,0:T(8,128)(2,1)S(1)} %add_convert_fusion.1.refs_0_), channel_id=1, source_target_pairs={{0,12},{4,8},{8,4},{12,0},{1,13},{5,9},{9,5},{13,1},{2,14},{6,10},... | collective-permute-start | bytes 196616 | tf_op jit(solution)/shard_map/ppermute | solution.py:22
  12.0 13.6 %collective-permute-start.3 = (bf16[8,32,128]{2,1,0:T(8,128)(2,1)S(1)}, bf16[8,32,128]{2,1,0:T(8,128)(2,1)S(1)}, u32[]{:S(2)}, u32[]{:S(2)}) collective-permute-start(bf16[8,32,128]{2,1,0:T(8,128)(2,1)S(1)} %add_convert_fusion.1.refs_0_), channel_id=1, source_target_pairs={{0,8},{4,12},{8,0},{12,4},{1,9},{5,13},{9,1},{13,5},{2,10},{6,14},... | collective-permute-start | bytes 196616 | tf_op jit(solution)/shard_map/ppermute | solution.py:22
  12.7 12.8 %collective-permute-start.2 = (bf16[8,32,128]{2,1,0:T(8,128)(2,1)S(1)}, bf16[8,32,128]{2,1,0:T(8,128)(2,1)S(1)}, u32[]{:S(2)}, u32[]{:S(2)}) collective-permute-start(bf16[8,32,128]{2,1,0:T(8,128)(2,1)S(1)} %add_convert_fusion.1.refs_0_), channel_id=1, source_target_pairs={{0,4},{4,0},{8,12},{12,8},{1,5},{5,1},{9,13},{13,9},{2,6},{6,2},{1... | collective-permute-start | bytes 196616 | tf_op jit(solution)/shard_map/ppermute | solution.py:22
  22.3 8.7 %collective-permute-start.7 = (bf16[32,32,128]{2,1,0:T(8,128)(2,1)S(1)}, bf16[32,32,128]{2,1,0:T(8,128)(2,1)S(1)}, u32[]{:S(2)}, u32[]{:S(2)}) collective-permute-start(bf16[32,32,128]{2,1,0:T(8,128)(2,1)S(1)} %collective-permute-done.6.same_ref), channel_id=1, source_target_pairs={{0,2},{2,0},{1,3},{3,1},{4,6},{6,4},{5,7},{7,5},{8,10},{10,8},{9,1... | collective-permute-start | bytes 786440 | tf_op jit(solution)/shard_map/ppermute | solution.py:22
  25.6 11.9 %collective-permute-start.5 = (bf16[32,32,128]{2,1,0:T(8,128)(2,1)S(1)}, bf16[32,32,128]{2,1,0:T(8,128)(2,1)S(1)}, u32[]{:S(2)}, u32[]{:S(2)}) collective-permute-start(bf16[32,32,128]{2,1,0:T(8,128)(2,1)S(1)} %collective-permute-done.same_ref), channel_id=1, source_target_pairs={{0,2},{2,0},{1,3},{3,1},{4,6},{6,4},{5,7},{7,5},{8,10},{10,8},{9,1... | collective-permute-start | bytes 786440 | tf_op jit(solution)/shard_map/ppermute | solution.py:22
  27.6 9.8 %collective-permute-start.8 = (bf16[16,32,128]{2,1,0:T(8,128)(2,1)S(1)}, bf16[16,32,128]{2,1,0:T(8,128)(2,1)S(1)}, u32[]{:S(2)}, u32[]{:S(2)}) collective-permute-start(bf16[16,32,128]{2,1,0:T(8,128)(2,1)S(1)} %get-tuple-element.44), channel_id=1, source_target_pairs={{0,2},{2,0},{1,3},{3,1},{4,6},{6,4},{5,7},{7,5},{8,10},{10,8},{9,1... | collective-permute-start | bytes 393224 | tf_op jit(solution)/shard_map/ppermute | solution.py:22
  40.1 7.8 %collective-permute-start.10 = (bf16[40,32,128]{2,1,0:T(8,128)(2,1)S(1)}, bf16[40,32,128]{2,1,0:T(8,128)(2,1)S(1)}, u32[]{:S(2)}, u32[]{:S(2)}) collective-permute-start(bf16[40,32,128]{2,1,0:T(8,128)(2,1)S(1)} %get-tuple-element.48), channel_id=1, source_target_pairs={{0,2},{2,0},{1,3},{3,1},{4,6},{6,4},{5,7},{7,5},{8,10},{10,8},{9,1... | collective-permute-start | bytes 983048 | tf_op jit(solution)/shard_map/ppermute | solution.py:22
  40.4 11.9 %collective-permute-start.15 = (bf16[32,32,128]{2,1,0:T(8,128)(2,1)S(1)}, bf16[32,32,128]{2,1,0:T(8,128)(2,1)S(1)}, u32[]{:S(2)}, u32[]{:S(2)}) collective-permute-start(bf16[32,32,128]{2,1,0:T(8,128)(2,1)S(1)} %get-tuple-element.47.same_ref), channel_id=1, source_target_pairs={{0,12},{4,8},{8,4},{12,0},{1,13},{5,9},{9,5},{13,1},{2,14},{6,10},... | collective-permute-start | bytes 786440 | tf_op jit(solution)/shard_map/ppermute | solution.py:22
  43.8 12.3 %collective-permute-start.9 = (bf16[32,32,128]{2,1,0:T(8,128)(2,1)S(1)}, bf16[32,32,128]{2,1,0:T(8,128)(2,1)S(1)}, u32[]{:S(2)}, u32[]{:S(2)}) collective-permute-start(bf16[32,32,128]{2,1,0:T(8,128)(2,1)S(1)} %get-tuple-element.47.same_ref), channel_id=1, source_target_pairs={{0,4},{4,0},{8,12},{12,8},{1,5},{5,1},{9,13},{13,9},{2,6},{6,2},{1... | collective-permute-start | bytes 786440 | tf_op jit(solution)/shard_map/ppermute | solution.py:22
  47.9 9.4 %collective-permute-start.13 = (bf16[8,32,128]{2,1,0:T(8,128)(2,1)S(1)}, bf16[8,32,128]{2,1,0:T(8,128)(2,1)S(1)}, u32[]{:S(2)}, u32[]{:S(2)}) collective-permute-start(bf16[8,32,128]{2,1,0:T(8,128)(2,1)S(1)} %add_convert_fusion.refs_0_), channel_id=1, source_target_pairs={{0,12},{4,8},{8,4},{12,0},{1,13},{5,9},{9,5},{13,1},{2,14},{6,10},... | collective-permute-start | bytes 196616 | tf_op jit(solution)/shard_map/ppermute | solution.py:22
  49.2 9.2 %collective-permute-start.12 = (bf16[8,32,128]{2,1,0:T(8,128)(2,1)S(1)}, bf16[8,32,128]{2,1,0:T(8,128)(2,1)S(1)}, u32[]{:S(2)}, u32[]{:S(2)}) collective-permute-start(bf16[8,32,128]{2,1,0:T(8,128)(2,1)S(1)} %add_convert_fusion.refs_0_), channel_id=1, source_target_pairs={{0,8},{4,12},{8,0},{12,4},{1,9},{5,13},{9,1},{13,5},{2,10},{6,14},... | collective-permute-start | bytes 196616 | tf_op jit(solution)/shard_map/ppermute | solution.py:22
  50.5 8.0 %collective-permute-start.11 = (bf16[8,32,128]{2,1,0:T(8,128)(2,1)S(1)}, bf16[8,32,128]{2,1,0:T(8,128)(2,1)S(1)}, u32[]{:S(2)}, u32[]{:S(2)}) collective-permute-start(bf16[8,32,128]{2,1,0:T(8,128)(2,1)S(1)} %add_convert_fusion.refs_0_), channel_id=1, source_target_pairs={{0,4},{4,0},{8,12},{12,8},{1,5},{5,1},{9,13},{13,9},{2,6},{6,2},{1... | collective-permute-start | bytes 196616 | tf_op jit(solution)/shard_map/ppermute | solution.py:22
  52.4 9.3 %collective-permute-start.16 = (bf16[32,32,128]{2,1,0:T(8,128)(2,1)S(1)}, bf16[32,32,128]{2,1,0:T(8,128)(2,1)S(1)}, u32[]{:S(2)}, u32[]{:S(2)}) collective-permute-start(bf16[32,32,128]{2,1,0:T(8,128)(2,1)S(1)} %collective-permute-done.15.same_ref), channel_id=1, source_target_pairs={{0,2},{2,0},{1,3},{3,1},{4,6},{6,4},{5,7},{7,5},{8,10},{10,8},{9,1... | collective-permute-start | bytes 786440 | tf_op jit(solution)/shard_map/ppermute | solution.py:22
  58.5 8.7 %collective-permute-start.14 = (bf16[32,32,128]{2,1,0:T(8,128)(2,1)S(1)}, bf16[32,32,128]{2,1,0:T(8,128)(2,1)S(1)}, u32[]{:S(2)}, u32[]{:S(2)}) collective-permute-start(bf16[32,32,128]{2,1,0:T(8,128)(2,1)S(1)} %collective-permute-done.9.same_ref), channel_id=1, source_target_pairs={{0,2},{2,0},{1,3},{3,1},{4,6},{6,4},{5,7},{7,5},{8,10},{10,8},{9,1... | collective-permute-start | bytes 786440 | tf_op jit(solution)/shard_map/ppermute | solution.py:22
  61.5 5.7 %collective-permute-start.17 = (bf16[16,32,128]{2,1,0:T(8,128)(2,1)S(1)}, bf16[16,32,128]{2,1,0:T(8,128)(2,1)S(1)}, u32[]{:S(2)}, u32[]{:S(2)}) collective-permute-start(bf16[16,32,128]{2,1,0:T(8,128)(2,1)S(1)} %get-tuple-element.57), channel_id=1, source_target_pairs={{0,2},{2,0},{1,3},{3,1},{4,6},{6,4},{5,7},{7,5},{8,10},{10,8},{9,1... | collective-permute-start | bytes 393224 | tf_op jit(solution)/shard_map/ppermute | solution.py:22

commit v5 on v4

--- a/solution.py
+++ b/solution.py
@@ -72,9 +72,9 @@
     put_projection(mine_ref, basis_ref, keep_ref, send_ref, 0, parts)
 
 
-def put_sorted(words_ref, kinds, nothing, plan_ref):
-    count, width = words_ref.shape[1], plan_ref.shape[1]
-    across = jnp.broadcast_to(words_ref[...], (count, count))
+def put_sorted(words, kinds, nothing, plan_ref):
+    count, width = words.shape[1], plan_ref.shape[1]
+    across = jnp.broadcast_to(words, (count, count))
     down = across.T
     kind_across, kind_down = lax.shift_right_logical(across, 3 * FIELD), lax.shift_right_logical(down, 3 * FIELD)
     t = lax.broadcasted_iota(jnp.int32, (count, count), 1)
@@ -93,34 +93,58 @@
     plan_ref[kinds : kinds + 1] = totals
 
 
-def plan_kernel(nothing, near_ref, far_ref, near_plan_ref, far_plan_ref, near_plan, far_plan, sent):
-    put_sorted(near_ref, 3, nothing, near_plan)
-    put_sorted(far_ref, 2, nothing, far_plan)
-    near_copy = pltpu.make_async_copy(near_plan, near_plan_ref, sent.at[0])
-    far_copy = pltpu.make_async_copy(far_plan, far_plan_ref, sent.at[1])
-    near_copy.start()
-    far_copy.start()
-    near_copy.wait()
-    far_copy.wait()
-
-
-def prepare_kernel(far_plan_ref, blocks_hbm, coupling_hbm, blocks_ref, pairs_ref, coupling, turned, arrived):
-    pieces = arrived.shape[0] - 1
-    size = blocks_ref.shape[0] // pieces
-    first = pltpu.make_async_copy(coupling_hbm, coupling, arrived.at[pieces])
-    first.start()
-    copies = [
-        pltpu.make_async_copy(
-            blocks_hbm.at[pl.ds(i * size, size)], blocks_ref.at[pl.ds(i * size, size)], arrived.at[i]
-        )
-        for i in range(pieces)
+def put_plans(clusters, near_ref, far_ref, near_plan, far_plan):
+    here, basis = lax.axis_index("blk"), lax.axis_index("basis")
+    bits, half = clusters.bit_length() - 1, clusters // 2
+    rows, columns = near_ref[0:1], near_ref[1:2]
+    entry = lax.broadcasted_iota(jnp.int32, rows.shape, 1)
+    owner = lax.shift_right_logical(columns, bits)
+    kind = jnp.where(owner == here, 0, jnp.where(owner == (here ^ 1), 2, 1))
+    words = ((kind << FIELD | entry) << FIELD | (rows - here * clusters)) << FIELD | (columns & (clusters - 1))
+    put_sorted(words, 3, clusters << FIELD, near_plan)
+    rows, columns = far_ref[0:1], far_ref[1:2]
+    entry = lax.broadcasted_iota(jnp.int32, rows.shape, 1)
+    owner, source = lax.shift_right_logical(columns, bits), columns & (clusters - 1)
+    kind = jnp.where(lax.shift_right_logical(source, bits - 1) == basis, 0, 1)
+    place = (owner ^ here) * half + (source & (half - 1))
+    words = ((kind << FIELD | entry) << FIELD | (rows - here * clusters)) << FIELD | place
+    put_sorted(words, 2, clusters << FIELD, far_plan)
+
+
+def prepare_kernel(clusters, near_hbm, far_hbm, blocks_hbm, coupling_hbm, *refs):
+    near_plan_ref, far_plan_ref, blocks_ref, pairs_ref, coupling, turned, near_plan, far_plan, lists, arrived = refs
+
+    def copies_of(source, target, pieces, first):
+        size = target.shape[0] // pieces
+        parts = [pl.ds(i * size, size) for i in range(pieces)]
+        return [
+            pltpu.make_async_copy(source.at[part], target.at[part], arrived.at[first + i])
+            for i, part in enumerate(parts)
+        ]
+
+    coupling_copies = copies_of(coupling_hbm, coupling, 4, 0)
+    block_copies = copies_of(blocks_hbm, blocks_ref, 8, 4)
+    list_copies = [
+        pltpu.make_async_copy(source, lists.at[i], arrived.at[14 + i]) for i, source in enumerate((near_hbm, far_hbm))
     ]
-    for copy in copies:
+    for copy in list_copies + coupling_copies + block_copies:
         copy.start()
-    first.wait()
+    for copy in list_copies:
+        copy.wait()
+    put_plans(clusters, lists.at[0], lists.at[1], near_plan, far_plan)
+    plan_copies = [
+        pltpu.make_async_copy(near_plan, near_plan_ref, arrived.at[12]),
+        pltpu.make_async_copy(far_plan, far_plan_ref, arrived.at[13]),
+    ]
+    for copy in plan_copies:
+        copy.start()
     rank, _, count = coupling.shape
+    for copy in coupling_copies:
+        copy.wait()
     for k in range(rank):
         turned[k * count : (k + 1) * count] = coupling[k].astype(jnp.float32).T
+    for copy in plan_copies:
+        copy.wait()
 
     def step(i, carry):
         for j in range(FAR_UNROLL):
@@ -130,7 +154,7 @@
         return carry
 
     lax.fori_loop(0, lax.div(far_plan_ref[2, 0] + FAR_UNROLL - 1, FAR_UNROLL), step, 0)
-    for copy in copies:
+    for copy in block_copies:
         copy.wait()
 
 
@@ -237,18 +261,7 @@
     panel = right_panel.transpose(0, 2, 1)
     basis = cluster_basis.transpose(0, 2, 1)
     cycle = lax.axis_size("blk")
-    place = jnp.stack([lax.axis_index("blk"), lax.axis_index("basis")]).astype(jnp.int32)
     half, quarter = clusters // 2, clusters // 4
-    near_owner, far_owner = near_list[:, 1] // clusters, far_list[:, 1] // clusters
-    words = jnp.where(near_owner == place[0], 0, jnp.where(near_owner == place[0] ^ 1, 2, 1))
-    words = words << FIELD | jnp.arange(near_count, dtype=jnp.int32)
-    words = words << FIELD | near_list[:, 0] - place[0] * clusters
-    words = words << FIELD | near_list[:, 1] % clusters
-    far_source = far_list[:, 1] % clusters
-    far_words = (far_source // half != place[1]).astype(jnp.int32)
-    far_words = far_words << FIELD | jnp.arange(far_list.shape[0], dtype=jnp.int32)
-    far_words = far_words << FIELD | far_list[:, 0] - place[0] * clusters
-    far_words = far_words << FIELD | (place[0] ^ far_owner) * half + far_source % half
     f32, bf16 = jnp.float32, jnp.bfloat16
     mine_shape = jax.ShapeDtypeStruct((clusters, columns, slab), bf16)
     keep_shape = jax.ShapeDtypeStruct((quarter, columns, 2 * rank), f32)
@@ -272,40 +285,28 @@
         cost_estimate=cost(2),
         name="start",
     )(in_hbm(panel), in_hbm(basis))
-    near_plan, far_plan = pl.pallas_call(
-        functools.partial(plan_kernel, clusters << FIELD),
+    near_plan, far_plan, blocks, pairs = pl.pallas_call(
+        functools.partial(prepare_kernel, clusters),
         out_shape=(
             pltpu.SMEM(near_plan_shape.shape, jnp.int32),
             pltpu.SMEM(far_plan_shape.shape, jnp.int32),
-        ),
-        in_specs=[VMEM, VMEM],
-        out_specs=(SMEM, SMEM),
-        scratch_shapes=[
-            pltpu.VMEM(near_plan_shape.shape, jnp.int32),
-            pltpu.VMEM(far_plan_shape.shape, jnp.int32),
-            pltpu.SemaphoreType.DMA((2,)),
-        ],
-        compiler_params=params(),
-        cost_estimate=cost(1),
-        name="plan",
-    )(words[None], far_words[None])
-    blocks, pairs = pl.pallas_call(
-        prepare_kernel,
-        out_shape=(
             pltpu.VMEM(near_field_blocks.shape, bf16),
             pltpu.VMEM((coupling.shape[0] + FAR_UNROLL, rank, rank), bf16),
         ),
-        in_specs=[SMEM, HBM, HBM],
-        out_specs=(VMEM, VMEM),
+        in_specs=[HBM] * 4,
+        out_specs=(SMEM, SMEM, VMEM, VMEM),
         scratch_shapes=[
             pltpu.VMEM((rank, rank, coupling.shape[0]), bf16),
-            pltpu.VMEM((rank * coupling.shape[0], rank), f32),
-            pltpu.SemaphoreType.DMA((9,)),
+            pltpu.VMEM(((rank + 1) * coupling.shape[0], rank), f32),
+            pltpu.VMEM(near_plan_shape.shape, jnp.int32),
+            pltpu.VMEM(far_plan_shape.shape, jnp.int32),
+            pltpu.VMEM((2, 2, near_count), jnp.int32),
+            pltpu.SemaphoreType.DMA((16,)),
         ],
         compiler_params=params(20),
         cost_estimate=cost(4),
         name="prepare",
-    )(in_smem(far_plan), in_hbm(near_field_blocks), in_hbm(coupling.transpose(1, 2, 0)))
+    )(*(in_hbm(array) for array in (near_list.T, far_list.T, near_field_blocks, coupling.transpose(1, 2, 0))))
 
     def near_own(plan, blocks):
         return pl.pallas_call(
@@ -380,8 +381,12 @@
         else:
             acc = near_own(near_plan, blocks)
         held = [(keep + received[-quarter:].astype(f32)).astype(bf16)]
-        held += [swapped(held[0], "blk", lambda i, d=d: i ^ d) for d in range(1, cycle)]
-        between, acc, *held = lax.optimization_barrier((between, acc, *held))
+        got = {0: held[0]}
+        for d in reversed([1 << i for i in range(cycle.bit_length() - 1)]):
+            for e in list(got):
+                got[e ^ d] = swapped(got[e], "blk", lambda i, d=d: i ^ d)
+        held = [got[d] for d in range(cycle)]
+        between, acc, held[1], held[2] = lax.optimization_barrier((between, acc, held[1], held[2]))
         paired_other = other_basis(paired)
         between_other = other_basis(between)
         far_sum, far_send = far(far_plan, held)
@@ -457,6 +462,8 @@
 def on_device(right_panel, near_field_blocks, near_list, cluster_basis, coupling, far_list):
     cycle = lax.axis_size("blk")
     tiled = lax.axis_size("basis") == 2 and cluster_basis.shape[1] % 128 == 0 and cycle & (cycle - 1) == 0
+    clusters = right_panel.shape[0]
+    tiled = tiled and clusters & (clusters - 1) == 0
     run = tiled_on_device if tiled else general_on_device
     return run(right_panel, near_field_blocks, near_list, cluster_basis, coupling, far_list)
 

time: 70 us -> 69.4 us (level)
  other arithmetic: 0.82 us -> 0.03 us
    pallas_call x2, Pallas kernels: 5.16 us -> 6.09 us  [finish(): pl.pallas_call(finish_kernel, out_shape=outs, in_specs=[SMEM] + [VMEM] *...]
    pallas_call x2 -> x1, Pallas kernels: 6.27 us -> 5.35 us  [tiled_on_device(): pl.pallas_call(functools.partial(prepare_kernel, clusters), out_shape=(pl...]
    or x1 -> x0, other arithmetic: 0.78 us -> none  [tiled_on_device(): words = words << FIELD | near_list[:, 1] % clusters]
  transfers between devices with their start and end apart: 18 -> 18, of which waited for: 9 -> 10; matrix products, arithmetic and copies ran while one was open for 1% -> 0% of each run, Pallas kernels for 22% -> 21%
where the time goes in v5:
time: 69.4 us; the launch traced here: 68.9 us
  starting transfers between devices  24.3 us (35%)
  Pallas kernels  22.4 us (32%)
  waiting for transfers between devices  21.3 us (31%)
  between operations  0.76 us (1%)
    ppermute x18, starting transfers between devices, swapped(): lax.ppermute(array, axis, [(i, partner(i)) for i in range(lax.axis_size(a...  24.3 us
    ppermute x18, waiting for transfers between devices, swapped(): lax.ppermute(array, axis, [(i, partner(i)) for i in range(lax.axis_size(a...  21.3 us
    pallas_call x2, Pallas kernels, finish(): pl.pallas_call(finish_kernel, out_shape=outs, in_specs=[SMEM] + [VMEM] *...  6.09 us
    pallas_call x1, Pallas kernels, tiled_on_device(): pl.pallas_call(functools.partial(prepare_kernel, clusters), out_shape=(pl...  5.35 us
    pallas_call x3, Pallas kernels, near_halves(): pl.pallas_call(functools.partial(near_halves_kernel, kind), out_shape=acc...  4.55 us
    pallas_call x2, Pallas kernels, far(): pl.pallas_call(far_kernel, out_shape=(jax.ShapeDtypeStruct((clusters, col...  2.98 us
    pallas_call x1, Pallas kernels, tiled_on_device(): pl.pallas_call(start_kernel, out_shape=(mine_shape, jax.ShapeDtypeStruct(...  1.9 us
    pallas_call x1, Pallas kernels, near_own(): pl.pallas_call(near_own_kernel, out_shape=acc_shape, in_specs=[SMEM, HBM,...  1.56 us
  transfers between devices with their start and end apart: 18, of which 10 were waited for; matrix products, arithmetic and copies ran while one was open for 0% of the time, Pallas kernels for 21%

profile of v5, /device:TPU:0, one launch (start us, length us, event | category | flops | bytes accessed | tf_op | source)
XLA Modules:
  0.0 68.9 jit_solution(9000210750466125449)
XLA Ops:
  0.6 1.9 %start.1 = (bf16[32,32,128]{2,1,0:T(8,128)(2,1)S(1)}, bf16[32,64,128]{2,1,0:T(8,128)(2,1)S(1)}, f32[8,32,128]{2,1,0:T(8,128)S(1)}, bf16[8,32,128]{2,1,0:T(8,128)(2,1)S(1)}) custom-call(f32[32,32,256]{2,1,0:T(8,128)} %bitcast.7, bf16[32,64,128]{2,1,0:T(8,128)(2,1)} %bitcast.10), custom_call_target="tpu_custom_call" | custom-call | bytes 7380000 | tf_op jit(solution)/shard_map/start/pallas_call | solution.py:278
  2.6 3.0 %collective-permute-start.1 = (bf16[8,32,128]{2,1,0:T(8,128)(2,1)S(1)}, bf16[8,32,128]{2,1,0:T(8,128)(2,1)S(1)}, u32[]{:S(2)}, u32[]{:S(2)}) collective-permute-start(bf16[8,32,128]{2,1,0:T(8,128)(2,1)S(1)} %get-tuple-element.30), channel_id=1, source_target_pairs={{0,2},{2,0},{1,3},{3,1},{4,6},{6,4},{5,7},{7,5},{8,10},{10,8},{9,1... | collective-permute-start | bytes 196616 | tf_op jit(solution)/shard_map/ppermute | solution.py:22
  5.6 3.6 %collective-permute-start.5 = (bf16[32,32,128]{2,1,0:T(8,128)(2,1)S(1)}, bf16[32,32,128]{2,1,0:T(8,128)(2,1)S(1)}, u32[]{:S(2)}, u32[]{:S(2)}) collective-permute-start(bf16[32,32,128]{2,1,0:T(8,128)(2,1)S(1)} %get-tuple-element.27), channel_id=1, source_target_pairs={{0,12},{4,8},{8,4},{12,0},{1,13},{5,9},{9,5},{13,1},{2,14},{6,10},... | collective-permute-start | bytes 786440 | tf_op jit(solution)/shard_map/ppermute | solution.py:22
  9.2 1.8 %collective-permute-start.3 = (bf16[8,32,128]{2,1,0:T(8,128)(2,1)S(1)}, bf16[8,32,128]{2,1,0:T(8,128)(2,1)S(1)}, u32[]{:S(2)}, u32[]{:S(2)}) collective-permute-start(bf16[8,32,128]{2,1,0:T(8,128)(2,1)S(1)} %add_convert_fusion.1.refs_0_), channel_id=1, source_target_pairs={{0,8},{4,12},{8,0},{12,4},{1,9},{5,13},{9,1},{13,5},{2,10},{6,14},... | collective-permute-start | bytes 196616 | tf_op jit(solution)/shard_map/ppermute | solution.py:22
  11.0 1.6 %collective-permute-start.2 = (bf16[8,32,128]{2,1,0:T(8,128)(2,1)S(1)}, bf16[8,32,128]{2,1,0:T(8,128)(2,1)S(1)}, u32[]{:S(2)}, u32[]{:S(2)}) collective-permute-start(bf16[8,32,128]{2,1,0:T(8,128)(2,1)S(1)} %add_convert_fusion.1.refs_0_), channel_id=1, source_target_pairs={{0,4},{4,0},{8,12},{12,8},{1,5},{5,1},{9,13},{13,9},{2,6},{6,2},{1... | collective-permute-start | bytes 196616 | tf_op jit(solution)/shard_map/ppermute | solution.py:22
  12.6 5.4 %prepare.1 = (s32[4,144]{1,0:T(4,128)S(4)}, s32[3,160]{1,0:T(4,128)S(4)}, bf16[128,128,256]{2,1,0:T(8,128)(2,1)S(1)}, bf16[160,64,64]{2,1,0:T(8,128)(2,1)S(1)}) custom-call(s32[2,128]{1,0:T(2,128)} %bitcast.12, s32[2,128]{1,0:T(2,128)} %bitcast.13, bf16[128,128,256]{2,1,0:T(8,128)(2,1)} %blocks_hbm.1, bf16[64,64,128]{2,1,0:T(8,128)(2,1)} %bitcast.9), custom_call_target="tpu_custom_call" | custom-call | bytes 14760000 | tf_op jit(solution)/shard_map/prepare/pallas_call | solution.py:288
  18.0 1.6 %near_own.1.refs_0_ = f32[33,32,128]{2,1,0:T(8,128)S(1)} custom-call(s32[4,144]{1,0:T(4,128)S(4)} %get-tuple-element.26.plan_ref, f32[32,32,256]{2,1,0:T(8,128)S(1)} %bitcast.8, bf16[128,128,256]{2,1,0:T(8,128)(2,1)S(1)} %get-tuple-element.28.blocks_ref), custom_call_target="tpu_custom_call" | custom-call | bytes 11070000 | tf_op jit(solution)/shard_map/near_own/pallas_call | solution.py:312
  20.0 2.2 %collective-permute-done.3.refs_2_ = bf16[8,32,128]{2,1,0:T(8,128)(2,1)S(1)} collective-permute-done((bf16[8,32,128]{2,1,0:T(8,128)(2,1)S(1)}, bf16[8,32,128]{2,1,0:T(8,128)(2,1)S(1)}, u32[]{:S(2)}, u32[]{:S(2)}) %collective-permute-start.3) | collective-permute-done | bytes 65568 | tf_op jit(solution)/shard_map/ppermute | solution.py:22
  22.2 1.5 %collective-permute-done.2.refs_1_ = bf16[8,32,128]{2,1,0:T(8,128)(2,1)S(1)} collective-permute-done((bf16[8,32,128]{2,1,0:T(8,128)(2,1)S(1)}, bf16[8,32,128]{2,1,0:T(8,128)(2,1)S(1)}, u32[]{:S(2)}, u32[]{:S(2)}) %collective-permute-start.2) | collective-permute-done | bytes 65568 | tf_op jit(solution)/shard_map/ppermute | solution.py:22
  24.2 1.7 %collective-permute-start.7 = (bf16[8,32,128]{2,1,0:T(8,128)(2,1)S(1)}, bf16[8,32,128]{2,1,0:T(8,128)(2,1)S(1)}, u32[]{:S(2)}, u32[]{:S(2)}) collective-permute-start(bf16[8,32,128]{2,1,0:T(8,128)(2,1)S(1)} %collective-permute-done.3.refs_2_), channel_id=1, source_target_pairs={{0,4},{4,0},{8,12},{12,8},{1,5},{5,1},{9,13},{13,9},{2,6},{6,2},{1... | collective-permute-start | bytes 196616 | tf_op jit(solution)/shard_map/ppermute | solution.py:22
  25.9 2.6 %collective-permute-done.7.refs_3_ = bf16[8,32,128]{2,1,0:T(8,128)(2,1)S(1)} collective-permute-done((bf16[8,32,128]{2,1,0:T(8,128)(2,1)S(1)}, bf16[8,32,128]{2,1,0:T(8,128)(2,1)S(1)}, u32[]{:S(2)}, u32[]{:S(2)}) %collective-permute-start.7) | collective-permute-done | bytes 65568 | tf_op jit(solution)/shard_map/ppermute | solution.py:22
  28.5 1.5 %far.2 = (f32[32,32,64]{2,1,0:T(8,128)S(1)}, bf16[16,32,128]{2,1,0:T(8,128)(2,1)S(1)}) custom-call(s32[3,160]{1,0:T(4,128)S(4)} %get-tuple-element.33.plan_ref, bf16[160,64,64]{2,1,0:T(8,128)(2,1)S(1)} %get-tuple-element.34.pairs_ref, bf16[8,32,128]{2,1,0:T(8,128)(2,1)S(1)} %add_convert_fusion.1.refs_0_, ...), custom_call_target="tpu_custom_call" | custom-call | bytes 11070000 | tf_op jit(solution)/shard_map/far/pallas_call | solution.py:340
  30.0 1.2 %collective-permute-start.8 = (bf16[16,32,128]{2,1,0:T(8,128)(2,1)S(1)}, bf16[16,32,128]{2,1,0:T(8,128)(2,1)S(1)}, u32[]{:S(2)}, u32[]{:S(2)}) collective-permute-start(bf16[16,32,128]{2,1,0:T(8,128)(2,1)S(1)} %get-tuple-element.38), channel_id=1, source_target_pairs={{0,2},{2,0},{1,3},{3,1},{4,6},{6,4},{5,7},{7,5},{8,10},{10,8},{9,1... | collective-permute-start | bytes 393224 | tf_op jit(solution)/shard_map/ppermute | solution.py:22
  31.2 1.5 %near_halves.3.acc_in = f32[33,32,128]{2,1,0:T(8,128)S(1)} custom-call(s32[4,144]{1,0:T(4,128)S(4)} %get-tuple-element.26.plan_ref, bf16[32,32,128]{2,1,0:T(8,128)(2,1)S(1)} %collective-permute-done.5.same_ref, bf16[32,32,128]{2,1,0:T(8,128)(2,1)S(1)} %collective-permute-done.6.other_ref, bf16[128,128,256]{2,1,0:T(8,128)(2,1)S(1)} %get-tuple-element.28.blocks_ref, ...), custom_call_target="tpu_custom_call" | custom-call | bytes 7380000 | tf_op jit(solution)/shard_map/near_halves/pallas_call | solution.py:328
  32.7 2.3 %collective-permute-done.8.far_other_ref = bf16[16,32,128]{2,1,0:T(8,128)(2,1)S(1)} collective-permute-done((bf16[16,32,128]{2,1,0:T(8,128)(2,1)S(1)}, bf16[16,32,128]{2,1,0:T(8,128)(2,1)S(1)}, u32[]{:S(2)}, u32[]{:S(2)}) %collective-permute-start.8) | collective-permute-done | bytes 131104 | tf_op jit(solution)/shard_map/ppermute | solution.py:22
  35.0 3.1 %finish.2 = (f32[32,32,128]{2,1,0:T(8,128)}, bf16[32,32,128]{2,1,0:T(8,128)(2,1)S(1)}, f32[8,32,128]{2,1,0:T(8,128)S(1)}, bf16[40,32,128]{2,1,0:T(8,128)(2,1)S(1)}) custom-call(s32[4,144]{1,0:T(4,128)S(4)} %get-tuple-element.26.plan_ref, bf16[32,32,128]{2,1,0:T(8,128)(2,1)S(1)} %collective-permute-done.same_ref, ...), custom_call_target="tpu_custom_call" | custom-call | bytes 14760000 | tf_op jit(solution)/shard_map/finish/pallas_call | solution.py:359
  38.2 1.2 %collective-permute-start.10 = (bf16[40,32,128]{2,1,0:T(8,128)(2,1)S(1)}, bf16[40,32,128]{2,1,0:T(8,128)(2,1)S(1)}, u32[]{:S(2)}, u32[]{:S(2)}) collective-permute-start(bf16[40,32,128]{2,1,0:T(8,128)(2,1)S(1)} %get-tuple-element.42), channel_id=1, source_target_pairs={{0,2},{2,0},{1,3},{3,1},{4,6},{6,4},{5,7},{7,5},{8,10},{10,8},{9,1... | collective-permute-start | bytes 983048 | tf_op jit(solution)/shard_map/ppermute | solution.py:22
  39.3 1.2 %collective-permute-start.14 = (bf16[32,32,128]{2,1,0:T(8,128)(2,1)S(1)}, bf16[32,32,128]{2,1,0:T(8,128)(2,1)S(1)}, u32[]{:S(2)}, u32[]{:S(2)}) collective-permute-start(bf16[32,32,128]{2,1,0:T(8,128)(2,1)S(1)} %get-tuple-element.41.same_ref), channel_id=1, source_target_pairs={{0,12},{4,8},{8,4},{12,0},{1,13},{5,9},{9,5},{13,1},{2,14},{6,10},... | collective-permute-start | bytes 786440 | tf_op jit(solution)/shard_map/ppermute | solution.py:22
  40.5 1.2 %collective-permute-start.9 = (bf16[32,32,128]{2,1,0:T(8,128)(2,1)S(1)}, bf16[32,32,128]{2,1,0:T(8,128)(2,1)S(1)}, u32[]{:S(2)}, u32[]{:S(2)}) collective-permute-start(bf16[32,32,128]{2,1,0:T(8,128)(2,1)S(1)} %get-tuple-element.41.same_ref), channel_id=1, source_target_pairs={{0,4},{4,0},{8,12},{12,8},{1,5},{5,1},{9,13},{13,9},{2,6},{6,2},{1... | collective-permute-start | bytes 786440 | tf_op jit(solution)/shard_map/ppermute | solution.py:22
  41.7 4.3 %collective-permute-done.10.other_ref = bf16[40,32,128]{2,1,0:T(8,128)(2,1)S(1)} collective-permute-done((bf16[40,32,128]{2,1,0:T(8,128)(2,1)S(1)}, bf16[40,32,128]{2,1,0:T(8,128)(2,1)S(1)}, u32[]{:S(2)}, u32[]{:S(2)}) %collective-permute-start.10) | collective-permute-done | bytes 327712 | tf_op jit(solution)/shard_map/ppermute | solution.py:22
  46.0 1.0 %collective-permute-start.12 = (bf16[8,32,128]{2,1,0:T(8,128)(2,1)S(1)}, bf16[8,32,128]{2,1,0:T(8,128)(2,1)S(1)}, u32[]{:S(2)}, u32[]{:S(2)}) collective-permute-start(bf16[8,32,128]{2,1,0:T(8,128)(2,1)S(1)} %add_convert_fusion.refs_0_), channel_id=1, source_target_pairs={{0,8},{4,12},{8,0},{12,4},{1,9},{5,13},{9,1},{13,5},{2,10},{6,14},... | collective-permute-start | bytes 196616 | tf_op jit(solution)/shard_map/ppermute | solution.py:22
  47.8 2.8 %collective-permute-done.14.same_ref = bf16[32,32,128]{2,1,0:T(8,128)(2,1)S(1)} collective-permute-done((bf16[32,32,128]{2,1,0:T(8,128)(2,1)S(1)}, bf16[32,32,128]{2,1,0:T(8,128)(2,1)S(1)}, u32[]{:S(2)}, u32[]{:S(2)}) %collective-permute-start.14) | collective-permute-done | bytes 262176 | tf_op jit(solution)/shard_map/ppermute | solution.py:22
  50.6 0.8 %collective-permute-start.15 = (bf16[32,32,128]{2,1,0:T(8,128)(2,1)S(1)}, bf16[32,32,128]{2,1,0:T(8,128)(2,1)S(1)}, u32[]{:S(2)}, u32[]{:S(2)}) collective-permute-start(bf16[32,32,128]{2,1,0:T(8,128)(2,1)S(1)} %collective-permute-done.14.same_ref), channel_id=1, source_target_pairs={{0,2},{2,0},{1,3},{3,1},{4,6},{6,4},{5,7},{7,5},{8,10},{10,8},{9,1... | collective-permute-start | bytes 786440 | tf_op jit(solution)/shard_map/ppermute | solution.py:22
  51.4 1.5 %near_halves.4.refs_0_ = f32[33,32,128]{2,1,0:T(8,128)S(1)} custom-call(s32[4,144]{1,0:T(4,128)S(4)} %get-tuple-element.26.plan_ref, bf16[32,32,128]{2,1,0:T(8,128)(2,1)S(1)} %get-tuple-element.41.same_ref, bf16[40,32,128]{2,1,0:T(8,128)(2,1)S(1)} %collective-permute-done.10.other_ref, bf16[128,128,256]{2,1,0:T(8,128)(2,1)S(1)} %get-tuple-element.28.blocks_ref), custom_call_target="tpu_custom_call" | custom-call | bytes 7380000 | tf_op jit(solution)/shard_map/near_halves/pallas_call | solution.py:328
  53.8 1.3 %collective-permute-start.13 = (bf16[32,32,128]{2,1,0:T(8,128)(2,1)S(1)}, bf16[32,32,128]{2,1,0:T(8,128)(2,1)S(1)}, u32[]{:S(2)}, u32[]{:S(2)}) collective-permute-start(bf16[32,32,128]{2,1,0:T(8,128)(2,1)S(1)} %collective-permute-done.9.same_ref), channel_id=1, source_target_pairs={{0,2},{2,0},{1,3},{3,1},{4,6},{6,4},{5,7},{7,5},{8,10},{10,8},{9,1... | collective-permute-start | bytes 786440 | tf_op jit(solution)/shard_map/ppermute | solution.py:22
  55.1 1.9 %collective-permute-start.16 = (bf16[8,32,128]{2,1,0:T(8,128)(2,1)S(1)}, bf16[8,32,128]{2,1,0:T(8,128)(2,1)S(1)}, u32[]{:S(2)}, u32[]{:S(2)}) collective-permute-start(bf16[8,32,128]{2,1,0:T(8,128)(2,1)S(1)} %collective-permute-done.12.refs_2_), channel_id=1, source_target_pairs={{0,4},{4,0},{8,12},{12,8},{1,5},{5,1},{9,13},{13,9},{2,6},{6,2},{1... | collective-permute-start | bytes 196616 | tf_op jit(solution)/shard_map/ppermute | solution.py:22
  57.0 2.4 %collective-permute-done.16.refs_3_ = bf16[8,32,128]{2,1,0:T(8,128)(2,1)S(1)} collective-permute-done((bf16[8,32,128]{2,1,0:T(8,128)(2,1)S(1)}, bf16[8,32,128]{2,1,0:T(8,128)(2,1)S(1)}, u32[]{:S(2)}, u32[]{:S(2)}) %collective-permute-start.16) | collective-permute-done | bytes 65568 | tf_op jit(solution)/shard_map/ppermute | solution.py:22
  59.4 1.5 %far.3 = (f32[32,32,64]{2,1,0:T(8,128)S(1)}, bf16[16,32,128]{2,1,0:T(8,128)(2,1)S(1)}) custom-call(s32[3,160]{1,0:T(4,128)S(4)} %get-tuple-element.33.plan_ref, bf16[160,64,64]{2,1,0:T(8,128)(2,1)S(1)} %get-tuple-element.34.pairs_ref, bf16[8,32,128]{2,1,0:T(8,128)(2,1)S(1)} %add_convert_fusion.refs_0_, ...), custom_call_target="tpu_custom_call" | custom-call | bytes 11070000 | tf_op jit(solution)/shard_map/far/pallas_call | solution.py:340
  60.9 1.1 %collective-permute-start.17 = (bf16[16,32,128]{2,1,0:T(8,128)(2,1)S(1)}, bf16[16,32,128]{2,1,0:T(8,128)(2,1)S(1)}, u32[]{:S(2)}, u32[]{:S(2)}) collective-permute-start(bf16[16,32,128]{2,1,0:T(8,128)(2,1)S(1)} %get-tuple-element.49), channel_id=1, source_target_pairs={{0,2},{2,0},{1,3},{3,1},{4,6},{6,4},{5,7},{7,5},{8,10},{10,8},{9,1... | collective-permute-start | bytes 393224 | tf_op jit(solution)/shard_map/ppermute | solution.py:22
  62.0 1.5 %near_halves.5.acc_in = f32[33,32,128]{2,1,0:T(8,128)S(1)} custom-call(s32[4,144]{1,0:T(4,128)S(4)} %get-tuple-element.26.plan_ref, bf16[32,32,128]{2,1,0:T(8,128)(2,1)S(1)} %collective-permute-done.14.same_ref, bf16[32,32,128]{2,1,0:T(8,128)(2,1)S(1)} %collective-permute-done.15.other_ref, bf16[128,128,256]{2,1,0:T(8,128)(2,1)S(1)} %get-tuple-element.28.blocks_ref, ...), custom_call_target="tpu_custom_call" | custom-call | bytes 7380000 | tf_op jit(solution)/shard_map/near_halves/pallas_call | solution.py:328
  63.5 2.4 %collective-permute-done.17.far_other_ref = bf16[16,32,128]{2,1,0:T(8,128)(2,1)S(1)} collective-permute-done((bf16[16,32,128]{2,1,0:T(8,128)(2,1)S(1)}, bf16[16,32,128]{2,1,0:T(8,128)(2,1)S(1)}, u32[]{:S(2)}, u32[]{:S(2)}) %collective-permute-start.17) | collective-permute-done | bytes 131104 | tf_op jit(solution)/shard_map/ppermute | solution.py:22
  65.9 3.0 %finish.3 = f32[32,32,128]{2,1,0:T(8,128)} custom-call(s32[4,144]{1,0:T(4,128)S(4)} %get-tuple-element.26.plan_ref, bf16[32,32,128]{2,1,0:T(8,128)(2,1)S(1)} %collective-permute-done.9.same_ref, bf16[32,32,128]{2,1,0:T(8,128)(2,1)S(1)} %collective-permute-done.13.other_ref, bf16[128,128,256]{2,1,0:T(8,128)(2,1)S(1)} %get-tuple-element.28.blocks_ref, ...), custom_call_target="tpu_custom_call" | custom-call | bytes 14760000 | tf_op jit(solution)/shard_map/finish/pallas_call | solution.py:359
  (18 shorter events, 2.7 us)
Async XLA Ops:
  0.6 17.3 %copy-start = (f32[32,256,32]{1,2,0:T(8,128)S(1)}, f32[32,256,32]{1,2,0:T(8,128)}, u32[]{:S(2)}) copy-start(f32[32,256,32]{1,2,0:T(8,128)} %param.6) | copy-start | bytes 3145732
  2.6 6.6 %collective-permute-start.1 = (bf16[8,32,128]{2,1,0:T(8,128)(2,1)S(1)}, bf16[8,32,128]{2,1,0:T(8,128)(2,1)S(1)}, u32[]{:S(2)}, u32[]{:S(2)}) collective-permute-start(bf16[8,32,128]{2,1,0:T(8,128)(2,1)S(1)} %get-tuple-element.30), channel_id=1, source_target_pairs={{0,2},{2,0},{1,3},{3,1},{4,6},{6,4},{5,7},{7,5},{8,10},{10,8},{9,1... | collective-permute-start | bytes 196616 | tf_op jit(solution)/shard_map/ppermute | solution.py:22
  5.6 14.0 %collective-permute-start.5 = (bf16[32,32,128]{2,1,0:T(8,128)(2,1)S(1)}, bf16[32,32,128]{2,1,0:T(8,128)(2,1)S(1)}, u32[]{:S(2)}, u32[]{:S(2)}) collective-permute-start(bf16[32,32,128]{2,1,0:T(8,128)(2,1)S(1)} %get-tuple-element.27), channel_id=1, source_target_pairs={{0,12},{4,8},{8,4},{12,0},{1,13},{5,9},{9,5},{13,1},{2,14},{6,10},... | collective-permute-start | bytes 786440 | tf_op jit(solution)/shard_map/ppermute | solution.py:22
  9.2 14.6 %collective-permute-start = (bf16[32,32,128]{2,1,0:T(8,128)(2,1)S(1)}, bf16[32,32,128]{2,1,0:T(8,128)(2,1)S(1)}, u32[]{:S(2)}, u32[]{:S(2)}) collective-permute-start(bf16[32,32,128]{2,1,0:T(8,128)(2,1)S(1)} %get-tuple-element.27), channel_id=1, source_target_pairs={{0,4},{4,0},{8,12},{12,8},{1,5},{5,1},{9,13},{13,9},{2,6},{6,2},{1... | collective-permute-start | bytes 786440 | tf_op jit(solution)/shard_map/ppermute | solution.py:22
  9.2 13.0 %collective-permute-start.3 = (bf16[8,32,128]{2,1,0:T(8,128)(2,1)S(1)}, bf16[8,32,128]{2,1,0:T(8,128)(2,1)S(1)}, u32[]{:S(2)}, u32[]{:S(2)}) collective-permute-start(bf16[8,32,128]{2,1,0:T(8,128)(2,1)S(1)} %add_convert_fusion.1.refs_0_), channel_id=1, source_target_pairs={{0,8},{4,12},{8,0},{12,4},{1,9},{5,13},{9,1},{13,5},{2,10},{6,14},... | collective-permute-start | bytes 196616 | tf_op jit(solution)/shard_map/ppermute | solution.py:22
  11.0 12.7 %collective-permute-start.2 = (bf16[8,32,128]{2,1,0:T(8,128)(2,1)S(1)}, bf16[8,32,128]{2,1,0:T(8,128)(2,1)S(1)}, u32[]{:S(2)}, u32[]{:S(2)}) collective-permute-start(bf16[8,32,128]{2,1,0:T(8,128)(2,1)S(1)} %add_convert_fusion.1.refs_0_), channel_id=1, source_target_pairs={{0,4},{4,0},{8,12},{12,8},{1,5},{5,1},{9,13},{13,9},{2,6},{6,2},{1... | collective-permute-start | bytes 196616 | tf_op jit(solution)/shard_map/ppermute | solution.py:22
  19.5 11.6 %collective-permute-start.6 = (bf16[32,32,128]{2,1,0:T(8,128)(2,1)S(1)}, bf16[32,32,128]{2,1,0:T(8,128)(2,1)S(1)}, u32[]{:S(2)}, u32[]{:S(2)}) collective-permute-start(bf16[32,32,128]{2,1,0:T(8,128)(2,1)S(1)} %collective-permute-done.5.same_ref), channel_id=1, source_target_pairs={{0,2},{2,0},{1,3},{3,1},{4,6},{6,4},{5,7},{7,5},{8,10},{10,8},{9,1... | collective-permute-start | bytes 786440 | tf_op jit(solution)/shard_map/ppermute | solution.py:22
  23.7 11.3 %collective-permute-start.4 = (bf16[32,32,128]{2,1,0:T(8,128)(2,1)S(1)}, bf16[32,32,128]{2,1,0:T(8,128)(2,1)S(1)}, u32[]{:S(2)}, u32[]{:S(2)}) collective-permute-start(bf16[32,32,128]{2,1,0:T(8,128)(2,1)S(1)} %collective-permute-done.same_ref), channel_id=1, source_target_pairs={{0,2},{2,0},{1,3},{3,1},{4,6},{6,4},{5,7},{7,5},{8,10},{10,8},{9,1... | collective-permute-start | bytes 786440 | tf_op jit(solution)/shard_map/ppermute | solution.py:22
  24.2 4.3 %collective-permute-start.7 = (bf16[8,32,128]{2,1,0:T(8,128)(2,1)S(1)}, bf16[8,32,128]{2,1,0:T(8,128)(2,1)S(1)}, u32[]{:S(2)}, u32[]{:S(2)}) collective-permute-start(bf16[8,32,128]{2,1,0:T(8,128)(2,1)S(1)} %collective-permute-done.3.refs_2_), channel_id=1, source_target_pairs={{0,4},{4,0},{8,12},{12,8},{1,5},{5,1},{9,13},{13,9},{2,6},{6,2},{1... | collective-permute-start | bytes 196616 | tf_op jit(solution)/shard_map/ppermute | solution.py:22
  30.0 5.0 %collective-permute-start.8 = (bf16[16,32,128]{2,1,0:T(8,128)(2,1)S(1)}, bf16[16,32,128]{2,1,0:T(8,128)(2,1)S(1)}, u32[]{:S(2)}, u32[]{:S(2)}) collective-permute-start(bf16[16,32,128]{2,1,0:T(8,128)(2,1)S(1)} %get-tuple-element.38), channel_id=1, source_target_pairs={{0,2},{2,0},{1,3},{3,1},{4,6},{6,4},{5,7},{7,5},{8,10},{10,8},{9,1... | collective-permute-start | bytes 393224 | tf_op jit(solution)/shard_map/ppermute | solution.py:22
  38.2 7.8 %collective-permute-start.10 = (bf16[40,32,128]{2,1,0:T(8,128)(2,1)S(1)}, bf16[40,32,128]{2,1,0:T(8,128)(2,1)S(1)}, u32[]{:S(2)}, u32[]{:S(2)}) collective-permute-start(bf16[40,32,128]{2,1,0:T(8,128)(2,1)S(1)} %get-tuple-element.42), channel_id=1, source_target_pairs={{0,2},{2,0},{1,3},{3,1},{4,6},{6,4},{5,7},{7,5},{8,10},{10,8},{9,1... | collective-permute-start | bytes 983048 | tf_op jit(solution)/shard_map/ppermute | solution.py:22
  39.3 11.2 %collective-permute-start.14 = (bf16[32,32,128]{2,1,0:T(8,128)(2,1)S(1)}, bf16[32,32,128]{2,1,0:T(8,128)(2,1)S(1)}, u32[]{:S(2)}, u32[]{:S(2)}) collective-permute-start(bf16[32,32,128]{2,1,0:T(8,128)(2,1)S(1)} %get-tuple-element.41.same_ref), channel_id=1, source_target_pairs={{0,12},{4,8},{8,4},{12,0},{1,13},{5,9},{9,5},{13,1},{2,14},{6,10},... | collective-permute-start | bytes 786440 | tf_op jit(solution)/shard_map/ppermute | solution.py:22
  40.5 12.4 %collective-permute-start.9 = (bf16[32,32,128]{2,1,0:T(8,128)(2,1)S(1)}, bf16[32,32,128]{2,1,0:T(8,128)(2,1)S(1)}, u32[]{:S(2)}, u32[]{:S(2)}) collective-permute-start(bf16[32,32,128]{2,1,0:T(8,128)(2,1)S(1)} %get-tuple-element.41.same_ref), channel_id=1, source_target_pairs={{0,4},{4,0},{8,12},{12,8},{1,5},{5,1},{9,13},{13,9},{2,6},{6,2},{1... | collective-permute-start | bytes 786440 | tf_op jit(solution)/shard_map/ppermute | solution.py:22
  46.0 7.6 %collective-permute-start.12 = (bf16[8,32,128]{2,1,0:T(8,128)(2,1)S(1)}, bf16[8,32,128]{2,1,0:T(8,128)(2,1)S(1)}, u32[]{:S(2)}, u32[]{:S(2)}) collective-permute-start(bf16[8,32,128]{2,1,0:T(8,128)(2,1)S(1)} %add_convert_fusion.refs_0_), channel_id=1, source_target_pairs={{0,8},{4,12},{8,0},{12,4},{1,9},{5,13},{9,1},{13,5},{2,10},{6,14},... | collective-permute-start | bytes 196616 | tf_op jit(solution)/shard_map/ppermute | solution.py:22
  47.0 6.8 %collective-permute-start.11 = (bf16[8,32,128]{2,1,0:T(8,128)(2,1)S(1)}, bf16[8,32,128]{2,1,0:T(8,128)(2,1)S(1)}, u32[]{:S(2)}, u32[]{:S(2)}) collective-permute-start(bf16[8,32,128]{2,1,0:T(8,128)(2,1)S(1)} %add_convert_fusion.refs_0_), channel_id=1, source_target_pairs={{0,4},{4,0},{8,12},{12,8},{1,5},{5,1},{9,13},{13,9},{2,6},{6,2},{1... | collective-permute-start | bytes 196616 | tf_op jit(solution)/shard_map/ppermute | solution.py:22
  50.6 11.4 %collective-permute-start.15 = (bf16[32,32,128]{2,1,0:T(8,128)(2,1)S(1)}, bf16[32,32,128]{2,1,0:T(8,128)(2,1)S(1)}, u32[]{:S(2)}, u32[]{:S(2)}) collective-permute-start(bf16[32,32,128]{2,1,0:T(8,128)(2,1)S(1)} %collective-permute-done.14.same_ref), channel_id=1, source_target_pairs={{0,2},{2,0},{1,3},{3,1},{4,6},{6,4},{5,7},{7,5},{8,10},{10,8},{9,1... | collective-permute-start | bytes 786440 | tf_op jit(solution)/shard_map/ppermute | solution.py:22
  53.8 12.1 %collective-permute-start.13 = (bf16[32,32,128]{2,1,0:T(8,128)(2,1)S(1)}, bf16[32,32,128]{2,1,0:T(8,128)(2,1)S(1)}, u32[]{:S(2)}, u32[]{:S(2)}) collective-permute-start(bf16[32,32,128]{2,1,0:T(8,128)(2,1)S(1)} %collective-permute-done.9.same_ref), channel_id=1, source_target_pairs={{0,2},{2,0},{1,3},{3,1},{4,6},{6,4},{5,7},{7,5},{8,10},{10,8},{9,1... | collective-permute-start | bytes 786440 | tf_op jit(solution)/shard_map/ppermute | solution.py:22
  55.1 4.3 %collective-permute-start.16 = (bf16[8,32,128]{2,1,0:T(8,128)(2,1)S(1)}, bf16[8,32,128]{2,1,0:T(8,128)(2,1)S(1)}, u32[]{:S(2)}, u32[]{:S(2)}) collective-permute-start(bf16[8,32,128]{2,1,0:T(8,128)(2,1)S(1)} %collective-permute-done.12.refs_2_), channel_id=1, source_target_pairs={{0,4},{4,0},{8,12},{12,8},{1,5},{5,1},{9,13},{13,9},{2,6},{6,2},{1... | collective-permute-start | bytes 196616 | tf_op jit(solution)/shard_map/ppermute | solution.py:22
  60.9 5.0 %collective-permute-start.17 = (bf16[16,32,128]{2,1,0:T(8,128)(2,1)S(1)}, bf16[16,32,128]{2,1,0:T(8,128)(2,1)S(1)}, u32[]{:S(2)}, u32[]{:S(2)}) collective-permute-start(bf16[16,32,128]{2,1,0:T(8,128)(2,1)S(1)} %get-tuple-element.49), channel_id=1, source_target_pairs={{0,2},{2,0},{1,3},{3,1},{4,6},{6,4},{5,7},{7,5},{8,10},{10,8},{9,1... | collective-permute-start | bytes 393224 | tf_op jit(solution)/shard_map/ppermute | solution.py:22

commit v6 on v5

--- a/solution.py
+++ b/solution.py
@@ -373,8 +373,8 @@
         return swapped(array, "basis", lambda i: 1 - i)
 
     def apply_operator(mine, keep, send, near_plan, last):
-        paired = swapped(mine, "blk", lambda i: (((i + 1) % cycle ^ 1) - 1) % cycle)
-        between = swapped(mine, "blk", lambda i: i ^ 1)
+        crossing = swapped(mine, "blk", lambda i: (((i + 1) % cycle ^ 1) - 1) % cycle)
+        paired = swapped(mine, "blk", lambda i: i ^ 1)
         received = other_basis(send)
         if last:
             acc = near_halves(near_plan, blocks, 0, mine, received)
@@ -386,13 +386,16 @@
             for e in list(got):
                 got[e ^ d] = swapped(got[e], "blk", lambda i, d=d: i ^ d)
         held = [got[d] for d in range(cycle)]
-        between, acc, held[1], held[2] = lax.optimization_barrier((between, acc, held[1], held[2]))
+        if last:
+            paired, acc, held[1], held[2] = lax.optimization_barrier((paired, acc, held[1], held[2]))
+        else:
+            paired, acc, held[2] = lax.optimization_barrier((paired, acc, held[2]))
+        crossing_other = other_basis(crossing)
         paired_other = other_basis(paired)
-        between_other = other_basis(between)
         far_sum, far_send = far(far_plan, held)
         far_other = other_basis(far_send)
-        acc = near_halves(near_plan, blocks, 1, paired, paired_other, acc)
-        return finish(near_plan, blocks, between, between_other, acc, far_sum, far_other, last), near_plan
+        acc = near_halves(near_plan, blocks, 1, crossing, crossing_other, acc)
+        return finish(near_plan, blocks, paired, paired_other, acc, far_sum, far_other, last), near_plan
 
     (first, mine, keep, send), near_plan = apply_operator(mine, keep, send, near_plan, False)
     (second,), _ = apply_operator(mine, keep, send, near_plan, True)
@@ -461,7 +464,8 @@
 
 def on_device(right_panel, near_field_blocks, near_list, cluster_basis, coupling, far_list):
     cycle = lax.axis_size("blk")
-    tiled = lax.axis_size("basis") == 2 and cluster_basis.shape[1] % 128 == 0 and cycle & (cycle - 1) == 0
+    tiled = lax.axis_size("basis") == 2 and cluster_basis.shape[1] % 128 == 0
+    tiled = tiled and cycle >= 4 and cycle & (cycle - 1) == 0
     clusters = right_panel.shape[0]
     tiled = tiled and clusters & (clusters - 1) == 0
     run = tiled_on_device if tiled else general_on_device

time: 69.4 us -> 69 us (level); the launches traced: 68.9 us -> 67.8 us
  starting transfers between devices: 24.3 us -> 28.6 us
  Pallas kernels: 22.4 us -> 19.6 us
  waiting for transfers between devices: 21.3 us -> 18.7 us
    ppermute x18, starting transfers between devices: 24.3 us -> 28.6 us  [swapped(): lax.ppermute(array, axis, [(i, partner(i)) for i in range(lax.axis_size(a...]
    ppermute x18, waiting for transfers between devices: 21.3 us -> 18.7 us  [swapped(): lax.ppermute(array, axis, [(i, partner(i)) for i in range(lax.axis_size(a...]
    pallas_call x1, Pallas kernels: 5.35 us -> 4.26 us  [tiled_on_device(): pl.pallas_call(functools.partial(prepare_kernel, clusters), out_shape=(pl...]
    pallas_call x2, Pallas kernels: 6.09 us -> 5.16 us  [finish(): pl.pallas_call(finish_kernel, out_shape=outs, in_specs=[SMEM] + [VMEM] *...]
    pallas_call x2, Pallas kernels: 2.98 us -> 2.19 us  [far(): pl.pallas_call(far_kernel, out_shape=(jax.ShapeDtypeStruct((clusters, col...]
  transfers between devices with their start and end apart: 18 -> 18, of which waited for: 10 -> 10; matrix products, arithmetic and copies ran while one was open for 0% -> 0% of each run, Pallas kernels for 21% -> 19%
where the time goes in v6:
time: 69 us; the launch traced here: 67.8 us
  starting transfers between devices  28.6 us (41%)
  Pallas kernels  19.6 us (28%)
  waiting for transfers between devices  18.7 us (27%)
  between operations  0.75 us (1%)
    ppermute x18, starting transfers between devices, swapped(): lax.ppermute(array, axis, [(i, partner(i)) for i in range(lax.axis_size(a...  28.6 us
    ppermute x18, waiting for transfers between devices, swapped(): lax.ppermute(array, axis, [(i, partner(i)) for i in range(lax.axis_size(a...  18.7 us
    pallas_call x2, Pallas kernels, finish(): pl.pallas_call(finish_kernel, out_shape=outs, in_specs=[SMEM] + [VMEM] *...  5.16 us
    pallas_call x3, Pallas kernels, near_halves(): pl.pallas_call(functools.partial(near_halves_kernel, kind), out_shape=acc...  4.55 us
    pallas_call x1, Pallas kernels, tiled_on_device(): pl.pallas_call(functools.partial(prepare_kernel, clusters), out_shape=(pl...  4.26 us
    pallas_call x2, Pallas kernels, far(): pl.pallas_call(far_kernel, out_shape=(jax.ShapeDtypeStruct((clusters, col...  2.19 us
    pallas_call x1, Pallas kernels, tiled_on_device(): pl.pallas_call(start_kernel, out_shape=(mine_shape, jax.ShapeDtypeStruct(...  1.9 us
    pallas_call x1, Pallas kernels, near_own(): pl.pallas_call(near_own_kernel, out_shape=acc_shape, in_specs=[SMEM, HBM,...  1.56 us
  transfers between devices with their start and end apart: 18, of which 10 were waited for; matrix products, arithmetic and copies ran while one was open for 0% of the time, Pallas kernels for 19%

profile of v6, /device:TPU:0, one launch (start us, length us, event | category | flops | bytes accessed | tf_op | source)
XLA Modules:
  0.0 67.8 jit_solution(16965903129695603327)
XLA Ops:
  0.6 1.9 %start.1 = (bf16[32,32,128]{2,1,0:T(8,128)(2,1)S(1)}, bf16[32,64,128]{2,1,0:T(8,128)(2,1)S(1)}, f32[8,32,128]{2,1,0:T(8,128)S(1)}, bf16[8,32,128]{2,1,0:T(8,128)(2,1)S(1)}) custom-call(f32[32,32,256]{2,1,0:T(8,128)} %bitcast.7, bf16[32,64,128]{2,1,0:T(8,128)(2,1)} %bitcast.10), custom_call_target="tpu_custom_call" | custom-call | bytes 7380000 | tf_op jit(solution)/shard_map/start/pallas_call | solution.py:278
  2.6 3.0 %collective-permute-start.1 = (bf16[8,32,128]{2,1,0:T(8,128)(2,1)S(1)}, bf16[8,32,128]{2,1,0:T(8,128)(2,1)S(1)}, u32[]{:S(2)}, u32[]{:S(2)}) collective-permute-start(bf16[8,32,128]{2,1,0:T(8,128)(2,1)S(1)} %get-tuple-element.29), channel_id=1, source_target_pairs={{0,2},{2,0},{1,3},{3,1},{4,6},{6,4},{5,7},{7,5},{8,10},{10,8},{9,1... | collective-permute-start | bytes 196616 | tf_op jit(solution)/shard_map/ppermute | solution.py:22
  5.6 3.6 %collective-permute-start.4 = (bf16[32,32,128]{2,1,0:T(8,128)(2,1)S(1)}, bf16[32,32,128]{2,1,0:T(8,128)(2,1)S(1)}, u32[]{:S(2)}, u32[]{:S(2)}) collective-permute-start(bf16[32,32,128]{2,1,0:T(8,128)(2,1)S(1)} %get-tuple-element.26), channel_id=1, source_target_pairs={{0,12},{4,8},{8,4},{12,0},{1,13},{5,9},{9,5},{13,1},{2,14},{6,10},... | collective-permute-start | bytes 786440 | tf_op jit(solution)/shard_map/ppermute | solution.py:22
  9.2 1.8 %collective-permute-start.2 = (bf16[8,32,128]{2,1,0:T(8,128)(2,1)S(1)}, bf16[8,32,128]{2,1,0:T(8,128)(2,1)S(1)}, u32[]{:S(2)}, u32[]{:S(2)}) collective-permute-start(bf16[8,32,128]{2,1,0:T(8,128)(2,1)S(1)} %add_convert_fusion.1.refs_0_), channel_id=1, source_target_pairs={{0,8},{4,12},{8,0},{12,4},{1,9},{5,13},{9,1},{13,5},{2,10},{6,14},... | collective-permute-start | bytes 196616 | tf_op jit(solution)/shard_map/ppermute | solution.py:22
  11.0 4.3 %prepare.1 = (s32[4,144]{1,0:T(4,128)S(4)}, s32[3,160]{1,0:T(4,128)S(4)}, bf16[128,128,256]{2,1,0:T(8,128)(2,1)S(1)}, bf16[160,64,64]{2,1,0:T(8,128)(2,1)S(1)}) custom-call(s32[2,128]{1,0:T(2,128)} %bitcast.12, s32[2,128]{1,0:T(2,128)} %bitcast.13, bf16[128,128,256]{2,1,0:T(8,128)(2,1)} %blocks_hbm.1, bf16[64,64,128]{2,1,0:T(8,128)(2,1)} %bitcast.9), custom_call_target="tpu_custom_call" | custom-call | bytes 14760000 | tf_op jit(solution)/shard_map/prepare/pallas_call | solution.py:288
  15.3 1.6 %near_own.1.refs_0_ = f32[33,32,128]{2,1,0:T(8,128)S(1)} custom-call(s32[4,144]{1,0:T(4,128)S(4)} %get-tuple-element.25.plan_ref, f32[32,32,256]{2,1,0:T(8,128)S(1)} %bitcast.8, bf16[128,128,256]{2,1,0:T(8,128)(2,1)S(1)} %get-tuple-element.27.blocks_ref), custom_call_target="tpu_custom_call" | custom-call | bytes 11070000 | tf_op jit(solution)/shard_map/near_own/pallas_call | solution.py:312
  16.9 2.6 %collective-permute-start.5 = (bf16[32,32,128]{2,1,0:T(8,128)(2,1)S(1)}, bf16[32,32,128]{2,1,0:T(8,128)(2,1)S(1)}, u32[]{:S(2)}, u32[]{:S(2)}) collective-permute-start(bf16[32,32,128]{2,1,0:T(8,128)(2,1)S(1)} %collective-permute-done.4.same_ref), channel_id=1, source_target_pairs={{0,2},{2,0},{1,3},{3,1},{4,6},{6,4},{5,7},{7,5},{8,10},{10,8},{9,1... | collective-permute-start | bytes 786440 | tf_op jit(solution)/shard_map/ppermute | solution.py:22
  19.5 3.2 %collective-permute-done.2.refs_2_ = bf16[8,32,128]{2,1,0:T(8,128)(2,1)S(1)} collective-permute-done((bf16[8,32,128]{2,1,0:T(8,128)(2,1)S(1)}, bf16[8,32,128]{2,1,0:T(8,128)(2,1)S(1)}, u32[]{:S(2)}, u32[]{:S(2)}) %collective-permute-start.2) | collective-permute-done | bytes 65568 | tf_op jit(solution)/shard_map/ppermute | solution.py:22
  23.3 0.7 collective-permute-start.6
  24.0 1.4 %collective-permute-start.7 = (bf16[8,32,128]{2,1,0:T(8,128)(2,1)S(1)}, bf16[8,32,128]{2,1,0:T(8,128)(2,1)S(1)}, u32[]{:S(2)}, u32[]{:S(2)}) collective-permute-start(bf16[8,32,128]{2,1,0:T(8,128)(2,1)S(1)} %collective-permute-done.2.refs_2_), channel_id=1, source_target_pairs={{0,4},{4,0},{8,12},{12,8},{1,5},{5,1},{9,13},{13,9},{2,6},{6,2},{1... | collective-permute-start | bytes 196616 | tf_op jit(solution)/shard_map/ppermute | solution.py:22
  25.3 2.2 %collective-permute-done.6.refs_1_ = bf16[8,32,128]{2,1,0:T(8,128)(2,1)S(1)} collective-permute-done((bf16[8,32,128]{2,1,0:T(8,128)(2,1)S(1)}, bf16[8,32,128]{2,1,0:T(8,128)(2,1)S(1)}, u32[]{:S(2)}, u32[]{:S(2)}) %collective-permute-start.6) | collective-permute-done | bytes 65568 | tf_op jit(solution)/shard_map/ppermute | solution.py:22
  27.6 0.7 %collective-permute-done.7.refs_3_ = bf16[8,32,128]{2,1,0:T(8,128)(2,1)S(1)} collective-permute-done((bf16[8,32,128]{2,1,0:T(8,128)(2,1)S(1)}, bf16[8,32,128]{2,1,0:T(8,128)(2,1)S(1)}, u32[]{:S(2)}, u32[]{:S(2)}) %collective-permute-start.7) | collective-permute-done | bytes 65568 | tf_op jit(solution)/shard_map/ppermute | solution.py:22
  28.3 1.1 %far.2 = (f32[32,32,64]{2,1,0:T(8,128)S(1)}, bf16[16,32,128]{2,1,0:T(8,128)(2,1)S(1)}) custom-call(s32[3,160]{1,0:T(4,128)S(4)} %get-tuple-element.32.plan_ref, bf16[160,64,64]{2,1,0:T(8,128)(2,1)S(1)} %get-tuple-element.33.pairs_ref, bf16[8,32,128]{2,1,0:T(8,128)(2,1)S(1)} %add_convert_fusion.1.refs_0_, ...), custom_call_target="tpu_custom_call" | custom-call | bytes 11070000 | tf_op jit(solution)/shard_map/far/pallas_call | solution.py:340
  29.4 2.0 %collective-permute-start.8 = (bf16[16,32,128]{2,1,0:T(8,128)(2,1)S(1)}, bf16[16,32,128]{2,1,0:T(8,128)(2,1)S(1)}, u32[]{:S(2)}, u32[]{:S(2)}) collective-permute-start(bf16[16,32,128]{2,1,0:T(8,128)(2,1)S(1)} %get-tuple-element.36), channel_id=1, source_target_pairs={{0,2},{2,0},{1,3},{3,1},{4,6},{6,4},{5,7},{7,5},{8,10},{10,8},{9,1... | collective-permute-start | bytes 393224 | tf_op jit(solution)/shard_map/ppermute | solution.py:22
  31.3 1.5 %near_halves.3.acc_in = f32[33,32,128]{2,1,0:T(8,128)S(1)} custom-call(s32[4,144]{1,0:T(4,128)S(4)} %get-tuple-element.25.plan_ref, bf16[32,32,128]{2,1,0:T(8,128)(2,1)S(1)} %collective-permute-done.4.same_ref, bf16[32,32,128]{2,1,0:T(8,128)(2,1)S(1)} %collective-permute-done.5.other_ref, bf16[128,128,256]{2,1,0:T(8,128)(2,1)S(1)} %get-tuple-element.27.blocks_ref, ...), custom_call_target="tpu_custom_call" | custom-call | bytes 7380000 | tf_op jit(solution)/shard_map/near_halves/pallas_call | solution.py:328
  32.9 1.5 %collective-permute-done.8.far_other_ref = bf16[16,32,128]{2,1,0:T(8,128)(2,1)S(1)} collective-permute-done((bf16[16,32,128]{2,1,0:T(8,128)(2,1)S(1)}, bf16[16,32,128]{2,1,0:T(8,128)(2,1)S(1)}, u32[]{:S(2)}, u32[]{:S(2)}) %collective-permute-start.8) | collective-permute-done | bytes 131104 | tf_op jit(solution)/shard_map/ppermute | solution.py:22
  34.4 2.7 %finish.2 = (f32[32,32,128]{2,1,0:T(8,128)}, bf16[32,32,128]{2,1,0:T(8,128)(2,1)S(1)}, f32[8,32,128]{2,1,0:T(8,128)S(1)}, bf16[40,32,128]{2,1,0:T(8,128)(2,1)S(1)}) custom-call(s32[4,144]{1,0:T(4,128)S(4)} %get-tuple-element.25.plan_ref, bf16[32,32,128]{2,1,0:T(8,128)(2,1)S(1)} %collective-permute-done.same_ref, ...), custom_call_target="tpu_custom_call" | custom-call | bytes 14760000 | tf_op jit(solution)/shard_map/finish/pallas_call | solution.py:359
  37.1 2.0 %collective-permute-start.10 = (bf16[40,32,128]{2,1,0:T(8,128)(2,1)S(1)}, bf16[40,32,128]{2,1,0:T(8,128)(2,1)S(1)}, u32[]{:S(2)}, u32[]{:S(2)}) collective-permute-start(bf16[40,32,128]{2,1,0:T(8,128)(2,1)S(1)} %get-tuple-element.40), channel_id=1, source_target_pairs={{0,2},{2,0},{1,3},{3,1},{4,6},{6,4},{5,7},{7,5},{8,10},{10,8},{9,1... | collective-permute-start | bytes 983048 | tf_op jit(solution)/shard_map/ppermute | solution.py:22
  39.0 2.5 %collective-permute-start.14 = (bf16[32,32,128]{2,1,0:T(8,128)(2,1)S(1)}, bf16[32,32,128]{2,1,0:T(8,128)(2,1)S(1)}, u32[]{:S(2)}, u32[]{:S(2)}) collective-permute-start(bf16[32,32,128]{2,1,0:T(8,128)(2,1)S(1)} %get-tuple-element.39.same_ref), channel_id=1, source_target_pairs={{0,12},{4,8},{8,4},{12,0},{1,13},{5,9},{9,5},{13,1},{2,14},{6,10},... | collective-permute-start | bytes 786440 | tf_op jit(solution)/shard_map/ppermute | solution.py:22
  41.5 2.7 %collective-permute-done.10.other_ref = bf16[40,32,128]{2,1,0:T(8,128)(2,1)S(1)} collective-permute-done((bf16[40,32,128]{2,1,0:T(8,128)(2,1)S(1)}, bf16[40,32,128]{2,1,0:T(8,128)(2,1)S(1)}, u32[]{:S(2)}, u32[]{:S(2)}) %collective-permute-start.10) | collective-permute-done | bytes 327712 | tf_op jit(solution)/shard_map/ppermute | solution.py:22
  44.2 2.3 %collective-permute-start.12 = (bf16[8,32,128]{2,1,0:T(8,128)(2,1)S(1)}, bf16[8,32,128]{2,1,0:T(8,128)(2,1)S(1)}, u32[]{:S(2)}, u32[]{:S(2)}) collective-permute-start(bf16[8,32,128]{2,1,0:T(8,128)(2,1)S(1)} %add_convert_fusion.refs_0_), channel_id=1, source_target_pairs={{0,8},{4,12},{8,0},{12,4},{1,9},{5,13},{9,1},{13,5},{2,10},{6,14},... | collective-permute-start | bytes 196616 | tf_op jit(solution)/shard_map/ppermute | solution.py:22
  46.5 1.6 %collective-permute-start.11 = (bf16[8,32,128]{2,1,0:T(8,128)(2,1)S(1)}, bf16[8,32,128]{2,1,0:T(8,128)(2,1)S(1)}, u32[]{:S(2)}, u32[]{:S(2)}) collective-permute-start(bf16[8,32,128]{2,1,0:T(8,128)(2,1)S(1)} %add_convert_fusion.refs_0_), channel_id=1, source_target_pairs={{0,4},{4,0},{8,12},{12,8},{1,5},{5,1},{9,13},{13,9},{2,6},{6,2},{1... | collective-permute-start | bytes 196616 | tf_op jit(solution)/shard_map/ppermute | solution.py:22
  48.1 1.7 %collective-permute-done.14.same_ref = bf16[32,32,128]{2,1,0:T(8,128)(2,1)S(1)} collective-permute-done((bf16[32,32,128]{2,1,0:T(8,128)(2,1)S(1)}, bf16[32,32,128]{2,1,0:T(8,128)(2,1)S(1)}, u32[]{:S(2)}, u32[]{:S(2)}) %collective-permute-start.14) | collective-permute-done | bytes 262176 | tf_op jit(solution)/shard_map/ppermute | solution.py:22
  50.0 1.5 %near_halves.4.refs_0_ = f32[33,32,128]{2,1,0:T(8,128)S(1)} custom-call(s32[4,144]{1,0:T(4,128)S(4)} %get-tuple-element.25.plan_ref, bf16[32,32,128]{2,1,0:T(8,128)(2,1)S(1)} %get-tuple-element.39.same_ref, bf16[40,32,128]{2,1,0:T(8,128)(2,1)S(1)} %collective-permute-done.10.other_ref, bf16[128,128,256]{2,1,0:T(8,128)(2,1)S(1)} %get-tuple-element.27.blocks_ref), custom_call_target="tpu_custom_call" | custom-call | bytes 7380000 | tf_op jit(solution)/shard_map/near_halves/pallas_call | solution.py:328
  52.0 2.1 %collective-permute-done.12.refs_2_ = bf16[8,32,128]{2,1,0:T(8,128)(2,1)S(1)} collective-permute-done((bf16[8,32,128]{2,1,0:T(8,128)(2,1)S(1)}, bf16[8,32,128]{2,1,0:T(8,128)(2,1)S(1)}, u32[]{:S(2)}, u32[]{:S(2)}) %collective-permute-start.12) | collective-permute-done | bytes 65568 | tf_op jit(solution)/shard_map/ppermute | solution.py:22
  54.5 2.4 %collective-permute-start.16 = (bf16[8,32,128]{2,1,0:T(8,128)(2,1)S(1)}, bf16[8,32,128]{2,1,0:T(8,128)(2,1)S(1)}, u32[]{:S(2)}, u32[]{:S(2)}) collective-permute-start(bf16[8,32,128]{2,1,0:T(8,128)(2,1)S(1)} %collective-permute-done.12.refs_2_), channel_id=1, source_target_pairs={{0,4},{4,0},{8,12},{12,8},{1,5},{5,1},{9,13},{13,9},{2,6},{6,2},{1... | collective-permute-start | bytes 196616 | tf_op jit(solution)/shard_map/ppermute | solution.py:22
  56.9 2.2 %collective-permute-done.16.refs_3_ = bf16[8,32,128]{2,1,0:T(8,128)(2,1)S(1)} collective-permute-done((bf16[8,32,128]{2,1,0:T(8,128)(2,1)S(1)}, bf16[8,32,128]{2,1,0:T(8,128)(2,1)S(1)}, u32[]{:S(2)}, u32[]{:S(2)}) %collective-permute-start.16) | collective-permute-done | bytes 65568 | tf_op jit(solution)/shard_map/ppermute | solution.py:22
  59.1 1.1 %far.3 = (f32[32,32,64]{2,1,0:T(8,128)S(1)}, bf16[16,32,128]{2,1,0:T(8,128)(2,1)S(1)}) custom-call(s32[3,160]{1,0:T(4,128)S(4)} %get-tuple-element.32.plan_ref, bf16[160,64,64]{2,1,0:T(8,128)(2,1)S(1)} %get-tuple-element.33.pairs_ref, bf16[8,32,128]{2,1,0:T(8,128)(2,1)S(1)} %add_convert_fusion.refs_0_, ...), custom_call_target="tpu_custom_call" | custom-call | bytes 11070000 | tf_op jit(solution)/shard_map/far/pallas_call | solution.py:340
  60.2 1.7 %collective-permute-start.17 = (bf16[16,32,128]{2,1,0:T(8,128)(2,1)S(1)}, bf16[16,32,128]{2,1,0:T(8,128)(2,1)S(1)}, u32[]{:S(2)}, u32[]{:S(2)}) collective-permute-start(bf16[16,32,128]{2,1,0:T(8,128)(2,1)S(1)} %get-tuple-element.47), channel_id=1, source_target_pairs={{0,2},{2,0},{1,3},{3,1},{4,6},{6,4},{5,7},{7,5},{8,10},{10,8},{9,1... | collective-permute-start | bytes 393224 | tf_op jit(solution)/shard_map/ppermute | solution.py:22
  62.0 1.5 %near_halves.5.acc_in = f32[33,32,128]{2,1,0:T(8,128)S(1)} custom-call(s32[4,144]{1,0:T(4,128)S(4)} %get-tuple-element.25.plan_ref, bf16[32,32,128]{2,1,0:T(8,128)(2,1)S(1)} %collective-permute-done.14.same_ref, bf16[32,32,128]{2,1,0:T(8,128)(2,1)S(1)} %collective-permute-done.15.other_ref, bf16[128,128,256]{2,1,0:T(8,128)(2,1)S(1)} %get-tuple-element.27.blocks_ref, ...), custom_call_target="tpu_custom_call" | custom-call | bytes 7380000 | tf_op jit(solution)/shard_map/near_halves/pallas_call | solution.py:328
  63.5 1.8 %collective-permute-done.17.far_other_ref = bf16[16,32,128]{2,1,0:T(8,128)(2,1)S(1)} collective-permute-done((bf16[16,32,128]{2,1,0:T(8,128)(2,1)S(1)}, bf16[16,32,128]{2,1,0:T(8,128)(2,1)S(1)}, u32[]{:S(2)}, u32[]{:S(2)}) %collective-permute-start.17) | collective-permute-done | bytes 131104 | tf_op jit(solution)/shard_map/ppermute | solution.py:22
  65.3 2.5 %finish.3 = f32[32,32,128]{2,1,0:T(8,128)} custom-call(s32[4,144]{1,0:T(4,128)S(4)} %get-tuple-element.25.plan_ref, bf16[32,32,128]{2,1,0:T(8,128)(2,1)S(1)} %collective-permute-done.9.same_ref, bf16[32,32,128]{2,1,0:T(8,128)(2,1)S(1)} %collective-permute-done.13.other_ref, bf16[128,128,256]{2,1,0:T(8,128)(2,1)S(1)} %get-tuple-element.27.blocks_ref, ...), custom_call_target="tpu_custom_call" | custom-call | bytes 14760000 | tf_op jit(solution)/shard_map/finish/pallas_call | solution.py:359
  (18 shorter events, 1.6 us)
Async XLA Ops:
  0.6 14.6 %copy-start = (f32[32,256,32]{1,2,0:T(8,128)S(1)}, f32[32,256,32]{1,2,0:T(8,128)}, u32[]{:S(2)}) copy-start(f32[32,256,32]{1,2,0:T(8,128)} %param.6) | copy-start | bytes 3145732
  2.6 6.6 %collective-permute-start.1 = (bf16[8,32,128]{2,1,0:T(8,128)(2,1)S(1)}, bf16[8,32,128]{2,1,0:T(8,128)(2,1)S(1)}, u32[]{:S(2)}, u32[]{:S(2)}) collective-permute-start(bf16[8,32,128]{2,1,0:T(8,128)(2,1)S(1)} %get-tuple-element.29), channel_id=1, source_target_pairs={{0,2},{2,0},{1,3},{3,1},{4,6},{6,4},{5,7},{7,5},{8,10},{10,8},{9,1... | collective-permute-start | bytes 196616 | tf_op jit(solution)/shard_map/ppermute | solution.py:22
  5.6 11.3 %collective-permute-start.4 = (bf16[32,32,128]{2,1,0:T(8,128)(2,1)S(1)}, bf16[32,32,128]{2,1,0:T(8,128)(2,1)S(1)}, u32[]{:S(2)}, u32[]{:S(2)}) collective-permute-start(bf16[32,32,128]{2,1,0:T(8,128)(2,1)S(1)} %get-tuple-element.26), channel_id=1, source_target_pairs={{0,12},{4,8},{8,4},{12,0},{1,13},{5,9},{9,5},{13,1},{2,14},{6,10},... | collective-permute-start | bytes 786440 | tf_op jit(solution)/shard_map/ppermute | solution.py:22
  9.2 13.6 %collective-permute-start = (bf16[32,32,128]{2,1,0:T(8,128)(2,1)S(1)}, bf16[32,32,128]{2,1,0:T(8,128)(2,1)S(1)}, u32[]{:S(2)}, u32[]{:S(2)}) collective-permute-start(bf16[32,32,128]{2,1,0:T(8,128)(2,1)S(1)} %get-tuple-element.26), channel_id=1, source_target_pairs={{0,4},{4,0},{8,12},{12,8},{1,5},{5,1},{9,13},{13,9},{2,6},{6,2},{1... | collective-permute-start | bytes 786440 | tf_op jit(solution)/shard_map/ppermute | solution.py:22
  9.2 13.6 %collective-permute-start.2 = (bf16[8,32,128]{2,1,0:T(8,128)(2,1)S(1)}, bf16[8,32,128]{2,1,0:T(8,128)(2,1)S(1)}, u32[]{:S(2)}, u32[]{:S(2)}) collective-permute-start(bf16[8,32,128]{2,1,0:T(8,128)(2,1)S(1)} %add_convert_fusion.1.refs_0_), channel_id=1, source_target_pairs={{0,8},{4,12},{8,0},{12,4},{1,9},{5,13},{9,1},{13,5},{2,10},{6,14},... | collective-permute-start | bytes 196616 | tf_op jit(solution)/shard_map/ppermute | solution.py:22
  16.9 14.5 %collective-permute-start.5 = (bf16[32,32,128]{2,1,0:T(8,128)(2,1)S(1)}, bf16[32,32,128]{2,1,0:T(8,128)(2,1)S(1)}, u32[]{:S(2)}, u32[]{:S(2)}) collective-permute-start(bf16[32,32,128]{2,1,0:T(8,128)(2,1)S(1)} %collective-permute-done.4.same_ref), channel_id=1, source_target_pairs={{0,2},{2,0},{1,3},{3,1},{4,6},{6,4},{5,7},{7,5},{8,10},{10,8},{9,1... | collective-permute-start | bytes 786440 | tf_op jit(solution)/shard_map/ppermute | solution.py:22
  22.8 11.6 %collective-permute-start.3 = (bf16[32,32,128]{2,1,0:T(8,128)(2,1)S(1)}, bf16[32,32,128]{2,1,0:T(8,128)(2,1)S(1)}, u32[]{:S(2)}, u32[]{:S(2)}) collective-permute-start(bf16[32,32,128]{2,1,0:T(8,128)(2,1)S(1)} %collective-permute-done.same_ref), channel_id=1, source_target_pairs={{0,2},{2,0},{1,3},{3,1},{4,6},{6,4},{5,7},{7,5},{8,10},{10,8},{9,1... | collective-permute-start | bytes 786440 | tf_op jit(solution)/shard_map/ppermute | solution.py:22
  23.3 4.3 %collective-permute-start.6 = (bf16[8,32,128]{2,1,0:T(8,128)(2,1)S(1)}, bf16[8,32,128]{2,1,0:T(8,128)(2,1)S(1)}, u32[]{:S(2)}, u32[]{:S(2)}) collective-permute-start(bf16[8,32,128]{2,1,0:T(8,128)(2,1)S(1)} %add_convert_fusion.1.refs_0_), channel_id=1, source_target_pairs={{0,4},{4,0},{8,12},{12,8},{1,5},{5,1},{9,13},{13,9},{2,6},{6,2},{1... | collective-permute-start | bytes 196616 | tf_op jit(solution)/shard_map/ppermute | solution.py:22
  24.0 4.3 %collective-permute-start.7 = (bf16[8,32,128]{2,1,0:T(8,128)(2,1)S(1)}, bf16[8,32,128]{2,1,0:T(8,128)(2,1)S(1)}, u32[]{:S(2)}, u32[]{:S(2)}) collective-permute-start(bf16[8,32,128]{2,1,0:T(8,128)(2,1)S(1)} %collective-permute-done.2.refs_2_), channel_id=1, source_target_pairs={{0,4},{4,0},{8,12},{12,8},{1,5},{5,1},{9,13},{13,9},{2,6},{6,2},{1... | collective-permute-start | bytes 196616 | tf_op jit(solution)/shard_map/ppermute | solution.py:22
  29.4 5.0 %collective-permute-start.8 = (bf16[16,32,128]{2,1,0:T(8,128)(2,1)S(1)}, bf16[16,32,128]{2,1,0:T(8,128)(2,1)S(1)}, u32[]{:S(2)}, u32[]{:S(2)}) collective-permute-start(bf16[16,32,128]{2,1,0:T(8,128)(2,1)S(1)} %get-tuple-element.36), channel_id=1, source_target_pairs={{0,2},{2,0},{1,3},{3,1},{4,6},{6,4},{5,7},{7,5},{8,10},{10,8},{9,1... | collective-permute-start | bytes 393224 | tf_op jit(solution)/shard_map/ppermute | solution.py:22
  37.1 7.1 %collective-permute-start.10 = (bf16[40,32,128]{2,1,0:T(8,128)(2,1)S(1)}, bf16[40,32,128]{2,1,0:T(8,128)(2,1)S(1)}, u32[]{:S(2)}, u32[]{:S(2)}) collective-permute-start(bf16[40,32,128]{2,1,0:T(8,128)(2,1)S(1)} %get-tuple-element.40), channel_id=1, source_target_pairs={{0,2},{2,0},{1,3},{3,1},{4,6},{6,4},{5,7},{7,5},{8,10},{10,8},{9,1... | collective-permute-start | bytes 983048 | tf_op jit(solution)/shard_map/ppermute | solution.py:22
  39.0 10.8 %collective-permute-start.14 = (bf16[32,32,128]{2,1,0:T(8,128)(2,1)S(1)}, bf16[32,32,128]{2,1,0:T(8,128)(2,1)S(1)}, u32[]{:S(2)}, u32[]{:S(2)}) collective-permute-start(bf16[32,32,128]{2,1,0:T(8,128)(2,1)S(1)} %get-tuple-element.39.same_ref), channel_id=1, source_target_pairs={{0,12},{4,8},{8,4},{12,0},{1,13},{5,9},{9,5},{13,1},{2,14},{6,10},... | collective-permute-start | bytes 786440 | tf_op jit(solution)/shard_map/ppermute | solution.py:22
  41.5 10.5 %collective-permute-start.9 = (bf16[32,32,128]{2,1,0:T(8,128)(2,1)S(1)}, bf16[32,32,128]{2,1,0:T(8,128)(2,1)S(1)}, u32[]{:S(2)}, u32[]{:S(2)}) collective-permute-start(bf16[32,32,128]{2,1,0:T(8,128)(2,1)S(1)} %get-tuple-element.39.same_ref), channel_id=1, source_target_pairs={{0,4},{4,0},{8,12},{12,8},{1,5},{5,1},{9,13},{13,9},{2,6},{6,2},{1... | collective-permute-start | bytes 786440 | tf_op jit(solution)/shard_map/ppermute | solution.py:22
  44.2 9.9 %collective-permute-start.12 = (bf16[8,32,128]{2,1,0:T(8,128)(2,1)S(1)}, bf16[8,32,128]{2,1,0:T(8,128)(2,1)S(1)}, u32[]{:S(2)}, u32[]{:S(2)}) collective-permute-start(bf16[8,32,128]{2,1,0:T(8,128)(2,1)S(1)} %add_convert_fusion.refs_0_), channel_id=1, source_target_pairs={{0,8},{4,12},{8,0},{12,4},{1,9},{5,13},{9,1},{13,5},{2,10},{6,14},... | collective-permute-start | bytes 196616 | tf_op jit(solution)/shard_map/ppermute | solution.py:22
  46.5 7.5 %collective-permute-start.11 = (bf16[8,32,128]{2,1,0:T(8,128)(2,1)S(1)}, bf16[8,32,128]{2,1,0:T(8,128)(2,1)S(1)}, u32[]{:S(2)}, u32[]{:S(2)}) collective-permute-start(bf16[8,32,128]{2,1,0:T(8,128)(2,1)S(1)} %add_convert_fusion.refs_0_), channel_id=1, source_target_pairs={{0,4},{4,0},{8,12},{12,8},{1,5},{5,1},{9,13},{13,9},{2,6},{6,2},{1... | collective-permute-start | bytes 196616 | tf_op jit(solution)/shard_map/ppermute | solution.py:22
  49.8 12.1 %collective-permute-start.15 = (bf16[32,32,128]{2,1,0:T(8,128)(2,1)S(1)}, bf16[32,32,128]{2,1,0:T(8,128)(2,1)S(1)}, u32[]{:S(2)}, u32[]{:S(2)}) collective-permute-start(bf16[32,32,128]{2,1,0:T(8,128)(2,1)S(1)} %collective-permute-done.14.same_ref), channel_id=1, source_target_pairs={{0,2},{2,0},{1,3},{3,1},{4,6},{6,4},{5,7},{7,5},{8,10},{10,8},{9,1... | collective-permute-start | bytes 786440 | tf_op jit(solution)/shard_map/ppermute | solution.py:22
  54.1 11.2 %collective-permute-start.13 = (bf16[32,32,128]{2,1,0:T(8,128)(2,1)S(1)}, bf16[32,32,128]{2,1,0:T(8,128)(2,1)S(1)}, u32[]{:S(2)}, u32[]{:S(2)}) collective-permute-start(bf16[32,32,128]{2,1,0:T(8,128)(2,1)S(1)} %collective-permute-done.9.same_ref), channel_id=1, source_target_pairs={{0,2},{2,0},{1,3},{3,1},{4,6},{6,4},{5,7},{7,5},{8,10},{10,8},{9,1... | collective-permute-start | bytes 786440 | tf_op jit(solution)/shard_map/ppermute | solution.py:22
  54.5 4.7 %collective-permute-start.16 = (bf16[8,32,128]{2,1,0:T(8,128)(2,1)S(1)}, bf16[8,32,128]{2,1,0:T(8,128)(2,1)S(1)}, u32[]{:S(2)}, u32[]{:S(2)}) collective-permute-start(bf16[8,32,128]{2,1,0:T(8,128)(2,1)S(1)} %collective-permute-done.12.refs_2_), channel_id=1, source_target_pairs={{0,4},{4,0},{8,12},{12,8},{1,5},{5,1},{9,13},{13,9},{2,6},{6,2},{1... | collective-permute-start | bytes 196616 | tf_op jit(solution)/shard_map/ppermute | solution.py:22
  60.2 5.0 %collective-permute-start.17 = (bf16[16,32,128]{2,1,0:T(8,128)(2,1)S(1)}, bf16[16,32,128]{2,1,0:T(8,128)(2,1)S(1)}, u32[]{:S(2)}, u32[]{:S(2)}) collective-permute-start(bf16[16,32,128]{2,1,0:T(8,128)(2,1)S(1)} %get-tuple-element.47), channel_id=1, source_target_pairs={{0,2},{2,0},{1,3},{3,1},{4,6},{6,4},{5,7},{7,5},{8,10},{10,8},{9,1... | collective-permute-start | bytes 393224 | tf_op jit(solution)/shard_map/ppermute | solution.py:22

commit v7 on v6

--- a/solution.py
+++ b/solution.py
@@ -9,7 +9,7 @@
 
 UNROLL = 16
 FIELD = 9
-FAR_UNROLL = 32
+FAR_UNROLL = 16
 VMEM = pl.BlockSpec(memory_space=pltpu.VMEM)
 ANY = pl.BlockSpec(memory_space=pl.ANY)
 HBM = pl.BlockSpec(memory_space=pltpu.HBM)

time: 69 us -> 68 us (0.986); the launches traced: 67.8 us -> 67.7 us
  starting transfers between devices: 28.6 us -> 27.8 us
    ppermute x18, starting transfers between devices: 28.6 us -> 27.8 us  [swapped(): lax.ppermute(array, axis, [(i, partner(i)) for i in range(lax.axis_size(a...]
  transfers between devices with their start and end apart: 18 -> 18, of which waited for: 10 -> 11; matrix products, arithmetic and copies ran while one was open for 0% -> 0% of each run, Pallas kernels for 19% -> 19%
where the time goes in v7:
time: 68 us; the launch traced here: 67.7 us
  starting transfers between devices  27.8 us (41%)
  Pallas kernels  20.1 us (30%)
  waiting for transfers between devices  19 us (28%)
  between operations  0.74 us (1%)
    ppermute x18, starting transfers between devices, swapped(): lax.ppermute(array, axis, [(i, partner(i)) for i in range(lax.axis_size(a...  27.8 us
    ppermute x18, waiting for transfers between devices, swapped(): lax.ppermute(array, axis, [(i, partner(i)) for i in range(lax.axis_size(a...  19 us
    pallas_call x2, Pallas kernels, finish(): pl.pallas_call(finish_kernel, out_shape=outs, in_specs=[SMEM] + [VMEM] *...  5.15 us
    pallas_call x3, Pallas kernels, near_halves(): pl.pallas_call(functools.partial(near_halves_kernel, kind), out_shape=acc...  4.55 us
    pallas_call x1, Pallas kernels, tiled_on_device(): pl.pallas_call(functools.partial(prepare_kernel, clusters), out_shape=(pl...  4.28 us
    pallas_call x2, Pallas kernels, far(): pl.pallas_call(far_kernel, out_shape=(jax.ShapeDtypeStruct((clusters, col...  2.67 us
    pallas_call x1, Pallas kernels, tiled_on_device(): pl.pallas_call(start_kernel, out_shape=(mine_shape, jax.ShapeDtypeStruct(...  1.9 us
    pallas_call x1, Pallas kernels, near_own(): pl.pallas_call(near_own_kernel, out_shape=acc_shape, in_specs=[SMEM, HBM,...  1.56 us
  transfers between devices with their start and end apart: 18, of which 11 were waited for; matrix products, arithmetic and copies ran while one was open for 0% of the time, Pallas kernels for 19%

profile of v7, /device:TPU:0, one launch (start us, length us, event | category | flops | bytes accessed | tf_op | source)
XLA Modules:
  0.0 67.7 jit_solution(8083942371960531100)
XLA Ops:
  0.6 1.9 %start.1 = (bf16[32,32,128]{2,1,0:T(8,128)(2,1)S(1)}, bf16[32,64,128]{2,1,0:T(8,128)(2,1)S(1)}, f32[8,32,128]{2,1,0:T(8,128)S(1)}, bf16[8,32,128]{2,1,0:T(8,128)(2,1)S(1)}) custom-call(f32[32,32,256]{2,1,0:T(8,128)} %bitcast.7, bf16[32,64,128]{2,1,0:T(8,128)(2,1)} %bitcast.10), custom_call_target="tpu_custom_call" | custom-call | bytes 7380000 | tf_op jit(solution)/shard_map/start/pallas_call | solution.py:278
  2.6 3.0 %collective-permute-start.1 = (bf16[8,32,128]{2,1,0:T(8,128)(2,1)S(1)}, bf16[8,32,128]{2,1,0:T(8,128)(2,1)S(1)}, u32[]{:S(2)}, u32[]{:S(2)}) collective-permute-start(bf16[8,32,128]{2,1,0:T(8,128)(2,1)S(1)} %get-tuple-element.29), channel_id=1, source_target_pairs={{0,2},{2,0},{1,3},{3,1},{4,6},{6,4},{5,7},{7,5},{8,10},{10,8},{9,1... | collective-permute-start | bytes 196616 | tf_op jit(solution)/shard_map/ppermute | solution.py:22
  5.6 3.6 %collective-permute-start.4 = (bf16[32,32,128]{2,1,0:T(8,128)(2,1)S(1)}, bf16[32,32,128]{2,1,0:T(8,128)(2,1)S(1)}, u32[]{:S(2)}, u32[]{:S(2)}) collective-permute-start(bf16[32,32,128]{2,1,0:T(8,128)(2,1)S(1)} %get-tuple-element.26), channel_id=1, source_target_pairs={{0,12},{4,8},{8,4},{12,0},{1,13},{5,9},{9,5},{13,1},{2,14},{6,10},... | collective-permute-start | bytes 786440 | tf_op jit(solution)/shard_map/ppermute | solution.py:22
  9.2 1.8 %collective-permute-start.2 = (bf16[8,32,128]{2,1,0:T(8,128)(2,1)S(1)}, bf16[8,32,128]{2,1,0:T(8,128)(2,1)S(1)}, u32[]{:S(2)}, u32[]{:S(2)}) collective-permute-start(bf16[8,32,128]{2,1,0:T(8,128)(2,1)S(1)} %add_convert_fusion.1.refs_0_), channel_id=1, source_target_pairs={{0,8},{4,12},{8,0},{12,4},{1,9},{5,13},{9,1},{13,5},{2,10},{6,14},... | collective-permute-start | bytes 196616 | tf_op jit(solution)/shard_map/ppermute | solution.py:22
  11.0 4.3 %prepare.1 = (s32[4,144]{1,0:T(4,128)S(4)}, s32[3,144]{1,0:T(4,128)S(4)}, bf16[128,128,256]{2,1,0:T(8,128)(2,1)S(1)}, bf16[144,64,64]{2,1,0:T(8,128)(2,1)S(1)}) custom-call(s32[2,128]{1,0:T(2,128)} %bitcast.12, s32[2,128]{1,0:T(2,128)} %bitcast.13, bf16[128,128,256]{2,1,0:T(8,128)(2,1)} %blocks_hbm.1, bf16[64,64,128]{2,1,0:T(8,128)(2,1)} %bitcast.9), custom_call_target="tpu_custom_call" | custom-call | bytes 14760000 | tf_op jit(solution)/shard_map/prepare/pallas_call | solution.py:288
  15.3 1.6 %near_own.1.refs_0_ = f32[33,32,128]{2,1,0:T(8,128)S(1)} custom-call(s32[4,144]{1,0:T(4,128)S(4)} %get-tuple-element.25.plan_ref, f32[32,32,256]{2,1,0:T(8,128)S(1)} %bitcast.8, bf16[128,128,256]{2,1,0:T(8,128)(2,1)S(1)} %get-tuple-element.27.blocks_ref), custom_call_target="tpu_custom_call" | custom-call | bytes 11070000 | tf_op jit(solution)/shard_map/near_own/pallas_call | solution.py:312
  16.9 2.1 %collective-permute-start.5 = (bf16[32,32,128]{2,1,0:T(8,128)(2,1)S(1)}, bf16[32,32,128]{2,1,0:T(8,128)(2,1)S(1)}, u32[]{:S(2)}, u32[]{:S(2)}) collective-permute-start(bf16[32,32,128]{2,1,0:T(8,128)(2,1)S(1)} %collective-permute-done.4.same_ref), channel_id=1, source_target_pairs={{0,2},{2,0},{1,3},{3,1},{4,6},{6,4},{5,7},{7,5},{8,10},{10,8},{9,1... | collective-permute-start | bytes 786440 | tf_op jit(solution)/shard_map/ppermute | solution.py:22
  19.0 3.8 %collective-permute-done.2.refs_2_ = bf16[8,32,128]{2,1,0:T(8,128)(2,1)S(1)} collective-permute-done((bf16[8,32,128]{2,1,0:T(8,128)(2,1)S(1)}, bf16[8,32,128]{2,1,0:T(8,128)(2,1)S(1)}, u32[]{:S(2)}, u32[]{:S(2)}) %collective-permute-start.2) | collective-permute-done | bytes 65568 | tf_op jit(solution)/shard_map/ppermute | solution.py:22
  23.3 0.7 collective-permute-start.6
  24.0 1.4 %collective-permute-start.7 = (bf16[8,32,128]{2,1,0:T(8,128)(2,1)S(1)}, bf16[8,32,128]{2,1,0:T(8,128)(2,1)S(1)}, u32[]{:S(2)}, u32[]{:S(2)}) collective-permute-start(bf16[8,32,128]{2,1,0:T(8,128)(2,1)S(1)} %collective-permute-done.2.refs_2_), channel_id=1, source_target_pairs={{0,4},{4,0},{8,12},{12,8},{1,5},{5,1},{9,13},{13,9},{2,6},{6,2},{1... | collective-permute-start | bytes 196616 | tf_op jit(solution)/shard_map/ppermute | solution.py:22
  25.3 2.2 %collective-permute-done.6.refs_1_ = bf16[8,32,128]{2,1,0:T(8,128)(2,1)S(1)} collective-permute-done((bf16[8,32,128]{2,1,0:T(8,128)(2,1)S(1)}, bf16[8,32,128]{2,1,0:T(8,128)(2,1)S(1)}, u32[]{:S(2)}, u32[]{:S(2)}) %collective-permute-start.6) | collective-permute-done | bytes 65568 | tf_op jit(solution)/shard_map/ppermute | solution.py:22
  27.6 0.7 %collective-permute-done.7.refs_3_ = bf16[8,32,128]{2,1,0:T(8,128)(2,1)S(1)} collective-permute-done((bf16[8,32,128]{2,1,0:T(8,128)(2,1)S(1)}, bf16[8,32,128]{2,1,0:T(8,128)(2,1)S(1)}, u32[]{:S(2)}, u32[]{:S(2)}) %collective-permute-start.7) | collective-permute-done | bytes 65568 | tf_op jit(solution)/shard_map/ppermute | solution.py:22
  28.3 1.3 %far.2 = (f32[32,32,64]{2,1,0:T(8,128)S(1)}, bf16[16,32,128]{2,1,0:T(8,128)(2,1)S(1)}) custom-call(s32[3,144]{1,0:T(4,128)S(4)} %get-tuple-element.32.plan_ref, bf16[144,64,64]{2,1,0:T(8,128)(2,1)S(1)} %get-tuple-element.33.pairs_ref, bf16[8,32,128]{2,1,0:T(8,128)(2,1)S(1)} %add_convert_fusion.1.refs_0_, ...), custom_call_target="tpu_custom_call" | custom-call | bytes 11070000 | tf_op jit(solution)/shard_map/far/pallas_call | solution.py:340
  29.6 1.8 %collective-permute-start.8 = (bf16[16,32,128]{2,1,0:T(8,128)(2,1)S(1)}, bf16[16,32,128]{2,1,0:T(8,128)(2,1)S(1)}, u32[]{:S(2)}, u32[]{:S(2)}) collective-permute-start(bf16[16,32,128]{2,1,0:T(8,128)(2,1)S(1)} %get-tuple-element.36), channel_id=1, source_target_pairs={{0,2},{2,0},{1,3},{3,1},{4,6},{6,4},{5,7},{7,5},{8,10},{10,8},{9,1... | collective-permute-start | bytes 393224 | tf_op jit(solution)/shard_map/ppermute | solution.py:22
  31.4 1.5 %near_halves.3.acc_in = f32[33,32,128]{2,1,0:T(8,128)S(1)} custom-call(s32[4,144]{1,0:T(4,128)S(4)} %get-tuple-element.25.plan_ref, bf16[32,32,128]{2,1,0:T(8,128)(2,1)S(1)} %collective-permute-done.4.same_ref, bf16[32,32,128]{2,1,0:T(8,128)(2,1)S(1)} %collective-permute-done.5.other_ref, bf16[128,128,256]{2,1,0:T(8,128)(2,1)S(1)} %get-tuple-element.27.blocks_ref, ...), custom_call_target="tpu_custom_call" | custom-call | bytes 7380000 | tf_op jit(solution)/shard_map/near_halves/pallas_call | solution.py:328
  33.0 1.7 %collective-permute-done.8.far_other_ref = bf16[16,32,128]{2,1,0:T(8,128)(2,1)S(1)} collective-permute-done((bf16[16,32,128]{2,1,0:T(8,128)(2,1)S(1)}, bf16[16,32,128]{2,1,0:T(8,128)(2,1)S(1)}, u32[]{:S(2)}, u32[]{:S(2)}) %collective-permute-start.8) | collective-permute-done | bytes 131104 | tf_op jit(solution)/shard_map/ppermute | solution.py:22
  34.6 2.7 %finish.2 = (f32[32,32,128]{2,1,0:T(8,128)}, bf16[32,32,128]{2,1,0:T(8,128)(2,1)S(1)}, f32[8,32,128]{2,1,0:T(8,128)S(1)}, bf16[40,32,128]{2,1,0:T(8,128)(2,1)S(1)}) custom-call(s32[4,144]{1,0:T(4,128)S(4)} %get-tuple-element.25.plan_ref, bf16[32,32,128]{2,1,0:T(8,128)(2,1)S(1)} %collective-permute-done.same_ref, ...), custom_call_target="tpu_custom_call" | custom-call | bytes 14760000 | tf_op jit(solution)/shard_map/finish/pallas_call | solution.py:359
  37.3 1.8 %collective-permute-start.10 = (bf16[40,32,128]{2,1,0:T(8,128)(2,1)S(1)}, bf16[40,32,128]{2,1,0:T(8,128)(2,1)S(1)}, u32[]{:S(2)}, u32[]{:S(2)}) collective-permute-start(bf16[40,32,128]{2,1,0:T(8,128)(2,1)S(1)} %get-tuple-element.40), channel_id=1, source_target_pairs={{0,2},{2,0},{1,3},{3,1},{4,6},{6,4},{5,7},{7,5},{8,10},{10,8},{9,1... | collective-permute-start | bytes 983048 | tf_op jit(solution)/shard_map/ppermute | solution.py:22
  39.1 2.9 %collective-permute-start.14 = (bf16[32,32,128]{2,1,0:T(8,128)(2,1)S(1)}, bf16[32,32,128]{2,1,0:T(8,128)(2,1)S(1)}, u32[]{:S(2)}, u32[]{:S(2)}) collective-permute-start(bf16[32,32,128]{2,1,0:T(8,128)(2,1)S(1)} %get-tuple-element.39.same_ref), channel_id=1, source_target_pairs={{0,12},{4,8},{8,4},{12,0},{1,13},{5,9},{9,5},{13,1},{2,14},{6,10},... | collective-permute-start | bytes 786440 | tf_op jit(solution)/shard_map/ppermute | solution.py:22
  42.0 2.4 %collective-permute-done.10.other_ref = bf16[40,32,128]{2,1,0:T(8,128)(2,1)S(1)} collective-permute-done((bf16[40,32,128]{2,1,0:T(8,128)(2,1)S(1)}, bf16[40,32,128]{2,1,0:T(8,128)(2,1)S(1)}, u32[]{:S(2)}, u32[]{:S(2)}) %collective-permute-start.10) | collective-permute-done | bytes 327712 | tf_op jit(solution)/shard_map/ppermute | solution.py:22
  44.5 2.9 %collective-permute-start.12 = (bf16[8,32,128]{2,1,0:T(8,128)(2,1)S(1)}, bf16[8,32,128]{2,1,0:T(8,128)(2,1)S(1)}, u32[]{:S(2)}, u32[]{:S(2)}) collective-permute-start(bf16[8,32,128]{2,1,0:T(8,128)(2,1)S(1)} %add_convert_fusion.refs_0_), channel_id=1, source_target_pairs={{0,8},{4,12},{8,0},{12,4},{1,9},{5,13},{9,1},{13,5},{2,10},{6,14},... | collective-permute-start | bytes 196616 | tf_op jit(solution)/shard_map/ppermute | solution.py:22
  48.0 2.1 %collective-permute-done.14.same_ref = bf16[32,32,128]{2,1,0:T(8,128)(2,1)S(1)} collective-permute-done((bf16[32,32,128]{2,1,0:T(8,128)(2,1)S(1)}, bf16[32,32,128]{2,1,0:T(8,128)(2,1)S(1)}, u32[]{:S(2)}, u32[]{:S(2)}) %collective-permute-start.14) | collective-permute-done | bytes 262176 | tf_op jit(solution)/shard_map/ppermute | solution.py:22
  50.4 1.5 %near_halves.4.refs_0_ = f32[33,32,128]{2,1,0:T(8,128)S(1)} custom-call(s32[4,144]{1,0:T(4,128)S(4)} %get-tuple-element.25.plan_ref, bf16[32,32,128]{2,1,0:T(8,128)(2,1)S(1)} %get-tuple-element.39.same_ref, bf16[40,32,128]{2,1,0:T(8,128)(2,1)S(1)} %collective-permute-done.10.other_ref, bf16[128,128,256]{2,1,0:T(8,128)(2,1)S(1)} %get-tuple-element.27.blocks_ref), custom_call_target="tpu_custom_call" | custom-call | bytes 7380000 | tf_op jit(solution)/shard_map/near_halves/pallas_call | solution.py:328
  51.9 1.2 %collective-permute-done.9.same_ref = bf16[32,32,128]{2,1,0:T(8,128)(2,1)S(1)} collective-permute-done((bf16[32,32,128]{2,1,0:T(8,128)(2,1)S(1)}, bf16[32,32,128]{2,1,0:T(8,128)(2,1)S(1)}, u32[]{:S(2)}, u32[]{:S(2)}) %collective-permute-start.9) | collective-permute-done | bytes 262176 | tf_op jit(solution)/shard_map/ppermute | solution.py:22
  53.2 0.7 %collective-permute-done.12.refs_2_ = bf16[8,32,128]{2,1,0:T(8,128)(2,1)S(1)} collective-permute-done((bf16[8,32,128]{2,1,0:T(8,128)(2,1)S(1)}, bf16[8,32,128]{2,1,0:T(8,128)(2,1)S(1)}, u32[]{:S(2)}, u32[]{:S(2)}) %collective-permute-start.12) | collective-permute-done | bytes 65568 | tf_op jit(solution)/shard_map/ppermute | solution.py:22
  54.5 2.0 %collective-permute-start.16 = (bf16[8,32,128]{2,1,0:T(8,128)(2,1)S(1)}, bf16[8,32,128]{2,1,0:T(8,128)(2,1)S(1)}, u32[]{:S(2)}, u32[]{:S(2)}) collective-permute-start(bf16[8,32,128]{2,1,0:T(8,128)(2,1)S(1)} %collective-permute-done.12.refs_2_), channel_id=1, source_target_pairs={{0,4},{4,0},{8,12},{12,8},{1,5},{5,1},{9,13},{13,9},{2,6},{6,2},{1... | collective-permute-start | bytes 196616 | tf_op jit(solution)/shard_map/ppermute | solution.py:22
  56.5 2.3 %collective-permute-done.16.refs_3_ = bf16[8,32,128]{2,1,0:T(8,128)(2,1)S(1)} collective-permute-done((bf16[8,32,128]{2,1,0:T(8,128)(2,1)S(1)}, bf16[8,32,128]{2,1,0:T(8,128)(2,1)S(1)}, u32[]{:S(2)}, u32[]{:S(2)}) %collective-permute-start.16) | collective-permute-done | bytes 65568 | tf_op jit(solution)/shard_map/ppermute | solution.py:22
  58.8 1.3 %far.3 = (f32[32,32,64]{2,1,0:T(8,128)S(1)}, bf16[16,32,128]{2,1,0:T(8,128)(2,1)S(1)}) custom-call(s32[3,144]{1,0:T(4,128)S(4)} %get-tuple-element.32.plan_ref, bf16[144,64,64]{2,1,0:T(8,128)(2,1)S(1)} %get-tuple-element.33.pairs_ref, bf16[8,32,128]{2,1,0:T(8,128)(2,1)S(1)} %add_convert_fusion.refs_0_, ...), custom_call_target="tpu_custom_call" | custom-call | bytes 11070000 | tf_op jit(solution)/shard_map/far/pallas_call | solution.py:340
  60.2 1.7 %collective-permute-start.17 = (bf16[16,32,128]{2,1,0:T(8,128)(2,1)S(1)}, bf16[16,32,128]{2,1,0:T(8,128)(2,1)S(1)}, u32[]{:S(2)}, u32[]{:S(2)}) collective-permute-start(bf16[16,32,128]{2,1,0:T(8,128)(2,1)S(1)} %get-tuple-element.47), channel_id=1, source_target_pairs={{0,2},{2,0},{1,3},{3,1},{4,6},{6,4},{5,7},{7,5},{8,10},{10,8},{9,1... | collective-permute-start | bytes 393224 | tf_op jit(solution)/shard_map/ppermute | solution.py:22
  61.9 1.5 %near_halves.5.acc_in = f32[33,32,128]{2,1,0:T(8,128)S(1)} custom-call(s32[4,144]{1,0:T(4,128)S(4)} %get-tuple-element.25.plan_ref, bf16[32,32,128]{2,1,0:T(8,128)(2,1)S(1)} %collective-permute-done.14.same_ref, bf16[32,32,128]{2,1,0:T(8,128)(2,1)S(1)} %collective-permute-done.15.other_ref, bf16[128,128,256]{2,1,0:T(8,128)(2,1)S(1)} %get-tuple-element.27.blocks_ref, ...), custom_call_target="tpu_custom_call" | custom-call | bytes 7380000 | tf_op jit(solution)/shard_map/near_halves/pallas_call | solution.py:328
  63.4 1.8 %collective-permute-done.17.far_other_ref = bf16[16,32,128]{2,1,0:T(8,128)(2,1)S(1)} collective-permute-done((bf16[16,32,128]{2,1,0:T(8,128)(2,1)S(1)}, bf16[16,32,128]{2,1,0:T(8,128)(2,1)S(1)}, u32[]{:S(2)}, u32[]{:S(2)}) %collective-permute-start.17) | collective-permute-done | bytes 131104 | tf_op jit(solution)/shard_map/ppermute | solution.py:22
  65.2 2.5 %finish.3 = f32[32,32,128]{2,1,0:T(8,128)} custom-call(s32[4,144]{1,0:T(4,128)S(4)} %get-tuple-element.25.plan_ref, bf16[32,32,128]{2,1,0:T(8,128)(2,1)S(1)} %collective-permute-done.9.same_ref, bf16[32,32,128]{2,1,0:T(8,128)(2,1)S(1)} %collective-permute-done.13.other_ref, bf16[128,128,256]{2,1,0:T(8,128)(2,1)S(1)} %get-tuple-element.27.blocks_ref, ...), custom_call_target="tpu_custom_call" | custom-call | bytes 14760000 | tf_op jit(solution)/shard_map/finish/pallas_call | solution.py:359
  (18 shorter events, 2.3 us)
Async XLA Ops:
  0.6 14.7 %copy-start = (f32[32,256,32]{1,2,0:T(8,128)S(1)}, f32[32,256,32]{1,2,0:T(8,128)}, u32[]{:S(2)}) copy-start(f32[32,256,32]{1,2,0:T(8,128)} %param.6) | copy-start | bytes 3145732
  2.6 6.6 %collective-permute-start.1 = (bf16[8,32,128]{2,1,0:T(8,128)(2,1)S(1)}, bf16[8,32,128]{2,1,0:T(8,128)(2,1)S(1)}, u32[]{:S(2)}, u32[]{:S(2)}) collective-permute-start(bf16[8,32,128]{2,1,0:T(8,128)(2,1)S(1)} %get-tuple-element.29), channel_id=1, source_target_pairs={{0,2},{2,0},{1,3},{3,1},{4,6},{6,4},{5,7},{7,5},{8,10},{10,8},{9,1... | collective-permute-start | bytes 196616 | tf_op jit(solution)/shard_map/ppermute | solution.py:22
  5.6 11.3 %collective-permute-start.4 = (bf16[32,32,128]{2,1,0:T(8,128)(2,1)S(1)}, bf16[32,32,128]{2,1,0:T(8,128)(2,1)S(1)}, u32[]{:S(2)}, u32[]{:S(2)}) collective-permute-start(bf16[32,32,128]{2,1,0:T(8,128)(2,1)S(1)} %get-tuple-element.26), channel_id=1, source_target_pairs={{0,12},{4,8},{8,4},{12,0},{1,13},{5,9},{9,5},{13,1},{2,14},{6,10},... | collective-permute-start | bytes 786440 | tf_op jit(solution)/shard_map/ppermute | solution.py:22
  9.2 13.6 %collective-permute-start = (bf16[32,32,128]{2,1,0:T(8,128)(2,1)S(1)}, bf16[32,32,128]{2,1,0:T(8,128)(2,1)S(1)}, u32[]{:S(2)}, u32[]{:S(2)}) collective-permute-start(bf16[32,32,128]{2,1,0:T(8,128)(2,1)S(1)} %get-tuple-element.26), channel_id=1, source_target_pairs={{0,4},{4,0},{8,12},{12,8},{1,5},{5,1},{9,13},{13,9},{2,6},{6,2},{1... | collective-permute-start | bytes 786440 | tf_op jit(solution)/shard_map/ppermute | solution.py:22
  9.2 13.6 %collective-permute-start.2 = (bf16[8,32,128]{2,1,0:T(8,128)(2,1)S(1)}, bf16[8,32,128]{2,1,0:T(8,128)(2,1)S(1)}, u32[]{:S(2)}, u32[]{:S(2)}) collective-permute-start(bf16[8,32,128]{2,1,0:T(8,128)(2,1)S(1)} %add_convert_fusion.1.refs_0_), channel_id=1, source_target_pairs={{0,8},{4,12},{8,0},{12,4},{1,9},{5,13},{9,1},{13,5},{2,10},{6,14},... | collective-permute-start | bytes 196616 | tf_op jit(solution)/shard_map/ppermute | solution.py:22
  16.9 14.5 %collective-permute-start.5 = (bf16[32,32,128]{2,1,0:T(8,128)(2,1)S(1)}, bf16[32,32,128]{2,1,0:T(8,128)(2,1)S(1)}, u32[]{:S(2)}, u32[]{:S(2)}) collective-permute-start(bf16[32,32,128]{2,1,0:T(8,128)(2,1)S(1)} %collective-permute-done.4.same_ref), channel_id=1, source_target_pairs={{0,2},{2,0},{1,3},{3,1},{4,6},{6,4},{5,7},{7,5},{8,10},{10,8},{9,1... | collective-permute-start | bytes 786440 | tf_op jit(solution)/shard_map/ppermute | solution.py:22
  22.8 11.9 %collective-permute-start.3 = (bf16[32,32,128]{2,1,0:T(8,128)(2,1)S(1)}, bf16[32,32,128]{2,1,0:T(8,128)(2,1)S(1)}, u32[]{:S(2)}, u32[]{:S(2)}) collective-permute-start(bf16[32,32,128]{2,1,0:T(8,128)(2,1)S(1)} %collective-permute-done.same_ref), channel_id=1, source_target_pairs={{0,2},{2,0},{1,3},{3,1},{4,6},{6,4},{5,7},{7,5},{8,10},{10,8},{9,1... | collective-permute-start | bytes 786440 | tf_op jit(solution)/shard_map/ppermute | solution.py:22
  23.3 4.3 %collective-permute-start.6 = (bf16[8,32,128]{2,1,0:T(8,128)(2,1)S(1)}, bf16[8,32,128]{2,1,0:T(8,128)(2,1)S(1)}, u32[]{:S(2)}, u32[]{:S(2)}) collective-permute-start(bf16[8,32,128]{2,1,0:T(8,128)(2,1)S(1)} %add_convert_fusion.1.refs_0_), channel_id=1, source_target_pairs={{0,4},{4,0},{8,12},{12,8},{1,5},{5,1},{9,13},{13,9},{2,6},{6,2},{1... | collective-permute-start | bytes 196616 | tf_op jit(solution)/shard_map/ppermute | solution.py:22
  24.0 4.3 %collective-permute-start.7 = (bf16[8,32,128]{2,1,0:T(8,128)(2,1)S(1)}, bf16[8,32,128]{2,1,0:T(8,128)(2,1)S(1)}, u32[]{:S(2)}, u32[]{:S(2)}) collective-permute-start(bf16[8,32,128]{2,1,0:T(8,128)(2,1)S(1)} %collective-permute-done.2.refs_2_), channel_id=1, source_target_pairs={{0,4},{4,0},{8,12},{12,8},{1,5},{5,1},{9,13},{13,9},{2,6},{6,2},{1... | collective-permute-start | bytes 196616 | tf_op jit(solution)/shard_map/ppermute | solution.py:22
  29.6 5.0 %collective-permute-start.8 = (bf16[16,32,128]{2,1,0:T(8,128)(2,1)S(1)}, bf16[16,32,128]{2,1,0:T(8,128)(2,1)S(1)}, u32[]{:S(2)}, u32[]{:S(2)}) collective-permute-start(bf16[16,32,128]{2,1,0:T(8,128)(2,1)S(1)} %get-tuple-element.36), channel_id=1, source_target_pairs={{0,2},{2,0},{1,3},{3,1},{4,6},{6,4},{5,7},{7,5},{8,10},{10,8},{9,1... | collective-permute-start | bytes 393224 | tf_op jit(solution)/shard_map/ppermute | solution.py:22
  37.3 7.1 %collective-permute-start.10 = (bf16[40,32,128]{2,1,0:T(8,128)(2,1)S(1)}, bf16[40,32,128]{2,1,0:T(8,128)(2,1)S(1)}, u32[]{:S(2)}, u32[]{:S(2)}) collective-permute-start(bf16[40,32,128]{2,1,0:T(8,128)(2,1)S(1)} %get-tuple-element.40), channel_id=1, source_target_pairs={{0,2},{2,0},{1,3},{3,1},{4,6},{6,4},{5,7},{7,5},{8,10},{10,8},{9,1... | collective-permute-start | bytes 983048 | tf_op jit(solution)/shard_map/ppermute | solution.py:22
  39.1 11.0 %collective-permute-start.14 = (bf16[32,32,128]{2,1,0:T(8,128)(2,1)S(1)}, bf16[32,32,128]{2,1,0:T(8,128)(2,1)S(1)}, u32[]{:S(2)}, u32[]{:S(2)}) collective-permute-start(bf16[32,32,128]{2,1,0:T(8,128)(2,1)S(1)} %get-tuple-element.39.same_ref), channel_id=1, source_target_pairs={{0,12},{4,8},{8,4},{12,0},{1,13},{5,9},{9,5},{13,1},{2,14},{6,10},... | collective-permute-start | bytes 786440 | tf_op jit(solution)/shard_map/ppermute | solution.py:22
  42.0 11.1 %collective-permute-start.9 = (bf16[32,32,128]{2,1,0:T(8,128)(2,1)S(1)}, bf16[32,32,128]{2,1,0:T(8,128)(2,1)S(1)}, u32[]{:S(2)}, u32[]{:S(2)}) collective-permute-start(bf16[32,32,128]{2,1,0:T(8,128)(2,1)S(1)} %get-tuple-element.39.same_ref), channel_id=1, source_target_pairs={{0,4},{4,0},{8,12},{12,8},{1,5},{5,1},{9,13},{13,9},{2,6},{6,2},{1... | collective-permute-start | bytes 786440 | tf_op jit(solution)/shard_map/ppermute | solution.py:22
  44.5 9.4 %collective-permute-start.12 = (bf16[8,32,128]{2,1,0:T(8,128)(2,1)S(1)}, bf16[8,32,128]{2,1,0:T(8,128)(2,1)S(1)}, u32[]{:S(2)}, u32[]{:S(2)}) collective-permute-start(bf16[8,32,128]{2,1,0:T(8,128)(2,1)S(1)} %add_convert_fusion.refs_0_), channel_id=1, source_target_pairs={{0,8},{4,12},{8,0},{12,4},{1,9},{5,13},{9,1},{13,5},{2,10},{6,14},... | collective-permute-start | bytes 196616 | tf_op jit(solution)/shard_map/ppermute | solution.py:22
  47.3 6.6 %collective-permute-start.11 = (bf16[8,32,128]{2,1,0:T(8,128)(2,1)S(1)}, bf16[8,32,128]{2,1,0:T(8,128)(2,1)S(1)}, u32[]{:S(2)}, u32[]{:S(2)}) collective-permute-start(bf16[8,32,128]{2,1,0:T(8,128)(2,1)S(1)} %add_convert_fusion.refs_0_), channel_id=1, source_target_pairs={{0,4},{4,0},{8,12},{12,8},{1,5},{5,1},{9,13},{13,9},{2,6},{6,2},{1... | collective-permute-start | bytes 196616 | tf_op jit(solution)/shard_map/ppermute | solution.py:22
  50.1 11.8 %collective-permute-start.15 = (bf16[32,32,128]{2,1,0:T(8,128)(2,1)S(1)}, bf16[32,32,128]{2,1,0:T(8,128)(2,1)S(1)}, u32[]{:S(2)}, u32[]{:S(2)}) collective-permute-start(bf16[32,32,128]{2,1,0:T(8,128)(2,1)S(1)} %collective-permute-done.14.same_ref), channel_id=1, source_target_pairs={{0,2},{2,0},{1,3},{3,1},{4,6},{6,4},{5,7},{7,5},{8,10},{10,8},{9,1... | collective-permute-start | bytes 786440 | tf_op jit(solution)/shard_map/ppermute | solution.py:22
  53.9 11.3 %collective-permute-start.13 = (bf16[32,32,128]{2,1,0:T(8,128)(2,1)S(1)}, bf16[32,32,128]{2,1,0:T(8,128)(2,1)S(1)}, u32[]{:S(2)}, u32[]{:S(2)}) collective-permute-start(bf16[32,32,128]{2,1,0:T(8,128)(2,1)S(1)} %collective-permute-done.9.same_ref), channel_id=1, source_target_pairs={{0,2},{2,0},{1,3},{3,1},{4,6},{6,4},{5,7},{7,5},{8,10},{10,8},{9,1... | collective-permute-start | bytes 786440 | tf_op jit(solution)/shard_map/ppermute | solution.py:22
  54.5 4.3 %collective-permute-start.16 = (bf16[8,32,128]{2,1,0:T(8,128)(2,1)S(1)}, bf16[8,32,128]{2,1,0:T(8,128)(2,1)S(1)}, u32[]{:S(2)}, u32[]{:S(2)}) collective-permute-start(bf16[8,32,128]{2,1,0:T(8,128)(2,1)S(1)} %collective-permute-done.12.refs_2_), channel_id=1, source_target_pairs={{0,4},{4,0},{8,12},{12,8},{1,5},{5,1},{9,13},{13,9},{2,6},{6,2},{1... | collective-permute-start | bytes 196616 | tf_op jit(solution)/shard_map/ppermute | solution.py:22
  60.2 5.0 %collective-permute-start.17 = (bf16[16,32,128]{2,1,0:T(8,128)(2,1)S(1)}, bf16[16,32,128]{2,1,0:T(8,128)(2,1)S(1)}, u32[]{:S(2)}, u32[]{:S(2)}) collective-permute-start(bf16[16,32,128]{2,1,0:T(8,128)(2,1)S(1)} %get-tuple-element.47), channel_id=1, source_target_pairs={{0,2},{2,0},{1,3},{3,1},{4,6},{6,4},{5,7},{7,5},{8,10},{10,8},{9,1... | collective-permute-start | bytes 393224 | tf_op jit(solution)/shard_map/ppermute | solution.py:22

commit v8 on v6

--- a/solution.py
+++ b/solution.py
@@ -7,7 +7,7 @@
 from jax.experimental.pallas import tpu as pltpu
 from jax.sharding import PartitionSpec as P
 
-UNROLL = 16
+UNROLL = 24
 FIELD = 9
 FAR_UNROLL = 32
 VMEM = pl.BlockSpec(memory_space=pltpu.VMEM)

time: 69 us -> 68.2 us (0.988); the launches traced: 67.8 us -> 68.1 us
  starting transfers between devices: 28.6 us -> 25.2 us
  Pallas kernels: 19.6 us -> 22.1 us
  waiting for transfers between devices: 18.7 us -> 20 us
    ppermute x18, starting transfers between devices: 28.6 us -> 25.2 us  [swapped(): lax.ppermute(array, axis, [(i, partner(i)) for i in range(lax.axis_size(a...]
    ppermute x18, waiting for transfers between devices: 18.7 us -> 20 us  [swapped(): lax.ppermute(array, axis, [(i, partner(i)) for i in range(lax.axis_size(a...]
    pallas_call x1, Pallas kernels: 4.26 us -> 5.35 us  [tiled_on_device(): pl.pallas_call(functools.partial(prepare_kernel, clusters), out_shape=(pl...]
    pallas_call x2, Pallas kernels: 2.19 us -> 2.98 us  [far(): pl.pallas_call(far_kernel, out_shape=(jax.ShapeDtypeStruct((clusters, col...]
  transfers between devices with their start and end apart: 18 -> 18, of which waited for: 10 -> 9; matrix products, arithmetic and copies ran while one was open for 0% -> 0% of each run, Pallas kernels for 19% -> 22%
where the time goes in v8:
time: 68.2 us; the launch traced here: 68.1 us
  starting transfers between devices  25.2 us (37%)
  Pallas kernels  22.1 us (32%)
  waiting for transfers between devices  20 us (29%)
  between operations  0.76 us (1%)
    ppermute x18, starting transfers between devices, swapped(): lax.ppermute(array, axis, [(i, partner(i)) for i in range(lax.axis_size(a...  25.2 us
    ppermute x18, waiting for transfers between devices, swapped(): lax.ppermute(array, axis, [(i, partner(i)) for i in range(lax.axis_size(a...  20 us
    pallas_call x1, Pallas kernels, tiled_on_device(): pl.pallas_call(functools.partial(prepare_kernel, clusters), out_shape=(pl...  5.35 us
    pallas_call x2, Pallas kernels, finish(): pl.pallas_call(finish_kernel, out_shape=outs, in_specs=[SMEM] + [VMEM] *...  4.94 us
    pallas_call x3, Pallas kernels, near_halves(): pl.pallas_call(functools.partial(near_halves_kernel, kind), out_shape=acc...  4.87 us
    pallas_call x2, Pallas kernels, far(): pl.pallas_call(far_kernel, out_shape=(jax.ShapeDtypeStruct((clusters, col...  2.98 us
    pallas_call x1, Pallas kernels, near_own(): pl.pallas_call(near_own_kernel, out_shape=acc_shape, in_specs=[SMEM, HBM,...  2.09 us
    pallas_call x1, Pallas kernels, tiled_on_device(): pl.pallas_call(start_kernel, out_shape=(mine_shape, jax.ShapeDtypeStruct(...  1.9 us
  transfers between devices with their start and end apart: 18, of which 9 were waited for; matrix products, arithmetic and copies ran while one was open for 0% of the time, Pallas kernels for 22%

profile of v8, /device:TPU:0, one launch (start us, length us, event | category | flops | bytes accessed | tf_op | source)
XLA Modules:
  0.0 68.1 jit_solution(5028322835927727588)
XLA Ops:
  0.6 1.9 %start.1 = (bf16[32,32,128]{2,1,0:T(8,128)(2,1)S(1)}, bf16[32,64,128]{2,1,0:T(8,128)(2,1)S(1)}, f32[8,32,128]{2,1,0:T(8,128)S(1)}, bf16[8,32,128]{2,1,0:T(8,128)(2,1)S(1)}) custom-call(f32[32,32,256]{2,1,0:T(8,128)} %bitcast.7, bf16[32,64,128]{2,1,0:T(8,128)(2,1)} %bitcast.10), custom_call_target="tpu_custom_call" | custom-call | bytes 7380000 | tf_op jit(solution)/shard_map/start/pallas_call | solution.py:278
  2.6 3.0 %collective-permute-start.1 = (bf16[8,32,128]{2,1,0:T(8,128)(2,1)S(1)}, bf16[8,32,128]{2,1,0:T(8,128)(2,1)S(1)}, u32[]{:S(2)}, u32[]{:S(2)}) collective-permute-start(bf16[8,32,128]{2,1,0:T(8,128)(2,1)S(1)} %get-tuple-element.29), channel_id=1, source_target_pairs={{0,2},{2,0},{1,3},{3,1},{4,6},{6,4},{5,7},{7,5},{8,10},{10,8},{9,1... | collective-permute-start | bytes 196616 | tf_op jit(solution)/shard_map/ppermute | solution.py:22
  5.6 3.6 %collective-permute-start.4 = (bf16[32,32,128]{2,1,0:T(8,128)(2,1)S(1)}, bf16[32,32,128]{2,1,0:T(8,128)(2,1)S(1)}, u32[]{:S(2)}, u32[]{:S(2)}) collective-permute-start(bf16[32,32,128]{2,1,0:T(8,128)(2,1)S(1)} %get-tuple-element.26), channel_id=1, source_target_pairs={{0,12},{4,8},{8,4},{12,0},{1,13},{5,9},{9,5},{13,1},{2,14},{6,10},... | collective-permute-start | bytes 786440 | tf_op jit(solution)/shard_map/ppermute | solution.py:22
  9.2 1.8 %collective-permute-start.2 = (bf16[8,32,128]{2,1,0:T(8,128)(2,1)S(1)}, bf16[8,32,128]{2,1,0:T(8,128)(2,1)S(1)}, u32[]{:S(2)}, u32[]{:S(2)}) collective-permute-start(bf16[8,32,128]{2,1,0:T(8,128)(2,1)S(1)} %add_convert_fusion.1.refs_0_), channel_id=1, source_target_pairs={{0,8},{4,12},{8,0},{12,4},{1,9},{5,13},{9,1},{13,5},{2,10},{6,14},... | collective-permute-start | bytes 196616 | tf_op jit(solution)/shard_map/ppermute | solution.py:22
  11.0 5.4 %prepare.1 = (s32[4,152]{1,0:T(4,128)S(4)}, s32[3,160]{1,0:T(4,128)S(4)}, bf16[128,128,256]{2,1,0:T(8,128)(2,1)S(1)}, bf16[160,64,64]{2,1,0:T(8,128)(2,1)S(1)}) custom-call(s32[2,128]{1,0:T(2,128)} %bitcast.12, s32[2,128]{1,0:T(2,128)} %bitcast.13, bf16[128,128,256]{2,1,0:T(8,128)(2,1)} %blocks_hbm.1, bf16[64,64,128]{2,1,0:T(8,128)(2,1)} %bitcast.9), custom_call_target="tpu_custom_call" | custom-call | bytes 14760000 | tf_op jit(solution)/shard_map/prepare/pallas_call | solution.py:288
  16.4 2.1 %near_own.1.refs_0_ = f32[33,32,128]{2,1,0:T(8,128)S(1)} custom-call(s32[4,152]{1,0:T(4,128)S(4)} %get-tuple-element.25.plan_ref, f32[32,32,256]{2,1,0:T(8,128)S(1)} %bitcast.8, bf16[128,128,256]{2,1,0:T(8,128)(2,1)S(1)} %get-tuple-element.27.blocks_ref), custom_call_target="tpu_custom_call" | custom-call | bytes 11070000 | tf_op jit(solution)/shard_map/near_own/pallas_call | solution.py:312
  19.0 3.8 %collective-permute-done.2.refs_2_ = bf16[8,32,128]{2,1,0:T(8,128)(2,1)S(1)} collective-permute-done((bf16[8,32,128]{2,1,0:T(8,128)(2,1)S(1)}, bf16[8,32,128]{2,1,0:T(8,128)(2,1)S(1)}, u32[]{:S(2)}, u32[]{:S(2)}) %collective-permute-start.2) | collective-permute-done | bytes 65568 | tf_op jit(solution)/shard_map/ppermute | solution.py:22
  23.3 0.7 collective-permute-start.6
  24.0 1.4 %collective-permute-start.7 = (bf16[8,32,128]{2,1,0:T(8,128)(2,1)S(1)}, bf16[8,32,128]{2,1,0:T(8,128)(2,1)S(1)}, u32[]{:S(2)}, u32[]{:S(2)}) collective-permute-start(bf16[8,32,128]{2,1,0:T(8,128)(2,1)S(1)} %collective-permute-done.2.refs_2_), channel_id=1, source_target_pairs={{0,4},{4,0},{8,12},{12,8},{1,5},{5,1},{9,13},{13,9},{2,6},{6,2},{1... | collective-permute-start | bytes 196616 | tf_op jit(solution)/shard_map/ppermute | solution.py:22
  25.3 2.2 %collective-permute-done.6.refs_1_ = bf16[8,32,128]{2,1,0:T(8,128)(2,1)S(1)} collective-permute-done((bf16[8,32,128]{2,1,0:T(8,128)(2,1)S(1)}, bf16[8,32,128]{2,1,0:T(8,128)(2,1)S(1)}, u32[]{:S(2)}, u32[]{:S(2)}) %collective-permute-start.6) | collective-permute-done | bytes 65568 | tf_op jit(solution)/shard_map/ppermute | solution.py:22
  27.6 0.7 %collective-permute-done.7.refs_3_ = bf16[8,32,128]{2,1,0:T(8,128)(2,1)S(1)} collective-permute-done((bf16[8,32,128]{2,1,0:T(8,128)(2,1)S(1)}, bf16[8,32,128]{2,1,0:T(8,128)(2,1)S(1)}, u32[]{:S(2)}, u32[]{:S(2)}) %collective-permute-start.7) | collective-permute-done | bytes 65568 | tf_op jit(solution)/shard_map/ppermute | solution.py:22
  28.3 1.5 %far.2 = (f32[32,32,64]{2,1,0:T(8,128)S(1)}, bf16[16,32,128]{2,1,0:T(8,128)(2,1)S(1)}) custom-call(s32[3,160]{1,0:T(4,128)S(4)} %get-tuple-element.32.plan_ref, bf16[160,64,64]{2,1,0:T(8,128)(2,1)S(1)} %get-tuple-element.33.pairs_ref, bf16[8,32,128]{2,1,0:T(8,128)(2,1)S(1)} %add_convert_fusion.1.refs_0_, ...), custom_call_target="tpu_custom_call" | custom-call | bytes 11070000 | tf_op jit(solution)/shard_map/far/pallas_call | solution.py:340
  29.8 1.2 %collective-permute-start.8 = (bf16[16,32,128]{2,1,0:T(8,128)(2,1)S(1)}, bf16[16,32,128]{2,1,0:T(8,128)(2,1)S(1)}, u32[]{:S(2)}, u32[]{:S(2)}) collective-permute-start(bf16[16,32,128]{2,1,0:T(8,128)(2,1)S(1)} %get-tuple-element.36), channel_id=1, source_target_pairs={{0,2},{2,0},{1,3},{3,1},{4,6},{6,4},{5,7},{7,5},{8,10},{10,8},{9,1... | collective-permute-start | bytes 393224 | tf_op jit(solution)/shard_map/ppermute | solution.py:22
  30.9 1.4 %near_halves.3.acc_in = f32[33,32,128]{2,1,0:T(8,128)S(1)} custom-call(s32[4,152]{1,0:T(4,128)S(4)} %get-tuple-element.25.plan_ref, bf16[32,32,128]{2,1,0:T(8,128)(2,1)S(1)} %collective-permute-done.4.same_ref, bf16[32,32,128]{2,1,0:T(8,128)(2,1)S(1)} %collective-permute-done.5.other_ref, bf16[128,128,256]{2,1,0:T(8,128)(2,1)S(1)} %get-tuple-element.27.blocks_ref, ...), custom_call_target="tpu_custom_call" | custom-call | bytes 7380000 | tf_op jit(solution)/shard_map/near_halves/pallas_call | solution.py:328
  32.4 2.4 %collective-permute-done.8.far_other_ref = bf16[16,32,128]{2,1,0:T(8,128)(2,1)S(1)} collective-permute-done((bf16[16,32,128]{2,1,0:T(8,128)(2,1)S(1)}, bf16[16,32,128]{2,1,0:T(8,128)(2,1)S(1)}, u32[]{:S(2)}, u32[]{:S(2)}) %collective-permute-start.8) | collective-permute-done | bytes 131104 | tf_op jit(solution)/shard_map/ppermute | solution.py:22
  34.8 2.5 %finish.2 = (f32[32,32,128]{2,1,0:T(8,128)}, bf16[32,32,128]{2,1,0:T(8,128)(2,1)S(1)}, f32[8,32,128]{2,1,0:T(8,128)S(1)}, bf16[40,32,128]{2,1,0:T(8,128)(2,1)S(1)}) custom-call(s32[4,152]{1,0:T(4,128)S(4)} %get-tuple-element.25.plan_ref, bf16[32,32,128]{2,1,0:T(8,128)(2,1)S(1)} %collective-permute-done.same_ref, ...), custom_call_target="tpu_custom_call" | custom-call | bytes 14760000 | tf_op jit(solution)/shard_map/finish/pallas_call | solution.py:359
  37.4 1.2 %collective-permute-start.10 = (bf16[40,32,128]{2,1,0:T(8,128)(2,1)S(1)}, bf16[40,32,128]{2,1,0:T(8,128)(2,1)S(1)}, u32[]{:S(2)}, u32[]{:S(2)}) collective-permute-start(bf16[40,32,128]{2,1,0:T(8,128)(2,1)S(1)} %get-tuple-element.40), channel_id=1, source_target_pairs={{0,2},{2,0},{1,3},{3,1},{4,6},{6,4},{5,7},{7,5},{8,10},{10,8},{9,1... | collective-permute-start | bytes 983048 | tf_op jit(solution)/shard_map/ppermute | solution.py:22
  38.5 3.3 %collective-permute-start.14 = (bf16[32,32,128]{2,1,0:T(8,128)(2,1)S(1)}, bf16[32,32,128]{2,1,0:T(8,128)(2,1)S(1)}, u32[]{:S(2)}, u32[]{:S(2)}) collective-permute-start(bf16[32,32,128]{2,1,0:T(8,128)(2,1)S(1)} %get-tuple-element.39.same_ref), channel_id=1, source_target_pairs={{0,12},{4,8},{8,4},{12,0},{1,13},{5,9},{9,5},{13,1},{2,14},{6,10},... | collective-permute-start | bytes 786440 | tf_op jit(solution)/shard_map/ppermute | solution.py:22
  41.8 2.7 %collective-permute-done.10.other_ref = bf16[40,32,128]{2,1,0:T(8,128)(2,1)S(1)} collective-permute-done((bf16[40,32,128]{2,1,0:T(8,128)(2,1)S(1)}, bf16[40,32,128]{2,1,0:T(8,128)(2,1)S(1)}, u32[]{:S(2)}, u32[]{:S(2)}) %collective-permute-start.10) | collective-permute-done | bytes 327712 | tf_op jit(solution)/shard_map/ppermute | solution.py:22
  44.5 2.6 %collective-permute-start.12 = (bf16[8,32,128]{2,1,0:T(8,128)(2,1)S(1)}, bf16[8,32,128]{2,1,0:T(8,128)(2,1)S(1)}, u32[]{:S(2)}, u32[]{:S(2)}) collective-permute-start(bf16[8,32,128]{2,1,0:T(8,128)(2,1)S(1)} %add_convert_fusion.refs_0_), channel_id=1, source_target_pairs={{0,8},{4,12},{8,0},{12,4},{1,9},{5,13},{9,1},{13,5},{2,10},{6,14},... | collective-permute-start | bytes 196616 | tf_op jit(solution)/shard_map/ppermute | solution.py:22
  47.6 1.8 %collective-permute-done.14.same_ref = bf16[32,32,128]{2,1,0:T(8,128)(2,1)S(1)} collective-permute-done((bf16[32,32,128]{2,1,0:T(8,128)(2,1)S(1)}, bf16[32,32,128]{2,1,0:T(8,128)(2,1)S(1)}, u32[]{:S(2)}, u32[]{:S(2)}) %collective-permute-start.14) | collective-permute-done | bytes 262176 | tf_op jit(solution)/shard_map/ppermute | solution.py:22
  49.4 1.1 %collective-permute-start.15 = (bf16[32,32,128]{2,1,0:T(8,128)(2,1)S(1)}, bf16[32,32,128]{2,1,0:T(8,128)(2,1)S(1)}, u32[]{:S(2)}, u32[]{:S(2)}) collective-permute-start(bf16[32,32,128]{2,1,0:T(8,128)(2,1)S(1)} %collective-permute-done.14.same_ref), channel_id=1, source_target_pairs={{0,2},{2,0},{1,3},{3,1},{4,6},{6,4},{5,7},{7,5},{8,10},{10,8},{9,1... | collective-permute-start | bytes 786440 | tf_op jit(solution)/shard_map/ppermute | solution.py:22
  50.5 2.0 %near_halves.4.refs_0_ = f32[33,32,128]{2,1,0:T(8,128)S(1)} custom-call(s32[4,152]{1,0:T(4,128)S(4)} %get-tuple-element.25.plan_ref, bf16[32,32,128]{2,1,0:T(8,128)(2,1)S(1)} %get-tuple-element.39.same_ref, bf16[40,32,128]{2,1,0:T(8,128)(2,1)S(1)} %collective-permute-done.10.other_ref, bf16[128,128,256]{2,1,0:T(8,128)(2,1)S(1)} %get-tuple-element.27.blocks_ref), custom_call_target="tpu_custom_call" | custom-call | bytes 7380000 | tf_op jit(solution)/shard_map/near_halves/pallas_call | solution.py:328
  52.6 1.0 %collective-permute-done.12.refs_2_ = bf16[8,32,128]{2,1,0:T(8,128)(2,1)S(1)} collective-permute-done((bf16[8,32,128]{2,1,0:T(8,128)(2,1)S(1)}, bf16[8,32,128]{2,1,0:T(8,128)(2,1)S(1)}, u32[]{:S(2)}, u32[]{:S(2)}) %collective-permute-start.12) | collective-permute-done | bytes 65568 | tf_op jit(solution)/shard_map/ppermute | solution.py:22
  53.6 1.1 %collective-permute-start.13 = (bf16[32,32,128]{2,1,0:T(8,128)(2,1)S(1)}, bf16[32,32,128]{2,1,0:T(8,128)(2,1)S(1)}, u32[]{:S(2)}, u32[]{:S(2)}) collective-permute-start(bf16[32,32,128]{2,1,0:T(8,128)(2,1)S(1)} %collective-permute-done.9.same_ref), channel_id=1, source_target_pairs={{0,2},{2,0},{1,3},{3,1},{4,6},{6,4},{5,7},{7,5},{8,10},{10,8},{9,1... | collective-permute-start | bytes 786440 | tf_op jit(solution)/shard_map/ppermute | solution.py:22
  54.7 2.2 %collective-permute-start.16 = (bf16[8,32,128]{2,1,0:T(8,128)(2,1)S(1)}, bf16[8,32,128]{2,1,0:T(8,128)(2,1)S(1)}, u32[]{:S(2)}, u32[]{:S(2)}) collective-permute-start(bf16[8,32,128]{2,1,0:T(8,128)(2,1)S(1)} %collective-permute-done.12.refs_2_), channel_id=1, source_target_pairs={{0,4},{4,0},{8,12},{12,8},{1,5},{5,1},{9,13},{13,9},{2,6},{6,2},{1... | collective-permute-start | bytes 196616 | tf_op jit(solution)/shard_map/ppermute | solution.py:22
  56.9 2.2 %collective-permute-done.16.refs_3_ = bf16[8,32,128]{2,1,0:T(8,128)(2,1)S(1)} collective-permute-done((bf16[8,32,128]{2,1,0:T(8,128)(2,1)S(1)}, bf16[8,32,128]{2,1,0:T(8,128)(2,1)S(1)}, u32[]{:S(2)}, u32[]{:S(2)}) %collective-permute-start.16) | collective-permute-done | bytes 65568 | tf_op jit(solution)/shard_map/ppermute | solution.py:22
  59.2 1.5 %far.3 = (f32[32,32,64]{2,1,0:T(8,128)S(1)}, bf16[16,32,128]{2,1,0:T(8,128)(2,1)S(1)}) custom-call(s32[3,160]{1,0:T(4,128)S(4)} %get-tuple-element.32.plan_ref, bf16[160,64,64]{2,1,0:T(8,128)(2,1)S(1)} %get-tuple-element.33.pairs_ref, bf16[8,32,128]{2,1,0:T(8,128)(2,1)S(1)} %add_convert_fusion.refs_0_, ...), custom_call_target="tpu_custom_call" | custom-call | bytes 11070000 | tf_op jit(solution)/shard_map/far/pallas_call | solution.py:340
  60.7 0.6 collective-permute-start.17
  61.3 1.4 %near_halves.5.acc_in = f32[33,32,128]{2,1,0:T(8,128)S(1)} custom-call(s32[4,152]{1,0:T(4,128)S(4)} %get-tuple-element.25.plan_ref, bf16[32,32,128]{2,1,0:T(8,128)(2,1)S(1)} %collective-permute-done.14.same_ref, bf16[32,32,128]{2,1,0:T(8,128)(2,1)S(1)} %collective-permute-done.15.other_ref, bf16[128,128,256]{2,1,0:T(8,128)(2,1)S(1)} %get-tuple-element.27.blocks_ref, ...), custom_call_target="tpu_custom_call" | custom-call | bytes 7380000 | tf_op jit(solution)/shard_map/near_halves/pallas_call | solution.py:328
  62.7 3.0 %collective-permute-done.17.far_other_ref = bf16[16,32,128]{2,1,0:T(8,128)(2,1)S(1)} collective-permute-done((bf16[16,32,128]{2,1,0:T(8,128)(2,1)S(1)}, bf16[16,32,128]{2,1,0:T(8,128)(2,1)S(1)}, u32[]{:S(2)}, u32[]{:S(2)}) %collective-permute-start.17) | collective-permute-done | bytes 131104 | tf_op jit(solution)/shard_map/ppermute | solution.py:22
  65.7 2.4 %finish.3 = f32[32,32,128]{2,1,0:T(8,128)} custom-call(s32[4,152]{1,0:T(4,128)S(4)} %get-tuple-element.25.plan_ref, bf16[32,32,128]{2,1,0:T(8,128)(2,1)S(1)} %collective-permute-done.9.same_ref, bf16[32,32,128]{2,1,0:T(8,128)(2,1)S(1)} %collective-permute-done.13.other_ref, bf16[128,128,256]{2,1,0:T(8,128)(2,1)S(1)} %get-tuple-element.27.blocks_ref, ...), custom_call_target="tpu_custom_call" | custom-call | bytes 14760000 | tf_op jit(solution)/shard_map/finish/pallas_call | solution.py:359
  (18 shorter events, 1.6 us)
Async XLA Ops:
  0.6 15.7 %copy-start = (f32[32,256,32]{1,2,0:T(8,128)S(1)}, f32[32,256,32]{1,2,0:T(8,128)}, u32[]{:S(2)}) copy-start(f32[32,256,32]{1,2,0:T(8,128)} %param.6) | copy-start | bytes 3145732
  2.6 6.6 %collective-permute-start.1 = (bf16[8,32,128]{2,1,0:T(8,128)(2,1)S(1)}, bf16[8,32,128]{2,1,0:T(8,128)(2,1)S(1)}, u32[]{:S(2)}, u32[]{:S(2)}) collective-permute-start(bf16[8,32,128]{2,1,0:T(8,128)(2,1)S(1)} %get-tuple-element.29), channel_id=1, source_target_pairs={{0,2},{2,0},{1,3},{3,1},{4,6},{6,4},{5,7},{7,5},{8,10},{10,8},{9,1... | collective-permute-start | bytes 196616 | tf_op jit(solution)/shard_map/ppermute | solution.py:22
  5.6 12.9 %collective-permute-start.4 = (bf16[32,32,128]{2,1,0:T(8,128)(2,1)S(1)}, bf16[32,32,128]{2,1,0:T(8,128)(2,1)S(1)}, u32[]{:S(2)}, u32[]{:S(2)}) collective-permute-start(bf16[32,32,128]{2,1,0:T(8,128)(2,1)S(1)} %get-tuple-element.26), channel_id=1, source_target_pairs={{0,12},{4,8},{8,4},{12,0},{1,13},{5,9},{9,5},{13,1},{2,14},{6,10},... | collective-permute-start | bytes 786440 | tf_op jit(solution)/shard_map/ppermute | solution.py:22
  9.2 13.6 %collective-permute-start = (bf16[32,32,128]{2,1,0:T(8,128)(2,1)S(1)}, bf16[32,32,128]{2,1,0:T(8,128)(2,1)S(1)}, u32[]{:S(2)}, u32[]{:S(2)}) collective-permute-start(bf16[32,32,128]{2,1,0:T(8,128)(2,1)S(1)} %get-tuple-element.26), channel_id=1, source_target_pairs={{0,4},{4,0},{8,12},{12,8},{1,5},{5,1},{9,13},{13,9},{2,6},{6,2},{1... | collective-permute-start | bytes 786440 | tf_op jit(solution)/shard_map/ppermute | solution.py:22
  9.2 13.6 %collective-permute-start.2 = (bf16[8,32,128]{2,1,0:T(8,128)(2,1)S(1)}, bf16[8,32,128]{2,1,0:T(8,128)(2,1)S(1)}, u32[]{:S(2)}, u32[]{:S(2)}) collective-permute-start(bf16[8,32,128]{2,1,0:T(8,128)(2,1)S(1)} %add_convert_fusion.1.refs_0_), channel_id=1, source_target_pairs={{0,8},{4,12},{8,0},{12,4},{1,9},{5,13},{9,1},{13,5},{2,10},{6,14},... | collective-permute-start | bytes 196616 | tf_op jit(solution)/shard_map/ppermute | solution.py:22
  18.5 12.4 %collective-permute-start.5 = (bf16[32,32,128]{2,1,0:T(8,128)(2,1)S(1)}, bf16[32,32,128]{2,1,0:T(8,128)(2,1)S(1)}, u32[]{:S(2)}, u32[]{:S(2)}) collective-permute-start(bf16[32,32,128]{2,1,0:T(8,128)(2,1)S(1)} %collective-permute-done.4.same_ref), channel_id=1, source_target_pairs={{0,2},{2,0},{1,3},{3,1},{4,6},{6,4},{5,7},{7,5},{8,10},{10,8},{9,1... | collective-permute-start | bytes 786440 | tf_op jit(solution)/shard_map/ppermute | solution.py:22
  22.8 12.0 %collective-permute-start.3 = (bf16[32,32,128]{2,1,0:T(8,128)(2,1)S(1)}, bf16[32,32,128]{2,1,0:T(8,128)(2,1)S(1)}, u32[]{:S(2)}, u32[]{:S(2)}) collective-permute-start(bf16[32,32,128]{2,1,0:T(8,128)(2,1)S(1)} %collective-permute-done.same_ref), channel_id=1, source_target_pairs={{0,2},{2,0},{1,3},{3,1},{4,6},{6,4},{5,7},{7,5},{8,10},{10,8},{9,1... | collective-permute-start | bytes 786440 | tf_op jit(solution)/shard_map/ppermute | solution.py:22
  23.3 4.3 %collective-permute-start.6 = (bf16[8,32,128]{2,1,0:T(8,128)(2,1)S(1)}, bf16[8,32,128]{2,1,0:T(8,128)(2,1)S(1)}, u32[]{:S(2)}, u32[]{:S(2)}) collective-permute-start(bf16[8,32,128]{2,1,0:T(8,128)(2,1)S(1)} %add_convert_fusion.1.refs_0_), channel_id=1, source_target_pairs={{0,4},{4,0},{8,12},{12,8},{1,5},{5,1},{9,13},{13,9},{2,6},{6,2},{1... | collective-permute-start | bytes 196616 | tf_op jit(solution)/shard_map/ppermute | solution.py:22
  24.0 4.3 %collective-permute-start.7 = (bf16[8,32,128]{2,1,0:T(8,128)(2,1)S(1)}, bf16[8,32,128]{2,1,0:T(8,128)(2,1)S(1)}, u32[]{:S(2)}, u32[]{:S(2)}) collective-permute-start(bf16[8,32,128]{2,1,0:T(8,128)(2,1)S(1)} %collective-permute-done.2.refs_2_), channel_id=1, source_target_pairs={{0,4},{4,0},{8,12},{12,8},{1,5},{5,1},{9,13},{13,9},{2,6},{6,2},{1... | collective-permute-start | bytes 196616 | tf_op jit(solution)/shard_map/ppermute | solution.py:22
  29.8 5.0 %collective-permute-start.8 = (bf16[16,32,128]{2,1,0:T(8,128)(2,1)S(1)}, bf16[16,32,128]{2,1,0:T(8,128)(2,1)S(1)}, u32[]{:S(2)}, u32[]{:S(2)}) collective-permute-start(bf16[16,32,128]{2,1,0:T(8,128)(2,1)S(1)} %get-tuple-element.36), channel_id=1, source_target_pairs={{0,2},{2,0},{1,3},{3,1},{4,6},{6,4},{5,7},{7,5},{8,10},{10,8},{9,1... | collective-permute-start | bytes 393224 | tf_op jit(solution)/shard_map/ppermute | solution.py:22
  37.4 7.1 %collective-permute-start.10 = (bf16[40,32,128]{2,1,0:T(8,128)(2,1)S(1)}, bf16[40,32,128]{2,1,0:T(8,128)(2,1)S(1)}, u32[]{:S(2)}, u32[]{:S(2)}) collective-permute-start(bf16[40,32,128]{2,1,0:T(8,128)(2,1)S(1)} %get-tuple-element.40), channel_id=1, source_target_pairs={{0,2},{2,0},{1,3},{3,1},{4,6},{6,4},{5,7},{7,5},{8,10},{10,8},{9,1... | collective-permute-start | bytes 983048 | tf_op jit(solution)/shard_map/ppermute | solution.py:22
  38.5 10.9 %collective-permute-start.14 = (bf16[32,32,128]{2,1,0:T(8,128)(2,1)S(1)}, bf16[32,32,128]{2,1,0:T(8,128)(2,1)S(1)}, u32[]{:S(2)}, u32[]{:S(2)}) collective-permute-start(bf16[32,32,128]{2,1,0:T(8,128)(2,1)S(1)} %get-tuple-element.39.same_ref), channel_id=1, source_target_pairs={{0,12},{4,8},{8,4},{12,0},{1,13},{5,9},{9,5},{13,1},{2,14},{6,10},... | collective-permute-start | bytes 786440 | tf_op jit(solution)/shard_map/ppermute | solution.py:22
  41.8 10.8 %collective-permute-start.9 = (bf16[32,32,128]{2,1,0:T(8,128)(2,1)S(1)}, bf16[32,32,128]{2,1,0:T(8,128)(2,1)S(1)}, u32[]{:S(2)}, u32[]{:S(2)}) collective-permute-start(bf16[32,32,128]{2,1,0:T(8,128)(2,1)S(1)} %get-tuple-element.39.same_ref), channel_id=1, source_target_pairs={{0,4},{4,0},{8,12},{12,8},{1,5},{5,1},{9,13},{13,9},{2,6},{6,2},{1... | collective-permute-start | bytes 786440 | tf_op jit(solution)/shard_map/ppermute | solution.py:22
  44.5 9.1 %collective-permute-start.12 = (bf16[8,32,128]{2,1,0:T(8,128)(2,1)S(1)}, bf16[8,32,128]{2,1,0:T(8,128)(2,1)S(1)}, u32[]{:S(2)}, u32[]{:S(2)}) collective-permute-start(bf16[8,32,128]{2,1,0:T(8,128)(2,1)S(1)} %add_convert_fusion.refs_0_), channel_id=1, source_target_pairs={{0,8},{4,12},{8,0},{12,4},{1,9},{5,13},{9,1},{13,5},{2,10},{6,14},... | collective-permute-start | bytes 196616 | tf_op jit(solution)/shard_map/ppermute | solution.py:22
  47.1 6.5 %collective-permute-start.11 = (bf16[8,32,128]{2,1,0:T(8,128)(2,1)S(1)}, bf16[8,32,128]{2,1,0:T(8,128)(2,1)S(1)}, u32[]{:S(2)}, u32[]{:S(2)}) collective-permute-start(bf16[8,32,128]{2,1,0:T(8,128)(2,1)S(1)} %add_convert_fusion.refs_0_), channel_id=1, source_target_pairs={{0,4},{4,0},{8,12},{12,8},{1,5},{5,1},{9,13},{13,9},{2,6},{6,2},{1... | collective-permute-start | bytes 196616 | tf_op jit(solution)/shard_map/ppermute | solution.py:22
  49.4 11.8 %collective-permute-start.15 = (bf16[32,32,128]{2,1,0:T(8,128)(2,1)S(1)}, bf16[32,32,128]{2,1,0:T(8,128)(2,1)S(1)}, u32[]{:S(2)}, u32[]{:S(2)}) collective-permute-start(bf16[32,32,128]{2,1,0:T(8,128)(2,1)S(1)} %collective-permute-done.14.same_ref), channel_id=1, source_target_pairs={{0,2},{2,0},{1,3},{3,1},{4,6},{6,4},{5,7},{7,5},{8,10},{10,8},{9,1... | collective-permute-start | bytes 786440 | tf_op jit(solution)/shard_map/ppermute | solution.py:22
  53.6 12.1 %collective-permute-start.13 = (bf16[32,32,128]{2,1,0:T(8,128)(2,1)S(1)}, bf16[32,32,128]{2,1,0:T(8,128)(2,1)S(1)}, u32[]{:S(2)}, u32[]{:S(2)}) collective-permute-start(bf16[32,32,128]{2,1,0:T(8,128)(2,1)S(1)} %collective-permute-done.9.same_ref), channel_id=1, source_target_pairs={{0,2},{2,0},{1,3},{3,1},{4,6},{6,4},{5,7},{7,5},{8,10},{10,8},{9,1... | collective-permute-start | bytes 786440 | tf_op jit(solution)/shard_map/ppermute | solution.py:22
  54.7 4.5 %collective-permute-start.16 = (bf16[8,32,128]{2,1,0:T(8,128)(2,1)S(1)}, bf16[8,32,128]{2,1,0:T(8,128)(2,1)S(1)}, u32[]{:S(2)}, u32[]{:S(2)}) collective-permute-start(bf16[8,32,128]{2,1,0:T(8,128)(2,1)S(1)} %collective-permute-done.12.refs_2_), channel_id=1, source_target_pairs={{0,4},{4,0},{8,12},{12,8},{1,5},{5,1},{9,13},{13,9},{2,6},{6,2},{1... | collective-permute-start | bytes 196616 | tf_op jit(solution)/shard_map/ppermute | solution.py:22
  60.7 5.0 %collective-permute-start.17 = (bf16[16,32,128]{2,1,0:T(8,128)(2,1)S(1)}, bf16[16,32,128]{2,1,0:T(8,128)(2,1)S(1)}, u32[]{:S(2)}, u32[]{:S(2)}) collective-permute-start(bf16[16,32,128]{2,1,0:T(8,128)(2,1)S(1)} %get-tuple-element.47), channel_id=1, source_target_pairs={{0,2},{2,0},{1,3},{3,1},{4,6},{6,4},{5,7},{7,5},{8,10},{10,8},{9,1... | collective-permute-start | bytes 393224 | tf_op jit(solution)/shard_map/ppermute | solution.py:22
